TPU v7x, 32 devices: a whole 2x2x4 slice. The times are simulated.
32 devices in a mesh: traj: 2 (over x), frame: 4 (over y, core), patch: 4 (over z).
Axes of the slice: x: 2, y: 2, z: 4, core: 2. Of those that a mesh axis runs over, the one named last changes fastest.
Arguments:
- queries: float32 [16, 256, 1024], P(('traj', 'frame'), 'patch'), parts along dimension 0, may hold values from -64 to 64
- key_rows: float32 [16, 256, 1024], P(('traj', 'frame'), 'patch'), parts along dimension 0, may hold values from -5 to 5
- value_rows: float32 [16, 256, 1024], P(('traj', 'frame'), 'patch'), parts along dimension 0, may hold values from -6 to 6
- cotangent: float32 [16, 256, 1024], P(('traj', 'frame'), 'patch'), parts along dimension 0, may hold values from -6 to 6
- lookback: int32 [16], P(('traj', 'frame')), parts along dimension 0, may hold values from 2 to 6
- window: int32 [32, 12], P(('traj', 'patch')), parts along dimension 0, may hold values from 0 to 15, as said below
Outputs:
- mixed: float32 [16, 256, 1024], P(('traj', 'frame'), 'patch'), parts along dimension 0
- grad_queries: float32 [16, 256, 1024], P(('traj', 'frame'), 'patch'), parts along dimension 0
- grad_keys: float32 [16, 256, 1024], P(('traj', 'frame'), 'patch'), parts along dimension 0
- grad_values: float32 [16, 256, 1024], P(('traj', 'frame'), 'patch'), parts along dimension 0
There are 2 independent parts, one for each index of `traj`. A program takes and returns all parts, laid end to end along the dimension named above; each array names one. Nothing has to cross between parts.
Inputs may be any that keep to these rules, and one draw needn't show every extreme that they name: `window`: row b lists 12 distinct blocks: b itself first, then blocks at cyclic distance 1 to 6 from b among the 16 blocks.
All inputs are finite; a program needn't handle non-finite values.
Results may differ from a plain program's by a relative error of at most 0.0003.
Values sent between devices are 32-bit elements; how exact they have to be, the bound alone decides.
No kernel may reach another device: no remote copies, remote signals or barrier semaphores. Data moves between devices by JAX's collectives and lax.ppermute only.
A program may use at most 128 MiB of HBM per device.

v0:
```python
import math

import jax
import jax.numpy as jnp
from jax import lax
from jax.experimental import pallas as pl
from jax.experimental.pallas import tpu as pltpu
from jax.sharding import PartitionSpec as P

H = 16
BLK = 16
LOOK = 6
REACH = 6


def shifted(x, axis, by):
    count = lax.axis_size(axis)
    pairs = [(i, i + by) for i in range(count) if 0 <= i + by < count]
    return lax.ppermute(x, axis, pairs)


def passed_along(block, axis, distance):
    devices = range(lax.axis_size(axis))
    route = [((i - distance) % len(devices), i) for i in devices]
    return lax.ppermute(block, axis, route)


def split_heads(tensor, size_head):
    return tensor.reshape(tensor.shape[0], tensor.shape[1], H, size_head)


def shards_general(queries, key_rows, value_rows, cotangent, lookback, window):
    frames_here, patches_here, model_width = queries.shape
    size_head = model_width // H
    score_scale = 1.0 / math.sqrt(size_head)
    highest = lax.Precision.HIGHEST
    frame_index = lax.axis_index("frame")
    cycle_depth = (LOOK + frames_here - 2) // frames_here
    earlier = []
    carried = (key_rows, value_rows)
    for distance in range(cycle_depth):
        carried = shifted((carried[0], carried[1]), "frame", 1)
        earlier.append(carried)
    bank_keys = jnp.concatenate(
        [earlier[cycle_depth - 1 - number][0] for number in range(cycle_depth)] + [key_rows], axis=0
    )
    bank_values = jnp.concatenate(
        [earlier[cycle_depth - 1 - number][1] for number in range(cycle_depth)] + [value_rows],
        axis=0,
    )
    bank_frames = bank_keys.shape[0]
    q_heads = split_heads(queries, size_head)
    key_heads = split_heads(bank_keys, size_head)
    value_heads = split_heads(bank_values, size_head)
    query_frame = frame_index * frames_here + jnp.arange(frames_here, dtype=jnp.int32)
    key_frame = (frame_index - cycle_depth) * frames_here + jnp.arange(bank_frames, dtype=jnp.int32)
    offset = query_frame[:, None] - key_frame[None, :]
    visible = (offset >= 0) & (offset < lookback[:, None]) & (key_frame[None, :] >= 0)
    scores = jnp.einsum("fphe,jphe->phfj", q_heads, key_heads, precision=highest) * score_scale
    scores = jnp.where(visible, scores, -jnp.inf)
    weights = jax.nn.softmax(scores, axis=-1)
    temporal = jnp.einsum("phfj,jphe->fphe", weights, value_heads, precision=highest).reshape(
        frames_here, patches_here, model_width
    )
    patch_count = lax.axis_size("patch")
    patch_index = lax.axis_index("patch")
    blocks_here = patches_here // BLK
    reach_devices = -(-REACH // blocks_here)
    offsets = []
    for stride in range(-reach_devices, reach_devices + 1):
        if all(((stride - earlier_step) % patch_count != 0 for earlier_step in offsets)):
            offsets.append(stride)
    entries = []
    running_base = 0
    for stride in offsets:
        count_here = blocks_here if stride != 0 and abs(stride) == reach_devices else blocks_here
        first_block = 0 if stride >= 0 else blocks_here - count_here
        entries.append((stride, first_block, count_here, running_base))
        running_base = running_base + count_here
    count_slots = running_base
    near_banks = []
    for stride, first_block, count_here, base_slot in entries:
        rows_from = first_block * BLK
        rows_to = (first_block + count_here) * BLK
        piece = (key_rows, temporal)
        if stride == 0:
            near_banks.append(piece)
        else:
            near_banks.append(passed_along((piece[0], piece[1]), "patch", -stride))
    near_keys = jnp.concatenate([entry[0] for entry in near_banks], axis=1)
    near_values = jnp.concatenate([entry[1] for entry in near_banks], axis=1)
    owner_device = window // blocks_here
    relative = (owner_device - patch_index) % patch_count
    base_of = jnp.zeros(window.shape, jnp.int32)
    first_of = jnp.zeros(window.shape, jnp.int32)
    for stride, first_block, count_here, base_slot in entries:
        matches = relative == stride % patch_count
        base_of = jnp.where(matches, base_slot, base_of)
        first_of = jnp.where(matches, first_block, first_of)
    slot_index = base_of + window % blocks_here - first_of
    window_count = window.shape[1]
    key_blocks = near_keys.reshape(frames_here, count_slots, BLK, model_width)
    value_blocks = near_values.reshape(frames_here, count_slots, BLK, model_width)

    def frame_step(frame_items):
        query_part, key_part, value_part, grad_part = frame_items
        key_win = key_part[slot_index].reshape(blocks_here, window_count * BLK, H, size_head)
        value_win = value_part[slot_index].reshape(blocks_here, window_count * BLK, H, size_head)
        query_win = query_part.reshape(blocks_here, BLK, H, size_head)
        grad_win = grad_part.reshape(blocks_here, BLK, H, size_head)
        logits = jnp.einsum("bxhe,byhe->bhxy", query_win, key_win, precision=highest) * score_scale
        attention = jax.nn.softmax(logits, axis=-1)
        mixed_rows = jnp.einsum("bhxy,byhe->bxhe", attention, value_win, precision=highest)
        grad_attention = jnp.einsum("bxhe,byhe->bhxy", grad_win, value_win, precision=highest)
        grad_logits = attention * (
            grad_attention - jnp.sum(attention * grad_attention, axis=-1, keepdims=True)
        )
        grad_query = (
            jnp.einsum("bhxy,byhe->bxhe", grad_logits, key_win, precision=highest) * score_scale
        )
        grad_key = (
            jnp.einsum("bhxy,bxhe->byhe", grad_logits, query_win, precision=highest) * score_scale
        )
        grad_value = jnp.einsum("bhxy,bxhe->byhe", attention, grad_win, precision=highest)
        block_shape = (blocks_here, window_count, BLK, model_width)
        key_back = (
            jnp.zeros((count_slots, BLK, model_width), jnp.float32)
            .at[slot_index]
            .add(grad_key.reshape(block_shape))
        )
        value_back = (
            jnp.zeros((count_slots, BLK, model_width), jnp.float32)
            .at[slot_index]
            .add(grad_value.reshape(block_shape))
        )
        return (
            mixed_rows.reshape(patches_here, model_width),
            grad_query.reshape(patches_here, model_width),
            key_back,
            value_back,
        )

    mixed, grad_query_space, key_back, value_back = lax.map(
        frame_step, (queries, key_blocks, value_blocks, cotangent)
    )
    key_back = key_back.reshape(frames_here, count_slots * BLK, model_width)
    value_back = value_back.reshape(frames_here, count_slots * BLK, model_width)
    grad_key_space = jnp.zeros(queries.shape, jnp.float32)
    grad_temporal = jnp.zeros(queries.shape, jnp.float32)
    for stride, first_block, count_here, base_slot in entries:
        slot_from = base_slot * BLK
        slot_to = (base_slot + count_here) * BLK
        returned = (key_back[:, slot_from:slot_to], value_back[:, slot_from:slot_to])
        if stride != 0:
            returned = passed_along((returned[0], returned[1]), "patch", stride)
        rows_from = first_block * BLK
        rows_to = (first_block + count_here) * BLK
        grad_key_space = grad_key_space.at[:, rows_from:rows_to].add(returned[0])
        grad_temporal = grad_temporal.at[:, rows_from:rows_to].add(returned[1])
    grad_heads = split_heads(grad_temporal, size_head)
    grad_weights = jnp.einsum("fphe,jphe->phfj", grad_heads, value_heads, precision=highest)
    grad_scores = weights * (grad_weights - jnp.sum(weights * grad_weights, axis=-1, keepdims=True))
    grad_query_time = (
        jnp.einsum("phfj,jphe->fphe", grad_scores, key_heads, precision=highest) * score_scale
    )
    key_terms = (
        jnp.einsum("phfj,fphe->jphe", grad_scores, q_heads, precision=highest) * score_scale
    ).reshape(cycle_depth + 1, frames_here, patches_here, model_width)
    value_terms = jnp.einsum("phfj,fphe->jphe", weights, grad_heads, precision=highest).reshape(
        cycle_depth + 1, frames_here, patches_here, model_width
    )
    carried = (key_terms[0], value_terms[0])
    for distance in range(1, cycle_depth + 1):
        carried = shifted((carried[0], carried[1]), "frame", -1)
        carried = (carried[0] + key_terms[distance], carried[1] + value_terms[distance])
    grad_key_time, grad_value_time = carried
    grad_queries = grad_query_space + grad_query_time.reshape(
        frames_here, patches_here, model_width
    )
    grad_keys = grad_key_space + grad_key_time
    return (mixed, grad_queries, grad_keys, grad_value_time)


LANES = 128
SIZE = LANES // 2
INFO = 8
NN = ((1,), (0,))
NT = ((1,), (1,))


def interleave(first, second):
    axis = first.ndim - 1
    low = lax.broadcasted_iota(jnp.int32, first.shape, axis) < SIZE
    return (
        jnp.where(low, first, pltpu.roll(second, SIZE, axis)),
        jnp.where(low, pltpu.roll(first, SIZE, axis), second),
    )


def dot(a, b, dims):
    return lax.dot_general(a, b, (dims, ((), ())), preferred_element_type=jnp.float32)


def split(x):
    high = x.astype(jnp.bfloat16)
    return high, (x - high.astype(jnp.float32)).astype(jnp.bfloat16)


def stacked(x, times):
    high, low = split(x)
    return jnp.concatenate([high] * times + [low] * times, axis=0)


def heads_dot(x, high, low, dims):
    both = stacked(x, 1)
    out = dot(both, high, dims)
    return out[:SIZE] + (out[SIZE:] + dot(both[:SIZE], low, dims))


def partners(frame_count, patch_count):
    return [(frame, patch) for frame in range(frame_count) for patch in range(patch_count)]


def place(partner, patch_count):
    frame = lax.bitwise_xor(lax.axis_index("frame"), partner[0])
    return frame * patch_count + lax.bitwise_xor(lax.axis_index("patch"), partner[1])


def pack_kernel(order, patch_count, window, lookback, *refs):
    arrays, out_refs = refs[:4], refs[4 : 4 + H]
    held, (packed, window_ref, lookback_ref, sems) = refs[4 + H : 8 + H], refs[8 + H :]
    moves = list(zip((*arrays, window, lookback), (*held, window_ref, lookback_ref)))
    copies = [pltpu.make_async_copy(a, b, sems.at[n]) for n, (a, b) in enumerate(moves)]
    for copy in copies:
        copy.start()
    rows = held[0].shape[1]
    for number, (copy, ref) in enumerate(zip(copies, held)):
        copy.wait()
        for pair in range(H // 2):
            cols = rows_of(pair, LANES)
            packed[2 * pair, rows_of(number, rows)], packed[2 * pair + 1, rows_of(number, rows)] = (
                interleave(ref[0, :, cols], ref[1, :, cols])
            )
    copies[4].wait()
    copies[5].wait()
    row = lax.broadcasted_iota(jnp.int32, (INFO, LANES), 0)
    lane = lax.broadcasted_iota(jnp.int32, (INFO, LANES), 1)
    info = jnp.zeros((INFO, LANES), jnp.int32)
    for block in range(rows // BLK):
        for column in range(window_ref.shape[1]):
            at = block * BLK + (column // INFO) * SIZE
            here = (row == column % INFO) & (lane >= at) & (lane < at + BLK)
            info = jnp.where(here, window_ref[block, column], info)
    for frame in range(2):
        here = (row == INFO - 2 + frame) & (lane >= SIZE)
        info = jnp.where(here, lookback_ref[frame], info)
    info = info.astype(jnp.float32)
    for partner, ref in zip(order, out_refs):
        ref[: 4 * rows] = packed[place(partner, patch_count)]
        ref[4 * rows :] = info


def unpack_kernel(order, patch_count, *refs):
    in_refs, out_refs, packed = refs[:H], refs[H:-1], refs[-1]
    rows = out_refs[0].shape[1]
    for partner, ref in zip(order, in_refs):
        packed[place(partner, patch_count)] = ref[...]
    for pair in range(H // 2):
        cols = rows_of(pair, LANES)
        for number, ref in enumerate(out_refs):
            at = rows_of(number, rows)
            ref[0, :, cols], ref[1, :, cols] = interleave(
                packed[2 * pair, at], packed[2 * pair + 1, at]
            )


def visible_keys(frame):
    return range(max(0, frame - LOOK + 1), frame + 1)


def rows_of(index, count):
    return slice(index * count, (index + 1) * count)


def head_kernel(order, parts, columns, *refs):
    in_refs, out_refs = refs[:H], refs[H : 2 * H]
    held, done, qt, kt, vt, ct, tt, gt, gq, gk, gv, wts, bias = refs[2 * H :]
    rows = done.shape[1] // 4
    frames, _, patches = wts.shape
    pairs = frames // 2
    scale = 1.0 / math.sqrt(SIZE)

    for partner, ref in zip(order, in_refs):
        held[place(partner, parts)] = ref[...]

    def natural(number, pair):
        return held[rows_of(pair, parts), rows_of(number, rows)].reshape(patches, LANES)

    info = [held[part, 4 * rows : 4 * rows + INFO] for part in range(parts)]
    sides = [interleave(info[part], info[part + 1]) for part in range(0, parts, 2)]
    first = jnp.concatenate([side[0] for side in sides], axis=1)
    last = jnp.concatenate([side[1] for side in sides], axis=1)
    key_block = (lax.broadcasted_iota(jnp.int32, (patches, patches), 0) // BLK).astype(jnp.float32)
    seen = key_block == first[0:1]
    for column in range(1, columns):
        of = first if column < INFO else last
        seen = seen | (key_block == of[column % INFO : column % INFO + 1])
    bias[...] = jnp.where(seen, 0.0, -jnp.inf)

    for pair in range(pairs):
        at = rows_of(pair, LANES)
        qt[at] = natural(0, pair).T * scale
        kt[at] = natural(1, pair).T
        vt[at] = natural(2, pair).T
        ct[at] = natural(3, pair).T

    for frame in range(frames):
        tile = held[(frame // 2) * parts, 4 * rows : 4 * rows + INFO]
        _, tile = interleave(tile, tile)
        at = INFO - 2 + frame % 2
        lookback = tile[at : at + 1]
        for chunk in range(patches // LANES):
            cols = rows_of(chunk, LANES)
            query = qt[rows_of(frame, SIZE), cols]
            keys = visible_keys(frame)
            scores = []
            for key in keys:
                score = jnp.sum(query * kt[rows_of(key, SIZE), cols], axis=0, keepdims=True)
                scores.append(jnp.where(lookback > float(frame - key), score, -jnp.inf))
            top = scores[0]
            for score in scores[1:]:
                top = jnp.maximum(top, score)
            exps = [jnp.exp(score - top) for score in scores]
            total = exps[0]
            for term in exps[1:]:
                total = total + term
            value = jnp.zeros((SIZE, LANES), jnp.float32)
            for key, term in zip(keys, exps):
                weight = term / total
                wts[frame, frame - key : frame - key + 1, cols] = weight
                value = value + weight * vt[rows_of(key, SIZE), cols]
            tt[rows_of(frame, SIZE), cols] = value

    for pair in range(pairs):
        at = rows_of(pair, LANES)
        keys = natural(1, pair)
        high = keys.astype(jnp.bfloat16).astype(jnp.float32)
        low = keys - high
        mid = low.astype(jnp.bfloat16).astype(jnp.float32)
        upper = [x.astype(jnp.bfloat16) for x in interleave(high, mid)]
        lower = [x.astype(jnp.bfloat16) for x in interleave(high, low - mid)]
        value = tt[at].T
        high = value.astype(jnp.bfloat16).astype(jnp.float32)
        values = [x.astype(jnp.bfloat16) for x in interleave(high, value - high)]
        mixed = []
        for half in range(2):
            mine = rows_of(2 * pair + half, SIZE)
            query, grad = qt[mine], ct[mine]
            high, mid = split(query)
            low = query - high.astype(jnp.float32) - mid.astype(jnp.float32)
            low = low.astype(jnp.bfloat16)
            logits = dot(
                jnp.concatenate([upper[half]] * 2, axis=1),
                jnp.concatenate([high, high, mid, mid], axis=0),
                NN,
            )
            logits = logits + dot(lower[half], jnp.concatenate([low, high], axis=0), NN)
            logits = logits + bias[...]
            grad_weights = dot(jnp.concatenate([values[half]] * 2, axis=1), stacked(grad, 2), NN)
            top = jnp.max(logits, axis=0, keepdims=True)
            exps = jnp.exp(logits - top)
            share = 1.0 / jnp.sum(exps, axis=0, keepdims=True)
            high, low = split(exps)
            mix = heads_dot(tt[mine], high, low, NN) * share
            mixed.append(mix)
            gt[mine] = heads_dot(grad * share, high, low, NT)
            delta = jnp.sum(grad * mix, axis=0, keepdims=True)
            high, low = split(exps * (grad_weights - delta))
            gq[mine] = heads_dot(kt[mine], high, low, NN) * share
            gk[mine] = heads_dot(query * share, high, low, NT)
        mixed = jnp.concatenate(mixed, axis=0).T.reshape(parts, rows, LANES)
        done[rows_of(pair, parts), rows_of(0, rows)] = mixed

    gv[...] = jnp.zeros(gv.shape, jnp.float32)
    for frame in range(frames):
        mine = rows_of(frame, SIZE)
        for chunk in range(patches // LANES):
            cols = rows_of(chunk, LANES)
            query, grad = qt[mine, cols], gt[mine, cols]
            weights, terms = [], []
            inner = jnp.zeros((1, LANES), jnp.float32)
            for key in visible_keys(frame):
                weight = wts[frame, frame - key : frame - key + 1, cols]
                term = jnp.sum(grad * vt[rows_of(key, SIZE), cols], axis=0, keepdims=True)
                inner = inner + weight * term
                weights.append(weight)
                terms.append(term)
            grad_query = gq[mine, cols]
            for key, weight, term in zip(visible_keys(frame), weights, terms):
                of = rows_of(key, SIZE)
                score = weight * (term - inner)
                grad_query = grad_query + score * kt[of, cols]
                gk[of, cols] = gk[of, cols] + score * query
                gv[of, cols] = gv[of, cols] + weight * grad
            gq[mine, cols] = grad_query * scale

    for pair in range(pairs):
        at = rows_of(pair, LANES)
        for number, ref in enumerate((gq, gk, gv)):
            done[rows_of(pair, parts), rows_of(number + 1, rows)] = ref[at].T.reshape(
                parts, rows, LANES
            )
    for partner, ref in zip(order, out_refs):
        ref[...] = done[place(partner, parts)]


def exchange(blocks, order, patch_count):
    out = []
    for block, (frame, patch) in zip(blocks, order):
        pairs = [
            (i * patch_count + j, (i ^ frame) * patch_count + (j ^ patch))
            for i in range(H // patch_count)
            for j in range(patch_count)
        ]
        out.append(block if frame == patch == 0 else lax.ppermute(block, ("frame", "patch"), pairs))
    return out


def shards_by_head(queries, key_rows, value_rows, cotangent, lookback, window):
    frames_here, patches_here, model_width = queries.shape
    parts = lax.axis_size("patch")
    frames = frames_here * lax.axis_size("frame")
    patches = patches_here * parts
    order = partners(lax.axis_size("frame"), parts)
    vmem = pl.BlockSpec(memory_space=pltpu.VMEM)
    anywhere = pl.BlockSpec(memory_space=pl.ANY)

    def blocks(rows):
        return [jax.ShapeDtypeStruct((rows, LANES), jnp.float32)] * H

    def params(mebibytes):
        return pltpu.CompilerParams(vmem_limit_bytes=mebibytes * 1024 * 1024)

    packed = pl.pallas_call(
        lambda *refs: pack_kernel(order, parts, *refs),
        out_shape=blocks(4 * patches_here + INFO),
        in_specs=[anywhere] * 6,
        out_specs=[vmem] * H,
        scratch_shapes=[pltpu.VMEM(queries.shape, jnp.float32)] * 4
        + [
            pltpu.VMEM((H, 4 * patches_here, LANES), jnp.float32),
            pltpu.SMEM(window.shape, jnp.int32),
            pltpu.SMEM(lookback.shape, jnp.int32),
            pltpu.SemaphoreType.DMA((6,)),
        ],
        compiler_params=params(56),
        name="pack_heads",
    )(window, lookback, queries, key_rows, value_rows, cotangent)
    across = pltpu.VMEM((frames * SIZE, patches), jnp.float32)
    done = pl.pallas_call(
        lambda *refs: head_kernel(order, parts, window.shape[1], *refs),
        out_shape=blocks(4 * patches_here),
        in_specs=[vmem] * H,
        out_specs=[vmem] * H,
        scratch_shapes=[
            pltpu.VMEM((H, 4 * patches_here + INFO, LANES), jnp.float32),
            pltpu.VMEM((H, 4 * patches_here, LANES), jnp.float32),
        ]
        + [across] * 9
        + [
            pltpu.VMEM((frames, 8, patches), jnp.float32),
            pltpu.VMEM((patches, patches), jnp.float32),
        ],
        compiler_params=params(40),
        name="one_head",
    )(*exchange(packed, order, parts))
    return pl.pallas_call(
        lambda *refs: unpack_kernel(order, parts, *refs),
        out_shape=[jax.ShapeDtypeStruct(queries.shape, jnp.float32)] * 4,
        in_specs=[vmem] * H,
        out_specs=[vmem] * 4,
        scratch_shapes=[pltpu.VMEM((H, 4 * patches_here, LANES), jnp.float32)],
        compiler_params=params(40),
        name="unpack_heads",
    )(*exchange(done, order, parts))


def shards(queries, key_rows, value_rows, cotangent, lookback, window):
    frames_here, patches_here, model_width = queries.shape
    fits = (
        lax.axis_size("frame") * lax.axis_size("patch") == H
        and frames_here == 2
        and patches_here == SIZE
        and lax.axis_size("patch") in (2, 4, 8)
        and model_width == H * SIZE
    )
    form = shards_by_head if fits else shards_general
    return tuple(form(queries, key_rows, value_rows, cotangent, lookback, window))


def solution(mesh):
    rows = P(("traj", "frame"), "patch", None)
    return jax.shard_map(
        shards,
        mesh=mesh,
        in_specs=(rows, rows, rows, rows, P(("traj", "frame")), P(("traj", "patch"), None)),
        out_specs=(rows,) * 4,
        check_vma=False,
    )
```

profile of v0, /device:TPU:0, one launch (start us, length us, event | category | flops | bytes accessed | tf_op | source)
XLA Modules:
  0.0 116.0 jit_solution(3486552012771081609)
XLA Ops:
  0.6 3.4 %pack_heads.1 = (f32[264,128]{1,0:T(8,128)}, f32[264,128]{1,0:T(8,128)}, f32[264,128]{1,0:T(8,128)}, f32[264,128]{1,0:T(8,128)}, f32[264,128]{1,0:T(8,128)}, /*i...) custom-call(s32[4,12]{1,0:T(4,128)} %refs_0_.1, ...), custom_call_target="tpu_custom_call" | custom-call | tf_op jit(solution)/shard_map/pack_heads/pallas_call | solution.py:444
  4.0 3.1 %collective-permute-start = (f32[264,128]{1,0:T(8,128)}, f32[264,128]{1,0:T(8,128)S(1)}, u32[]{:S(2)}, u32[]{:S(2)}) collective-permute-start(f32[264,128]{1,0:T(8,128)} %get-tuple-element.37), channel_id=1, source_target_pairs={{0,1},{1,0},{2,3},{3,2},{4,5},{5,4},{6,7},{7,6},{8,9},{9,8},{10,11... | collective-permute-start | bytes 405512 | tf_op jit(solution)/shard_map/ppermute | solution.py:425
  7.1 2.6 %collective-permute-start.1 = (f32[264,128]{1,0:T(8,128)}, f32[264,128]{1,0:T(8,128)S(1)}, u32[]{:S(2)}, u32[]{:S(2)}) collective-permute-start(f32[264,128]{1,0:T(8,128)} %get-tuple-element.38), channel_id=1, source_target_pairs={{0,2},{1,3},{2,0},{3,1},{4,6},{5,7},{6,4},{7,5},{8,10},{9,11},{10,... | collective-permute-start | bytes 405512 | tf_op jit(solution)/shard_map/ppermute | solution.py:425
  9.7 1.0 collective-permute-start.4
  10.7 1.8 %collective-permute-done.refs_1_ = f32[264,128]{1,0:T(8,128)S(1)} collective-permute-done((f32[264,128]{1,0:T(8,128)}, f32[264,128]{1,0:T(8,128)S(1)}, u32[]{:S(2)}, u32[]{:S(2)}) %collective-permute-start) | collective-permute-done | bytes 135200 | tf_op jit(solution)/shard_map/ppermute | solution.py:425
  12.6 1.3 %collective-permute-start.5 = (f32[264,128]{1,0:T(8,128)}, f32[264,128]{1,0:T(8,128)S(1)}, u32[]{:S(2)}, u32[]{:S(2)}) collective-permute-start(f32[264,128]{1,0:T(8,128)} %get-tuple-element.42), channel_id=1, source_target_pairs={{0,6},{1,7},{2,4},{3,5},{4,2},{5,3},{6,0},{7,1},{8,14},{9,15},{10,... | collective-permute-start | bytes 405512 | tf_op jit(solution)/shard_map/ppermute | solution.py:425
  13.8 6.7 %collective-permute-done.1.refs_2_ = f32[264,128]{1,0:T(8,128)S(1)} collective-permute-done((f32[264,128]{1,0:T(8,128)}, f32[264,128]{1,0:T(8,128)S(1)}, u32[]{:S(2)}, u32[]{:S(2)}) %collective-permute-start.1) | collective-permute-done | bytes 135200 | tf_op jit(solution)/shard_map/ppermute | solution.py:425
  20.6 1.5 %collective-permute-start.7 = (f32[264,128]{1,0:T(8,128)}, f32[264,128]{1,0:T(8,128)S(1)}, u32[]{:S(2)}, u32[]{:S(2)}) collective-permute-start(f32[264,128]{1,0:T(8,128)} %get-tuple-element.44), channel_id=1, source_target_pairs={{0,8},{1,9},{2,10},{3,11},{4,12},{5,13},{6,14},{7,15},{8,0},{9,1},... | collective-permute-start | bytes 405512 | tf_op jit(solution)/shard_map/ppermute | solution.py:425
  22.1 9.2 %collective-permute-start.8 = (f32[264,128]{1,0:T(8,128)}, f32[264,128]{1,0:T(8,128)S(1)}, u32[]{:S(2)}, u32[]{:S(2)}) collective-permute-start(f32[264,128]{1,0:T(8,128)} %get-tuple-element.45), channel_id=1, source_target_pairs={{0,9},{1,8},{2,11},{3,10},{4,13},{5,12},{6,15},{7,14},{8,1},{9,0},... | collective-permute-start | bytes 405512 | tf_op jit(solution)/shard_map/ppermute | solution.py:425
  31.3 0.9 collective-permute-start.9
  32.2 2.5 %collective-permute-start.10 = (f32[264,128]{1,0:T(8,128)}, f32[264,128]{1,0:T(8,128)S(1)}, u32[]{:S(2)}, u32[]{:S(2)}) collective-permute-start(f32[264,128]{1,0:T(8,128)} %get-tuple-element.47), channel_id=1, source_target_pairs={{0,11},{1,10},{2,9},{3,8},{4,15},{5,14},{6,13},{7,12},{8,3},{9,2},... | collective-permute-start | bytes 405512 | tf_op jit(solution)/shard_map/ppermute | solution.py:425
  34.7 2.2 %collective-permute-start.11 = (f32[264,128]{1,0:T(8,128)}, f32[264,128]{1,0:T(8,128)S(1)}, u32[]{:S(2)}, u32[]{:S(2)}) collective-permute-start(f32[264,128]{1,0:T(8,128)} %get-tuple-element.48), channel_id=1, source_target_pairs={{0,12},{1,13},{2,14},{3,15},{4,8},{5,9},{6,10},{7,11},{8,4},{9,5},... | collective-permute-start | bytes 405512 | tf_op jit(solution)/shard_map/ppermute | solution.py:425
  36.8 1.8 %collective-permute-start.12 = (f32[264,128]{1,0:T(8,128)}, f32[264,128]{1,0:T(8,128)S(1)}, u32[]{:S(2)}, u32[]{:S(2)}) collective-permute-start(f32[264,128]{1,0:T(8,128)} %get-tuple-element.49), channel_id=1, source_target_pairs={{0,13},{1,12},{2,15},{3,14},{4,9},{5,8},{6,11},{7,10},{8,5},{9,4},... | collective-permute-start | bytes 405512 | tf_op jit(solution)/shard_map/ppermute | solution.py:425
  38.6 4.1 %collective-permute-start.13 = (f32[264,128]{1,0:T(8,128)}, f32[264,128]{1,0:T(8,128)S(1)}, u32[]{:S(2)}, u32[]{:S(2)}) collective-permute-start(f32[264,128]{1,0:T(8,128)} %get-tuple-element.50), channel_id=1, source_target_pairs={{0,14},{1,15},{2,12},{3,13},{4,10},{5,11},{6,8},{7,9},{8,6},{9,7},... | collective-permute-start | bytes 405512 | tf_op jit(solution)/shard_map/ppermute | solution.py:425
  42.7 2.0 %collective-permute-done.9.refs_10_ = f32[264,128]{1,0:T(8,128)S(1)} collective-permute-done((f32[264,128]{1,0:T(8,128)}, f32[264,128]{1,0:T(8,128)S(1)}, u32[]{:S(2)}, u32[]{:S(2)}) %collective-permute-start.9) | collective-permute-done | bytes 135200 | tf_op jit(solution)/shard_map/ppermute | solution.py:425
  45.4 5.1 %collective-permute-done.11.refs_12_ = f32[264,128]{1,0:T(8,128)S(1)} collective-permute-done((f32[264,128]{1,0:T(8,128)}, f32[264,128]{1,0:T(8,128)S(1)}, u32[]{:S(2)}, u32[]{:S(2)}) %collective-permute-start.11) | collective-permute-done | bytes 135200 | tf_op jit(solution)/shard_map/ppermute | solution.py:425
  50.5 5.2 %collective-permute-done.14.refs_15_ = f32[264,128]{1,0:T(8,128)S(1)} collective-permute-done((f32[264,128]{1,0:T(8,128)}, f32[264,128]{1,0:T(8,128)S(1)}, u32[]{:S(2)}, u32[]{:S(2)}) %collective-permute-start.14) | collective-permute-done | bytes 135200 | tf_op jit(solution)/shard_map/ppermute | solution.py:425
  55.7 0.9 copy-done
  56.6 5.8 %one_head.1 = (f32[256,128]{1,0:T(8,128)S(1)}, f32[256,128]{1,0:T(8,128)S(1)}, f32[256,128]{1,0:T(8,128)S(1)}, f32[256,128]{1,0:T(8,128)S(1)}, f32[256,128]{1,0:...) custom-call(f32[264,128]{1,0:T(8,128)S(1)} %copy-done, ...), custom_call_target="tpu_custom_call" | custom-call | tf_op jit(solution)/shard_map/one_head/pallas_call | solution.py:460
  62.4 2.7 %collective-permute-start.15 = (f32[256,128]{1,0:T(8,128)S(1)}, f32[256,128]{1,0:T(8,128)S(1)}, u32[]{:S(2)}, u32[]{:S(2)}) collective-permute-start(f32[256,128]{1,0:T(8,128)S(1)} %get-tuple-element.53), channel_id=1, source_target_pairs={{0,1},{1,0},{2,3},{3,2},{4,5},{5,4},{6,7},{7,6},{8,9},{9,8},{10,11... | collective-permute-start | bytes 393224 | tf_op jit(solution)/shard_map/ppermute | solution.py:425
  65.1 1.3 %collective-permute-start.16 = (f32[256,128]{1,0:T(8,128)S(1)}, f32[256,128]{1,0:T(8,128)S(1)}, u32[]{:S(2)}, u32[]{:S(2)}) collective-permute-start(f32[256,128]{1,0:T(8,128)S(1)} %get-tuple-element.54), channel_id=1, source_target_pairs={{0,2},{1,3},{2,0},{3,1},{4,6},{5,7},{6,4},{7,5},{8,10},{9,11},{10,... | collective-permute-start | bytes 393224 | tf_op jit(solution)/shard_map/ppermute | solution.py:425
  66.4 1.4 %collective-permute-start.17 = (f32[256,128]{1,0:T(8,128)S(1)}, f32[256,128]{1,0:T(8,128)S(1)}, u32[]{:S(2)}, u32[]{:S(2)}) collective-permute-start(f32[256,128]{1,0:T(8,128)S(1)} %get-tuple-element.55), channel_id=1, source_target_pairs={{0,3},{1,2},{2,1},{3,0},{4,7},{5,6},{6,5},{7,4},{8,11},{9,10},{10,... | collective-permute-start | bytes 393224 | tf_op jit(solution)/shard_map/ppermute | solution.py:425
  67.8 1.0 collective-permute-start.19
  68.7 2.0 %collective-permute-done.15.refs_1_ = f32[256,128]{1,0:T(8,128)S(1)} collective-permute-done((f32[256,128]{1,0:T(8,128)S(1)}, f32[256,128]{1,0:T(8,128)S(1)}, u32[]{:S(2)}, u32[]{:S(2)}) %collective-permute-start.15) | collective-permute-done | bytes 131104 | tf_op jit(solution)/shard_map/ppermute | solution.py:425
  70.9 7.2 %collective-permute-done.16.refs_2_ = f32[256,128]{1,0:T(8,128)S(1)} collective-permute-done((f32[256,128]{1,0:T(8,128)S(1)}, f32[256,128]{1,0:T(8,128)S(1)}, u32[]{:S(2)}, u32[]{:S(2)}) %collective-permute-start.16) | collective-permute-done | bytes 131104 | tf_op jit(solution)/shard_map/ppermute | solution.py:425
  79.3 9.2 %collective-permute-start.23 = (f32[256,128]{1,0:T(8,128)S(1)}, f32[256,128]{1,0:T(8,128)S(1)}, u32[]{:S(2)}, u32[]{:S(2)}) collective-permute-start(f32[256,128]{1,0:T(8,128)S(1)} %get-tuple-element.61), channel_id=1, source_target_pairs={{0,9},{1,8},{2,11},{3,10},{4,13},{5,12},{6,15},{7,14},{8,1},{9,0},... | collective-permute-start | bytes 393224 | tf_op jit(solution)/shard_map/ppermute | solution.py:425
  89.4 2.2 %collective-permute-start.25 = (f32[256,128]{1,0:T(8,128)S(1)}, f32[256,128]{1,0:T(8,128)S(1)}, u32[]{:S(2)}, u32[]{:S(2)}) collective-permute-start(f32[256,128]{1,0:T(8,128)S(1)} %get-tuple-element.63), channel_id=1, source_target_pairs={{0,11},{1,10},{2,9},{3,8},{4,15},{5,14},{6,13},{7,12},{8,3},{9,2},... | collective-permute-start | bytes 393224 | tf_op jit(solution)/shard_map/ppermute | solution.py:425
  92.2 2.3 %collective-permute-start.27 = (f32[256,128]{1,0:T(8,128)S(1)}, f32[256,128]{1,0:T(8,128)S(1)}, u32[]{:S(2)}, u32[]{:S(2)}) collective-permute-start(f32[256,128]{1,0:T(8,128)S(1)} %get-tuple-element.65), channel_id=1, source_target_pairs={{0,13},{1,12},{2,15},{3,14},{4,9},{5,8},{6,11},{7,10},{8,5},{9,4},... | collective-permute-start | bytes 393224 | tf_op jit(solution)/shard_map/ppermute | solution.py:425
  95.0 11.8 %collective-permute-done.24.refs_10_ = f32[256,128]{1,0:T(8,128)S(1)} collective-permute-done((f32[256,128]{1,0:T(8,128)S(1)}, f32[256,128]{1,0:T(8,128)S(1)}, u32[]{:S(2)}, u32[]{:S(2)}) %collective-permute-start.24) | collective-permute-done | bytes 131104 | tf_op jit(solution)/shard_map/ppermute | solution.py:425
  106.8 2.9 %collective-permute-done.28.refs_14_ = f32[256,128]{1,0:T(8,128)S(1)} collective-permute-done((f32[256,128]{1,0:T(8,128)S(1)}, f32[256,128]{1,0:T(8,128)S(1)}, u32[]{:S(2)}, u32[]{:S(2)}) %collective-permute-start.28) | collective-permute-done | bytes 131104 | tf_op jit(solution)/shard_map/ppermute | solution.py:425
  109.7 4.3 %collective-permute-done.29.refs_15_ = f32[256,128]{1,0:T(8,128)S(1)} collective-permute-done((f32[256,128]{1,0:T(8,128)S(1)}, f32[256,128]{1,0:T(8,128)S(1)}, u32[]{:S(2)}, u32[]{:S(2)}) %collective-permute-start.29) | collective-permute-done | bytes 131104 | tf_op jit(solution)/shard_map/ppermute | solution.py:425
  114.0 2.0 %unpack_heads.1 = (f32[2,64,1024]{2,1,0:T(8,128)}, f32[2,64,1024]{2,1,0:T(8,128)}, f32[2,64,1024]{2,1,0:T(8,128)}, f32[2,64,1024]{2,1,0:T(8,128)}) custom-call(f32[256,128]{1,0:T(8,128)S(1)} %get-tuple-element.52.refs_0_, f32[256,128]{1,0:T(8,128)S(1)} %collective-permute-done.15.refs_1_, f32[256,128]{1,0:T(8,128)S(1)} %collective-permute-done.16.refs_2_, ...), custom_call_target="tpu_custom_call" | custom-call | tf_op jit(solution)/shard_map/unpack_heads/pallas_call | solution.py:477
  (33 shorter events, 3.9 us)
Async XLA Ops:
  4.0 8.5 %collective-permute-start = (f32[264,128]{1,0:T(8,128)}, f32[264,128]{1,0:T(8,128)S(1)}, u32[]{:S(2)}, u32[]{:S(2)}) collective-permute-start(f32[264,128]{1,0:T(8,128)} %get-tuple-element.37), channel_id=1, source_target_pairs={{0,1},{1,0},{2,3},{3,2},{4,5},{5,4},{6,7},{7,6},{8,9},{9,8},{10,11... | collective-permute-start | bytes 405512 | tf_op jit(solution)/shard_map/ppermute | solution.py:425
  7.1 13.4 %collective-permute-start.1 = (f32[264,128]{1,0:T(8,128)}, f32[264,128]{1,0:T(8,128)S(1)}, u32[]{:S(2)}, u32[]{:S(2)}) collective-permute-start(f32[264,128]{1,0:T(8,128)} %get-tuple-element.38), channel_id=1, source_target_pairs={{0,2},{1,3},{2,0},{3,1},{4,6},{5,7},{6,4},{7,5},{8,10},{9,11},{10,... | collective-permute-start | bytes 405512 | tf_op jit(solution)/shard_map/ppermute | solution.py:425
  9.7 10.8 %collective-permute-start.2 = (f32[264,128]{1,0:T(8,128)}, f32[264,128]{1,0:T(8,128)S(1)}, u32[]{:S(2)}, u32[]{:S(2)}) collective-permute-start(f32[264,128]{1,0:T(8,128)} %get-tuple-element.39), channel_id=1, source_target_pairs={{0,3},{1,2},{2,1},{3,0},{4,7},{5,6},{6,5},{7,4},{8,11},{9,10},{10,... | collective-permute-start | bytes 405512 | tf_op jit(solution)/shard_map/ppermute | solution.py:425
  9.7 12.4 %collective-permute-start.3 = (f32[264,128]{1,0:T(8,128)}, f32[264,128]{1,0:T(8,128)S(1)}, u32[]{:S(2)}, u32[]{:S(2)}) collective-permute-start(f32[264,128]{1,0:T(8,128)} %get-tuple-element.40), channel_id=1, source_target_pairs={{0,4},{1,5},{2,6},{3,7},{4,0},{5,1},{6,2},{7,3},{8,12},{9,13},{10,... | collective-permute-start | bytes 405512 | tf_op jit(solution)/shard_map/ppermute | solution.py:425
  9.7 21.5 %collective-permute-start.4 = (f32[264,128]{1,0:T(8,128)}, f32[264,128]{1,0:T(8,128)S(1)}, u32[]{:S(2)}, u32[]{:S(2)}) collective-permute-start(f32[264,128]{1,0:T(8,128)} %get-tuple-element.41), channel_id=1, source_target_pairs={{0,5},{1,4},{2,7},{3,6},{4,1},{5,0},{6,3},{7,2},{8,13},{9,12},{10,... | collective-permute-start | bytes 405512 | tf_op jit(solution)/shard_map/ppermute | solution.py:425
  12.6 19.6 %collective-permute-start.5 = (f32[264,128]{1,0:T(8,128)}, f32[264,128]{1,0:T(8,128)S(1)}, u32[]{:S(2)}, u32[]{:S(2)}) collective-permute-start(f32[264,128]{1,0:T(8,128)} %get-tuple-element.42), channel_id=1, source_target_pairs={{0,6},{1,7},{2,4},{3,5},{4,2},{5,3},{6,0},{7,1},{8,14},{9,15},{10,... | collective-permute-start | bytes 405512 | tf_op jit(solution)/shard_map/ppermute | solution.py:425
  20.5 14.1 %collective-permute-start.6 = (f32[264,128]{1,0:T(8,128)}, f32[264,128]{1,0:T(8,128)S(1)}, u32[]{:S(2)}, u32[]{:S(2)}) collective-permute-start(f32[264,128]{1,0:T(8,128)} %get-tuple-element.43), channel_id=1, source_target_pairs={{0,7},{1,6},{2,5},{3,4},{4,3},{5,2},{6,1},{7,0},{8,15},{9,14},{10,... | collective-permute-start | bytes 405512 | tf_op jit(solution)/shard_map/ppermute | solution.py:425
  20.6 16.3 %collective-permute-start.7 = (f32[264,128]{1,0:T(8,128)}, f32[264,128]{1,0:T(8,128)S(1)}, u32[]{:S(2)}, u32[]{:S(2)}) collective-permute-start(f32[264,128]{1,0:T(8,128)} %get-tuple-element.44), channel_id=1, source_target_pairs={{0,8},{1,9},{2,10},{3,11},{4,12},{5,13},{6,14},{7,15},{8,0},{9,1},... | collective-permute-start | bytes 405512 | tf_op jit(solution)/shard_map/ppermute | solution.py:425
  22.1 16.5 %collective-permute-start.8 = (f32[264,128]{1,0:T(8,128)}, f32[264,128]{1,0:T(8,128)S(1)}, u32[]{:S(2)}, u32[]{:S(2)}) collective-permute-start(f32[264,128]{1,0:T(8,128)} %get-tuple-element.45), channel_id=1, source_target_pairs={{0,9},{1,8},{2,11},{3,10},{4,13},{5,12},{6,15},{7,14},{8,1},{9,0},... | collective-permute-start | bytes 405512 | tf_op jit(solution)/shard_map/ppermute | solution.py:425
  31.3 13.5 %collective-permute-start.9 = (f32[264,128]{1,0:T(8,128)}, f32[264,128]{1,0:T(8,128)S(1)}, u32[]{:S(2)}, u32[]{:S(2)}) collective-permute-start(f32[264,128]{1,0:T(8,128)} %get-tuple-element.46), channel_id=1, source_target_pairs={{0,10},{1,11},{2,8},{3,9},{4,14},{5,15},{6,12},{7,13},{8,2},{9,3},... | collective-permute-start | bytes 405512 | tf_op jit(solution)/shard_map/ppermute | solution.py:425
  32.2 13.2 %collective-permute-start.10 = (f32[264,128]{1,0:T(8,128)}, f32[264,128]{1,0:T(8,128)S(1)}, u32[]{:S(2)}, u32[]{:S(2)}) collective-permute-start(f32[264,128]{1,0:T(8,128)} %get-tuple-element.47), channel_id=1, source_target_pairs={{0,11},{1,10},{2,9},{3,8},{4,15},{5,14},{6,13},{7,12},{8,3},{9,2},... | collective-permute-start | bytes 405512 | tf_op jit(solution)/shard_map/ppermute | solution.py:425
  34.7 15.8 %collective-permute-start.11 = (f32[264,128]{1,0:T(8,128)}, f32[264,128]{1,0:T(8,128)S(1)}, u32[]{:S(2)}, u32[]{:S(2)}) collective-permute-start(f32[264,128]{1,0:T(8,128)} %get-tuple-element.48), channel_id=1, source_target_pairs={{0,12},{1,13},{2,14},{3,15},{4,8},{5,9},{6,10},{7,11},{8,4},{9,5},... | collective-permute-start | bytes 405512 | tf_op jit(solution)/shard_map/ppermute | solution.py:425
  36.8 13.6 %collective-permute-start.12 = (f32[264,128]{1,0:T(8,128)}, f32[264,128]{1,0:T(8,128)S(1)}, u32[]{:S(2)}, u32[]{:S(2)}) collective-permute-start(f32[264,128]{1,0:T(8,128)} %get-tuple-element.49), channel_id=1, source_target_pairs={{0,13},{1,12},{2,15},{3,14},{4,9},{5,8},{6,11},{7,10},{8,5},{9,4},... | collective-permute-start | bytes 405512 | tf_op jit(solution)/shard_map/ppermute | solution.py:425
  38.6 11.9 %collective-permute-start.13 = (f32[264,128]{1,0:T(8,128)}, f32[264,128]{1,0:T(8,128)S(1)}, u32[]{:S(2)}, u32[]{:S(2)}) collective-permute-start(f32[264,128]{1,0:T(8,128)} %get-tuple-element.50), channel_id=1, source_target_pairs={{0,14},{1,15},{2,12},{3,13},{4,10},{5,11},{6,8},{7,9},{8,6},{9,7},... | collective-permute-start | bytes 405512 | tf_op jit(solution)/shard_map/ppermute | solution.py:425
  44.8 10.9 %collective-permute-start.14 = (f32[264,128]{1,0:T(8,128)}, f32[264,128]{1,0:T(8,128)S(1)}, u32[]{:S(2)}, u32[]{:S(2)}) collective-permute-start(f32[264,128]{1,0:T(8,128)} %get-tuple-element.51), channel_id=1, source_target_pairs={{0,15},{1,14},{2,13},{3,12},{4,11},{5,10},{6,9},{7,8},{8,7},{9,6},... | collective-permute-start | bytes 405512 | tf_op jit(solution)/shard_map/ppermute | solution.py:425
  55.7 0.9 copy-start
  62.4 8.3 %collective-permute-start.15 = (f32[256,128]{1,0:T(8,128)S(1)}, f32[256,128]{1,0:T(8,128)S(1)}, u32[]{:S(2)}, u32[]{:S(2)}) collective-permute-start(f32[256,128]{1,0:T(8,128)S(1)} %get-tuple-element.53), channel_id=1, source_target_pairs={{0,1},{1,0},{2,3},{3,2},{4,5},{5,4},{6,7},{7,6},{8,9},{9,8},{10,11... | collective-permute-start | bytes 393224 | tf_op jit(solution)/shard_map/ppermute | solution.py:425
  65.1 12.9 %collective-permute-start.16 = (f32[256,128]{1,0:T(8,128)S(1)}, f32[256,128]{1,0:T(8,128)S(1)}, u32[]{:S(2)}, u32[]{:S(2)}) collective-permute-start(f32[256,128]{1,0:T(8,128)S(1)} %get-tuple-element.54), channel_id=1, source_target_pairs={{0,2},{1,3},{2,0},{3,1},{4,6},{5,7},{6,4},{7,5},{8,10},{9,11},{10,... | collective-permute-start | bytes 393224 | tf_op jit(solution)/shard_map/ppermute | solution.py:425
  66.4 12.3 %collective-permute-start.17 = (f32[256,128]{1,0:T(8,128)S(1)}, f32[256,128]{1,0:T(8,128)S(1)}, u32[]{:S(2)}, u32[]{:S(2)}) collective-permute-start(f32[256,128]{1,0:T(8,128)S(1)} %get-tuple-element.55), channel_id=1, source_target_pairs={{0,3},{1,2},{2,1},{3,0},{4,7},{5,6},{6,5},{7,4},{8,11},{9,10},{10,... | collective-permute-start | bytes 393224 | tf_op jit(solution)/shard_map/ppermute | solution.py:425
  67.8 11.5 %collective-permute-start.18 = (f32[256,128]{1,0:T(8,128)S(1)}, f32[256,128]{1,0:T(8,128)S(1)}, u32[]{:S(2)}, u32[]{:S(2)}) collective-permute-start(f32[256,128]{1,0:T(8,128)S(1)} %get-tuple-element.56), channel_id=1, source_target_pairs={{0,4},{1,5},{2,6},{3,7},{4,0},{5,1},{6,2},{7,3},{8,12},{9,13},{10,... | collective-permute-start | bytes 393224 | tf_op jit(solution)/shard_map/ppermute | solution.py:425
  67.8 20.7 %collective-permute-start.19 = (f32[256,128]{1,0:T(8,128)S(1)}, f32[256,128]{1,0:T(8,128)S(1)}, u32[]{:S(2)}, u32[]{:S(2)}) collective-permute-start(f32[256,128]{1,0:T(8,128)S(1)} %get-tuple-element.57), channel_id=1, source_target_pairs={{0,5},{1,4},{2,7},{3,6},{4,1},{5,0},{6,3},{7,2},{8,13},{9,12},{10,... | collective-permute-start | bytes 393224 | tf_op jit(solution)/shard_map/ppermute | solution.py:425
  70.7 18.6 %collective-permute-start.20 = (f32[256,128]{1,0:T(8,128)S(1)}, f32[256,128]{1,0:T(8,128)S(1)}, u32[]{:S(2)}, u32[]{:S(2)}) collective-permute-start(f32[256,128]{1,0:T(8,128)S(1)} %get-tuple-element.58), channel_id=1, source_target_pairs={{0,6},{1,7},{2,4},{3,5},{4,2},{5,3},{6,0},{7,1},{8,14},{9,15},{10,... | collective-permute-start | bytes 393224 | tf_op jit(solution)/shard_map/ppermute | solution.py:425
  78.0 13.5 %collective-permute-start.21 = (f32[256,128]{1,0:T(8,128)S(1)}, f32[256,128]{1,0:T(8,128)S(1)}, u32[]{:S(2)}, u32[]{:S(2)}) collective-permute-start(f32[256,128]{1,0:T(8,128)S(1)} %get-tuple-element.59), channel_id=1, source_target_pairs={{0,7},{1,6},{2,5},{3,4},{4,3},{5,2},{6,1},{7,0},{8,15},{9,14},{10,... | collective-permute-start | bytes 393224 | tf_op jit(solution)/shard_map/ppermute | solution.py:425
  78.7 13.5 %collective-permute-start.22 = (f32[256,128]{1,0:T(8,128)S(1)}, f32[256,128]{1,0:T(8,128)S(1)}, u32[]{:S(2)}, u32[]{:S(2)}) collective-permute-start(f32[256,128]{1,0:T(8,128)S(1)} %get-tuple-element.60), channel_id=1, source_target_pairs={{0,8},{1,9},{2,10},{3,11},{4,12},{5,13},{6,14},{7,15},{8,0},{9,1},... | collective-permute-start | bytes 393224 | tf_op jit(solution)/shard_map/ppermute | solution.py:425
  79.3 15.2 %collective-permute-start.23 = (f32[256,128]{1,0:T(8,128)S(1)}, f32[256,128]{1,0:T(8,128)S(1)}, u32[]{:S(2)}, u32[]{:S(2)}) collective-permute-start(f32[256,128]{1,0:T(8,128)S(1)} %get-tuple-element.61), channel_id=1, source_target_pairs={{0,9},{1,8},{2,11},{3,10},{4,13},{5,12},{6,15},{7,14},{8,1},{9,0},... | collective-permute-start | bytes 393224 | tf_op jit(solution)/shard_map/ppermute | solution.py:425
  88.5 18.3 %collective-permute-start.24 = (f32[256,128]{1,0:T(8,128)S(1)}, f32[256,128]{1,0:T(8,128)S(1)}, u32[]{:S(2)}, u32[]{:S(2)}) collective-permute-start(f32[256,128]{1,0:T(8,128)S(1)} %get-tuple-element.62), channel_id=1, source_target_pairs={{0,10},{1,11},{2,8},{3,9},{4,14},{5,15},{6,12},{7,13},{8,2},{9,3},... | collective-permute-start | bytes 393224 | tf_op jit(solution)/shard_map/ppermute | solution.py:425
  89.4 17.4 %collective-permute-start.25 = (f32[256,128]{1,0:T(8,128)S(1)}, f32[256,128]{1,0:T(8,128)S(1)}, u32[]{:S(2)}, u32[]{:S(2)}) collective-permute-start(f32[256,128]{1,0:T(8,128)S(1)} %get-tuple-element.63), channel_id=1, source_target_pairs={{0,11},{1,10},{2,9},{3,8},{4,15},{5,14},{6,13},{7,12},{8,3},{9,2},... | collective-permute-start | bytes 393224 | tf_op jit(solution)/shard_map/ppermute | solution.py:425
  91.6 15.2 %collective-permute-start.26 = (f32[256,128]{1,0:T(8,128)S(1)}, f32[256,128]{1,0:T(8,128)S(1)}, u32[]{:S(2)}, u32[]{:S(2)}) collective-permute-start(f32[256,128]{1,0:T(8,128)S(1)} %get-tuple-element.64), channel_id=1, source_target_pairs={{0,12},{1,13},{2,14},{3,15},{4,8},{5,9},{6,10},{7,11},{8,4},{9,5},... | collective-permute-start | bytes 393224 | tf_op jit(solution)/shard_map/ppermute | solution.py:425
  92.2 14.6 %collective-permute-start.27 = (f32[256,128]{1,0:T(8,128)S(1)}, f32[256,128]{1,0:T(8,128)S(1)}, u32[]{:S(2)}, u32[]{:S(2)}) collective-permute-start(f32[256,128]{1,0:T(8,128)S(1)} %get-tuple-element.65), channel_id=1, source_target_pairs={{0,13},{1,12},{2,15},{3,14},{4,9},{5,8},{6,11},{7,10},{8,5},{9,4},... | collective-permute-start | bytes 393224 | tf_op jit(solution)/shard_map/ppermute | solution.py:425
  94.4 15.3 %collective-permute-start.28 = (f32[256,128]{1,0:T(8,128)S(1)}, f32[256,128]{1,0:T(8,128)S(1)}, u32[]{:S(2)}, u32[]{:S(2)}) collective-permute-start(f32[256,128]{1,0:T(8,128)S(1)} %get-tuple-element.66), channel_id=1, source_target_pairs={{0,14},{1,15},{2,12},{3,13},{4,10},{5,11},{6,8},{7,9},{8,6},{9,7},... | collective-permute-start | bytes 393224 | tf_op jit(solution)/shard_map/ppermute | solution.py:425
  106.8 7.2 %collective-permute-start.29 = (f32[256,128]{1,0:T(8,128)S(1)}, f32[256,128]{1,0:T(8,128)S(1)}, u32[]{:S(2)}, u32[]{:S(2)}) collective-permute-start(f32[256,128]{1,0:T(8,128)S(1)} %get-tuple-element.67), channel_id=1, source_target_pairs={{0,15},{1,14},{2,13},{3,12},{4,11},{5,10},{6,9},{7,8},{8,7},{9,6},... | collective-permute-start | bytes 393224 | tf_op jit(solution)/shard_map/ppermute | solution.py:425
where the time goes:
time: 116 us
  starting transfers between devices  54 us (47%)
  waiting for transfers between devices  49.2 us (42%)
  Pallas kernels  11.2 us (10%)
    ppermute x30, starting transfers between devices, exchange(): lax.ppermute(block, ('frame', 'patch'), pairs)  54 us
    ppermute x30, waiting for transfers between devices, exchange(): lax.ppermute(block, ('frame', 'patch'), pairs)  49.2 us
    pallas_call x1, Pallas kernels, shards_by_head(): pl.pallas_call(lambda *refs: head_kernel(order, parts, window.shape[1], *...  5.83 us
    pallas_call x1, Pallas kernels, shards_by_head(): pl.pallas_call(lambda *refs: pack_kernel(order, parts, *refs), out_shape=...  3.4 us
  transfers between devices with their start and end apart: 30, of which 10 were waited for; matrix products, arithmetic and copies ran while one was open for 0% of the time, Pallas kernels for 0%

commit v1 on v0

--- a/solution.py
+++ b/solution.py
@@ -218,31 +218,41 @@
 
 
 def partners(frame_count, patch_count):
-    return [(frame, patch) for frame in range(frame_count) for patch in range(patch_count)]
+    every = [(frame, patch) for frame in range(frame_count) for patch in range(patch_count)]
+    far = [at for at in every if at[1] >= patch_count // 2]
+    near = [at for at in every[1:] if at[1] < patch_count // 2]
+    order = every[:1] + far[:1]
+    for number, at in enumerate(far[1:]):
+        share = slice(number * len(near) // len(far[1:]), (number + 1) * len(near) // len(far[1:]))
+        order += near[share] + [at] if number else [at] + near[share]
+    return order
 
 
 def place(partner, patch_count):
-    frame = lax.bitwise_xor(lax.axis_index("frame"), partner[0])
-    return frame * patch_count + lax.bitwise_xor(lax.axis_index("patch"), partner[1])
+    return (
+        lax.bitwise_xor(lax.axis_index("frame"), partner[0]),
+        lax.bitwise_xor(lax.axis_index("patch"), partner[1]),
+    )
+
+
+def low_lanes(rows):
+    return lax.broadcasted_iota(jnp.int32, (rows, LANES), 1) < SIZE
+
+
+def head_columns(head):
+    return pl.ds(pl.multiple_of(head // 2 * LANES, LANES), LANES)
 
 
 def pack_kernel(order, patch_count, window, lookback, *refs):
     arrays, out_refs = refs[:4], refs[4 : 4 + H]
-    held, (packed, window_ref, lookback_ref, sems) = refs[4 + H : 8 + H], refs[8 + H :]
-    moves = list(zip((*arrays, window, lookback), (*held, window_ref, lookback_ref)))
+    held, (window_ref, lookback_ref, sems) = refs[4 + H : 8 + H], refs[8 + H :]
+    moves = list(zip((window, lookback, *arrays), (window_ref, lookback_ref, *held)))
     copies = [pltpu.make_async_copy(a, b, sems.at[n]) for n, (a, b) in enumerate(moves)]
     for copy in copies:
         copy.start()
+    copies[0].wait()
+    copies[1].wait()
     rows = held[0].shape[1]
-    for number, (copy, ref) in enumerate(zip(copies, held)):
-        copy.wait()
-        for pair in range(H // 2):
-            cols = rows_of(pair, LANES)
-            packed[2 * pair, rows_of(number, rows)], packed[2 * pair + 1, rows_of(number, rows)] = (
-                interleave(ref[0, :, cols], ref[1, :, cols])
-            )
-    copies[4].wait()
-    copies[5].wait()
     row = lax.broadcasted_iota(jnp.int32, (INFO, LANES), 0)
     lane = lax.broadcasted_iota(jnp.int32, (INFO, LANES), 1)
     info = jnp.zeros((INFO, LANES), jnp.int32)
@@ -255,23 +265,46 @@
         here = (row == INFO - 2 + frame) & (lane >= SIZE)
         info = jnp.where(here, lookback_ref[frame], info)
     info = info.astype(jnp.float32)
-    for partner, ref in zip(order, out_refs):
-        ref[: 4 * rows] = packed[place(partner, patch_count)]
-        ref[4 * rows :] = info
+    for ref in out_refs:
+        if ref.shape[0] > 4 * rows:
+            ref[4 * rows :] = info
+    low = low_lanes(rows).astype(jnp.int32)
+    for number, (copy, ref) in enumerate(zip(copies[2:], held)):
+        copy.wait()
+        for partner, out_ref in zip(order, out_refs):
+            frame, patch = place(partner, patch_count)
+            head = frame * patch_count + patch
+            odd = head % 2
+            cols = head_columns(head)
+            kept, moved = ref[odd, :, cols], ref[1 - odd, :, cols]
+            out_ref[rows_of(number, rows)] = jnp.where(
+                low != odd, kept, pltpu.roll(moved, SIZE, 1)
+            )
 
 
 def unpack_kernel(order, patch_count, *refs):
-    in_refs, out_refs, packed = refs[:H], refs[H:-1], refs[-1]
-    rows = out_refs[0].shape[1]
-    for partner, ref in zip(order, in_refs):
-        packed[place(partner, patch_count)] = ref[...]
-    for pair in range(H // 2):
-        cols = rows_of(pair, LANES)
-        for number, ref in enumerate(out_refs):
-            at = rows_of(number, rows)
-            ref[0, :, cols], ref[1, :, cols] = interleave(
-                packed[2 * pair, at], packed[2 * pair + 1, at]
-            )
+    in_refs, out_refs, held, sems = refs[:H], refs[H : H + 4], refs[H + 4 : H + 8], refs[H + 8]
+    rows = held[0].shape[1]
+    low = low_lanes(rows)
+    copies = []
+    for number, ref in enumerate(held):
+        at = rows_of(number, rows)
+        for (frame, patch), in_ref in zip(order, in_refs):
+            if patch % 2:
+                continue
+            other = in_refs[order.index((frame, patch + 1))]
+            frame, patch = place((frame, patch), patch_count)
+            head = frame * patch_count + patch
+            odd = jnp.full((rows, LANES), head % 2, jnp.int32) == 1
+            here, there = in_ref[at], other[at]
+            first, second = interleave(jnp.where(odd, there, here), jnp.where(odd, here, there))
+            cols = head_columns(head)
+            ref[0, :, cols] = first
+            ref[1, :, cols] = second
+        copies.append(pltpu.make_async_copy(ref, out_refs[number], sems.at[number]))
+        copies[-1].start()
+    for copy in copies:
+        copy.wait()
 
 
 def visible_keys(frame):
@@ -284,20 +317,32 @@
 
 def head_kernel(order, parts, columns, *refs):
     in_refs, out_refs = refs[:H], refs[H : 2 * H]
-    held, done, qt, kt, vt, ct, tt, gt, gq, gk, gv, wts, bias = refs[2 * H :]
+    held, done, windows, lookbacks = refs[2 * H : 2 * H + 4]
+    qt, kt, vt, ct, tt, gt, gq, gk, gv, wts, bias, sem = refs[2 * H + 4 :]
     rows = done.shape[1] // 4
     frames, _, patches = wts.shape
     pairs = frames // 2
     scale = 1.0 / math.sqrt(SIZE)
 
-    for partner, ref in zip(order, in_refs):
-        held[place(partner, parts)] = ref[...]
+    own = place(order[0], parts)
+    own = pltpu.make_async_copy(in_refs[0], held.at[own[0] * parts + own[1]], sem)
+    own.start()
+    for partner, ref in zip(order[1:], in_refs[1:]):
+        frame, patch = place(partner, parts)
+        held[frame * parts + patch, : 4 * rows] = ref[: 4 * rows]
+        if partner[0] == 0:
+            windows[patch] = ref[4 * rows :]
+        if partner[1] == 0:
+            lookbacks[frame] = ref[4 * rows :]
+    own.wait()
+    frame, patch = place(order[0], parts)
+    windows[patch] = held[frame * parts + patch, 4 * rows :]
+    lookbacks[frame] = held[frame * parts + patch, 4 * rows :]
 
     def natural(number, pair):
         return held[rows_of(pair, parts), rows_of(number, rows)].reshape(patches, LANES)
 
-    info = [held[part, 4 * rows : 4 * rows + INFO] for part in range(parts)]
-    sides = [interleave(info[part], info[part + 1]) for part in range(0, parts, 2)]
+    sides = [interleave(windows[part], windows[part + 1]) for part in range(0, parts, 2)]
     first = jnp.concatenate([side[0] for side in sides], axis=1)
     last = jnp.concatenate([side[1] for side in sides], axis=1)
     key_block = (lax.broadcasted_iota(jnp.int32, (patches, patches), 0) // BLK).astype(jnp.float32)
@@ -315,8 +360,7 @@
         ct[at] = natural(3, pair).T
 
     for frame in range(frames):
-        tile = held[(frame // 2) * parts, 4 * rows : 4 * rows + INFO]
-        _, tile = interleave(tile, tile)
+        _, tile = interleave(lookbacks[frame // 2], lookbacks[frame // 2])
         at = INFO - 2 + frame % 2
         lookback = tile[at : at + 1]
         for chunk in range(patches // LANES):
@@ -411,7 +455,8 @@
                 parts, rows, LANES
             )
     for partner, ref in zip(order, out_refs):
-        ref[...] = done[place(partner, parts)]
+        frame, patch = place(partner, parts)
+        ref[...] = done[frame * parts + patch]
 
 
 def exchange(blocks, order, patch_count):
@@ -435,20 +480,22 @@
     vmem = pl.BlockSpec(memory_space=pltpu.VMEM)
     anywhere = pl.BlockSpec(memory_space=pl.ANY)
 
-    def blocks(rows):
-        return [jax.ShapeDtypeStruct((rows, LANES), jnp.float32)] * H
+    def blocks(info):
+        return [
+            jax.ShapeDtypeStruct((4 * patches_here + info, LANES), jnp.float32)
+            for _ in order
+        ]
 
     def params(mebibytes):
         return pltpu.CompilerParams(vmem_limit_bytes=mebibytes * 1024 * 1024)
 
     packed = pl.pallas_call(
         lambda *refs: pack_kernel(order, parts, *refs),
-        out_shape=blocks(4 * patches_here + INFO),
+        out_shape=blocks(INFO),
         in_specs=[anywhere] * 6,
         out_specs=[vmem] * H,
         scratch_shapes=[pltpu.VMEM(queries.shape, jnp.float32)] * 4
         + [
-            pltpu.VMEM((H, 4 * patches_here, LANES), jnp.float32),
             pltpu.SMEM(window.shape, jnp.int32),
             pltpu.SMEM(lookback.shape, jnp.int32),
             pltpu.SemaphoreType.DMA((6,)),
@@ -459,17 +506,20 @@
     across = pltpu.VMEM((frames * SIZE, patches), jnp.float32)
     done = pl.pallas_call(
         lambda *refs: head_kernel(order, parts, window.shape[1], *refs),
-        out_shape=blocks(4 * patches_here),
-        in_specs=[vmem] * H,
+        out_shape=blocks(0),
+        in_specs=[anywhere] + [vmem] * (H - 1),
         out_specs=[vmem] * H,
         scratch_shapes=[
             pltpu.VMEM((H, 4 * patches_here + INFO, LANES), jnp.float32),
             pltpu.VMEM((H, 4 * patches_here, LANES), jnp.float32),
+            pltpu.VMEM((parts, INFO, LANES), jnp.float32),
+            pltpu.VMEM((H // parts, INFO, LANES), jnp.float32),
         ]
         + [across] * 9
         + [
             pltpu.VMEM((frames, 8, patches), jnp.float32),
             pltpu.VMEM((patches, patches), jnp.float32),
+            pltpu.SemaphoreType.DMA,
         ],
         compiler_params=params(40),
         name="one_head",
@@ -478,8 +528,9 @@
         lambda *refs: unpack_kernel(order, parts, *refs),
         out_shape=[jax.ShapeDtypeStruct(queries.shape, jnp.float32)] * 4,
         in_specs=[vmem] * H,
-        out_specs=[vmem] * 4,
-        scratch_shapes=[pltpu.VMEM((H, 4 * patches_here, LANES), jnp.float32)],
+        out_specs=[anywhere] * 4,
+        scratch_shapes=[pltpu.VMEM(queries.shape, jnp.float32)] * 4
+        + [pltpu.SemaphoreType.DMA((4,))],
         compiler_params=params(40),
         name="unpack_heads",
     )(*exchange(done, order, parts))

time: 116 us -> 114 us (0.983); the launches traced: 116 us -> 113 us
  waiting for transfers between devices: 49.2 us -> 25.3 us
  starting transfers between devices: 54 us -> 74.9 us
    ppermute x30, waiting for transfers between devices: 49.2 us -> 25.3 us  [exchange(): lax.ppermute(block, ('frame', 'patch'), pairs)]
    ppermute x30, starting transfers between devices: 54 us -> 74.9 us  [exchange(): lax.ppermute(block, ('frame', 'patch'), pairs)]
  transfers between devices with their start and end apart: 30 -> 30, of which waited for: 10 -> 8; matrix products, arithmetic and copies ran while one was open for 0% -> 0% of each run, Pallas kernels for 0% -> 0%
where the time goes in v1:
time: 114 us; the launch traced here: 113 us
  starting transfers between devices  74.9 us (66%)
  waiting for transfers between devices  25.3 us (22%)
  Pallas kernels  11 us (10%)
    ppermute x30, starting transfers between devices, exchange(): lax.ppermute(block, ('frame', 'patch'), pairs)  74.9 us
    ppermute x30, waiting for transfers between devices, exchange(): lax.ppermute(block, ('frame', 'patch'), pairs)  25.3 us
    pallas_call x1, Pallas kernels, shards_by_head(): pl.pallas_call(lambda *refs: head_kernel(order, parts, window.shape[1], *...  5.95 us
    pallas_call x1, Pallas kernels, shards_by_head(): pl.pallas_call(lambda *refs: pack_kernel(order, parts, *refs), out_shape=...  3.15 us
  transfers between devices with their start and end apart: 30, of which 8 were waited for; matrix products, arithmetic and copies ran while one was open for 0% of the time, Pallas kernels for 0%

profile of v1, /device:TPU:0, one launch (start us, length us, event | category | flops | bytes accessed | tf_op | source)
XLA Modules:
  0.0 112.7 jit_solution(630573074493538828)
XLA Ops:
  0.6 3.2 %pack_heads.1 = (f32[264,128]{1,0:T(8,128)}, f32[264,128]{1,0:T(8,128)}, f32[264,128]{1,0:T(8,128)}, f32[264,128]{1,0:T(8,128)}, f32[264,128]{1,0:T(8,128)}, /*i...) custom-call(s32[4,12]{1,0:T(4,128)} %refs_0_.1, ...), custom_call_target="tpu_custom_call" | custom-call | tf_op jit(solution)/shard_map/pack_heads/pallas_call | solution.py:492
  3.8 4.1 %collective-permute-start = (f32[264,128]{1,0:T(8,128)}, f32[264,128]{1,0:T(8,128)S(1)}, u32[]{:S(2)}, u32[]{:S(2)}) collective-permute-start(f32[264,128]{1,0:T(8,128)} %get-tuple-element.37), channel_id=1, source_target_pairs={{0,2},{1,3},{2,0},{3,1},{4,6},{5,7},{6,4},{7,5},{8,10},{9,11},{10,... | collective-permute-start | bytes 405512 | tf_op jit(solution)/shard_map/ppermute | solution.py:470
  7.9 1.3 %collective-permute-start.1 = (f32[264,128]{1,0:T(8,128)}, f32[264,128]{1,0:T(8,128)S(1)}, u32[]{:S(2)}, u32[]{:S(2)}) collective-permute-start(f32[264,128]{1,0:T(8,128)} %get-tuple-element.38), channel_id=1, source_target_pairs={{0,3},{1,2},{2,1},{3,0},{4,7},{5,6},{6,5},{7,4},{8,11},{9,10},{10,... | collective-permute-start | bytes 405512 | tf_op jit(solution)/shard_map/ppermute | solution.py:470
  9.5 2.9 %collective-permute-start.4 = (f32[264,128]{1,0:T(8,128)}, f32[264,128]{1,0:T(8,128)S(1)}, u32[]{:S(2)}, u32[]{:S(2)}) collective-permute-start(f32[264,128]{1,0:T(8,128)} %get-tuple-element.41), channel_id=1, source_target_pairs={{0,6},{1,7},{2,4},{3,5},{4,2},{5,3},{6,0},{7,1},{8,14},{9,15},{10,... | collective-permute-start | bytes 405512 | tf_op jit(solution)/shard_map/ppermute | solution.py:470
  12.4 6.5 %collective-permute-done.refs_1_ = f32[264,128]{1,0:T(8,128)S(1)} collective-permute-done((f32[264,128]{1,0:T(8,128)}, f32[264,128]{1,0:T(8,128)S(1)}, u32[]{:S(2)}, u32[]{:S(2)}) %collective-permute-start) | collective-permute-done | bytes 135200 | tf_op jit(solution)/shard_map/ppermute | solution.py:470
  18.9 2.9 %collective-permute-start.6 = (f32[264,128]{1,0:T(8,128)}, f32[264,128]{1,0:T(8,128)S(1)}, u32[]{:S(2)}, u32[]{:S(2)}) collective-permute-start(f32[264,128]{1,0:T(8,128)} %get-tuple-element.43), channel_id=1, source_target_pairs={{0,7},{1,6},{2,5},{3,4},{4,3},{5,2},{6,1},{7,0},{8,15},{9,14},{10,... | collective-permute-start | bytes 405512 | tf_op jit(solution)/shard_map/ppermute | solution.py:470
  21.7 1.5 %collective-permute-start.7 = (f32[264,128]{1,0:T(8,128)}, f32[264,128]{1,0:T(8,128)S(1)}, u32[]{:S(2)}, u32[]{:S(2)}) collective-permute-start(f32[264,128]{1,0:T(8,128)} %get-tuple-element.44), channel_id=1, source_target_pairs={{0,8},{1,9},{2,10},{3,11},{4,12},{5,13},{6,14},{7,15},{8,0},{9,1},... | collective-permute-start | bytes 405512 | tf_op jit(solution)/shard_map/ppermute | solution.py:470
  23.3 4.3 %collective-permute-start.8 = (f32[264,128]{1,0:T(8,128)}, f32[264,128]{1,0:T(8,128)S(1)}, u32[]{:S(2)}, u32[]{:S(2)}) collective-permute-start(f32[264,128]{1,0:T(8,128)} %get-tuple-element.45), channel_id=1, source_target_pairs={{0,10},{1,11},{2,8},{3,9},{4,14},{5,15},{6,12},{7,13},{8,2},{9,3},... | collective-permute-start | bytes 405512 | tf_op jit(solution)/shard_map/ppermute | solution.py:470
  27.5 3.5 %collective-permute-start.9 = (f32[264,128]{1,0:T(8,128)}, f32[264,128]{1,0:T(8,128)S(1)}, u32[]{:S(2)}, u32[]{:S(2)}) collective-permute-start(f32[264,128]{1,0:T(8,128)} %get-tuple-element.46), channel_id=1, source_target_pairs={{0,9},{1,8},{2,11},{3,10},{4,13},{5,12},{6,15},{7,14},{8,1},{9,0},... | collective-permute-start | bytes 405512 | tf_op jit(solution)/shard_map/ppermute | solution.py:470
  31.0 5.0 %collective-permute-start.10 = (f32[264,128]{1,0:T(8,128)}, f32[264,128]{1,0:T(8,128)S(1)}, u32[]{:S(2)}, u32[]{:S(2)}) collective-permute-start(f32[264,128]{1,0:T(8,128)} %get-tuple-element.47), channel_id=1, source_target_pairs={{0,11},{1,10},{2,9},{3,8},{4,15},{5,14},{6,13},{7,12},{8,3},{9,2},... | collective-permute-start | bytes 405512 | tf_op jit(solution)/shard_map/ppermute | solution.py:470
  36.4 2.3 %collective-permute-start.12 = (f32[264,128]{1,0:T(8,128)}, f32[264,128]{1,0:T(8,128)S(1)}, u32[]{:S(2)}, u32[]{:S(2)}) collective-permute-start(f32[264,128]{1,0:T(8,128)} %get-tuple-element.49), channel_id=1, source_target_pairs={{0,14},{1,15},{2,12},{3,13},{4,10},{5,11},{6,8},{7,9},{8,6},{9,7},... | collective-permute-start | bytes 405512 | tf_op jit(solution)/shard_map/ppermute | solution.py:470
  38.9 6.1 %collective-permute-start.13 = (f32[264,128]{1,0:T(8,128)}, f32[264,128]{1,0:T(8,128)S(1)}, u32[]{:S(2)}, u32[]{:S(2)}) collective-permute-start(f32[264,128]{1,0:T(8,128)} %get-tuple-element.50), channel_id=1, source_target_pairs={{0,13},{1,12},{2,15},{3,14},{4,9},{5,8},{6,11},{7,10},{8,5},{9,4},... | collective-permute-start | bytes 405512 | tf_op jit(solution)/shard_map/ppermute | solution.py:470
  45.0 2.8 %collective-permute-start.14 = (f32[264,128]{1,0:T(8,128)}, f32[264,128]{1,0:T(8,128)S(1)}, u32[]{:S(2)}, u32[]{:S(2)}) collective-permute-start(f32[264,128]{1,0:T(8,128)} %get-tuple-element.51), channel_id=1, source_target_pairs={{0,15},{1,14},{2,13},{3,12},{4,11},{5,10},{6,9},{7,8},{8,7},{9,6},... | collective-permute-start | bytes 405512 | tf_op jit(solution)/shard_map/ppermute | solution.py:470
  47.8 2.8 %collective-permute-done.12.refs_13_ = f32[264,128]{1,0:T(8,128)S(1)} collective-permute-done((f32[264,128]{1,0:T(8,128)}, f32[264,128]{1,0:T(8,128)S(1)}, u32[]{:S(2)}, u32[]{:S(2)}) %collective-permute-start.12) | collective-permute-done | bytes 135200 | tf_op jit(solution)/shard_map/ppermute | solution.py:470
  50.6 0.9 collective-permute-done.13.refs_14_
  51.4 3.3 %collective-permute-done.14.refs_15_ = f32[264,128]{1,0:T(8,128)S(1)} collective-permute-done((f32[264,128]{1,0:T(8,128)}, f32[264,128]{1,0:T(8,128)S(1)}, u32[]{:S(2)}, u32[]{:S(2)}) %collective-permute-start.14) | collective-permute-done | bytes 135200 | tf_op jit(solution)/shard_map/ppermute | solution.py:470
  54.8 0.9 copy-done
  55.7 6.0 %one_head.1 = (f32[256,128]{1,0:T(8,128)S(1)}, f32[256,128]{1,0:T(8,128)S(1)}, f32[256,128]{1,0:T(8,128)S(1)}, f32[256,128]{1,0:T(8,128)S(1)}, f32[256,128]{1,0:...) custom-call(f32[264,128]{1,0:T(8,128)S(1)} %copy-done, ...), custom_call_target="tpu_custom_call" | custom-call | tf_op jit(solution)/shard_map/one_head/pallas_call | solution.py:507
  61.6 4.0 %collective-permute-start.15 = (f32[256,128]{1,0:T(8,128)S(1)}, f32[256,128]{1,0:T(8,128)S(1)}, u32[]{:S(2)}, u32[]{:S(2)}) collective-permute-start(f32[256,128]{1,0:T(8,128)S(1)} %get-tuple-element.53), channel_id=1, source_target_pairs={{0,2},{1,3},{2,0},{3,1},{4,6},{5,7},{6,4},{7,5},{8,10},{9,11},{10,... | collective-permute-start | bytes 393224 | tf_op jit(solution)/shard_map/ppermute | solution.py:470
  65.7 1.1 %collective-permute-start.16 = (f32[256,128]{1,0:T(8,128)S(1)}, f32[256,128]{1,0:T(8,128)S(1)}, u32[]{:S(2)}, u32[]{:S(2)}) collective-permute-start(f32[256,128]{1,0:T(8,128)S(1)} %get-tuple-element.54), channel_id=1, source_target_pairs={{0,3},{1,2},{2,1},{3,0},{4,7},{5,6},{6,5},{7,4},{8,11},{9,10},{10,... | collective-permute-start | bytes 393224 | tf_op jit(solution)/shard_map/ppermute | solution.py:470
  67.3 2.9 %collective-permute-start.19 = (f32[256,128]{1,0:T(8,128)S(1)}, f32[256,128]{1,0:T(8,128)S(1)}, u32[]{:S(2)}, u32[]{:S(2)}) collective-permute-start(f32[256,128]{1,0:T(8,128)S(1)} %get-tuple-element.57), channel_id=1, source_target_pairs={{0,6},{1,7},{2,4},{3,5},{4,2},{5,3},{6,0},{7,1},{8,14},{9,15},{10,... | collective-permute-start | bytes 393224 | tf_op jit(solution)/shard_map/ppermute | solution.py:470
  70.2 5.4 %collective-permute-done.15.refs_1_ = f32[256,128]{1,0:T(8,128)S(1)} collective-permute-done((f32[256,128]{1,0:T(8,128)S(1)}, f32[256,128]{1,0:T(8,128)S(1)}, u32[]{:S(2)}, u32[]{:S(2)}) %collective-permute-start.15) | collective-permute-done | bytes 131104 | tf_op jit(solution)/shard_map/ppermute | solution.py:470
  75.7 3.3 %collective-permute-start.21 = (f32[256,128]{1,0:T(8,128)S(1)}, f32[256,128]{1,0:T(8,128)S(1)}, u32[]{:S(2)}, u32[]{:S(2)}) collective-permute-start(f32[256,128]{1,0:T(8,128)S(1)} %get-tuple-element.59), channel_id=1, source_target_pairs={{0,7},{1,6},{2,5},{3,4},{4,3},{5,2},{6,1},{7,0},{8,15},{9,14},{10,... | collective-permute-start | bytes 393224 | tf_op jit(solution)/shard_map/ppermute | solution.py:470
  79.2 5.8 %collective-permute-start.23 = (f32[256,128]{1,0:T(8,128)S(1)}, f32[256,128]{1,0:T(8,128)S(1)}, u32[]{:S(2)}, u32[]{:S(2)}) collective-permute-start(f32[256,128]{1,0:T(8,128)S(1)} %get-tuple-element.61), channel_id=1, source_target_pairs={{0,10},{1,11},{2,8},{3,9},{4,14},{5,15},{6,12},{7,13},{8,2},{9,3},... | collective-permute-start | bytes 393224 | tf_op jit(solution)/shard_map/ppermute | solution.py:470
  84.9 5.2 %collective-permute-start.24 = (f32[256,128]{1,0:T(8,128)S(1)}, f32[256,128]{1,0:T(8,128)S(1)}, u32[]{:S(2)}, u32[]{:S(2)}) collective-permute-start(f32[256,128]{1,0:T(8,128)S(1)} %get-tuple-element.62), channel_id=1, source_target_pairs={{0,9},{1,8},{2,11},{3,10},{4,13},{5,12},{6,15},{7,14},{8,1},{9,0},... | collective-permute-start | bytes 393224 | tf_op jit(solution)/shard_map/ppermute | solution.py:470
  90.1 2.4 %collective-permute-start.25 = (f32[256,128]{1,0:T(8,128)S(1)}, f32[256,128]{1,0:T(8,128)S(1)}, u32[]{:S(2)}, u32[]{:S(2)}) collective-permute-start(f32[256,128]{1,0:T(8,128)S(1)} %get-tuple-element.63), channel_id=1, source_target_pairs={{0,11},{1,10},{2,9},{3,8},{4,15},{5,14},{6,13},{7,12},{8,3},{9,2},... | collective-permute-start | bytes 393224 | tf_op jit(solution)/shard_map/ppermute | solution.py:470
  92.6 1.0 collective-permute-start.26
  93.6 2.2 %collective-permute-start.27 = (f32[256,128]{1,0:T(8,128)S(1)}, f32[256,128]{1,0:T(8,128)S(1)}, u32[]{:S(2)}, u32[]{:S(2)}) collective-permute-start(f32[256,128]{1,0:T(8,128)S(1)} %get-tuple-element.65), channel_id=1, source_target_pairs={{0,14},{1,15},{2,12},{3,13},{4,10},{5,11},{6,8},{7,9},{8,6},{9,7},... | collective-permute-start | bytes 393224 | tf_op jit(solution)/shard_map/ppermute | solution.py:470
  96.0 8.7 %collective-permute-start.29 = (f32[256,128]{1,0:T(8,128)S(1)}, f32[256,128]{1,0:T(8,128)S(1)}, u32[]{:S(2)}, u32[]{:S(2)}) collective-permute-start(f32[256,128]{1,0:T(8,128)S(1)} %get-tuple-element.67), channel_id=1, source_target_pairs={{0,15},{1,14},{2,13},{3,12},{4,11},{5,10},{6,9},{7,8},{8,7},{9,6},... | collective-permute-start | bytes 393224 | tf_op jit(solution)/shard_map/ppermute | solution.py:470
  104.6 1.4 %collective-permute-done.27.refs_13_ = f32[256,128]{1,0:T(8,128)S(1)} collective-permute-done((f32[256,128]{1,0:T(8,128)S(1)}, f32[256,128]{1,0:T(8,128)S(1)}, u32[]{:S(2)}, u32[]{:S(2)}) %collective-permute-start.27) | collective-permute-done | bytes 131104 | tf_op jit(solution)/shard_map/ppermute | solution.py:470
  106.0 4.9 %collective-permute-done.29.refs_15_ = f32[256,128]{1,0:T(8,128)S(1)} collective-permute-done((f32[256,128]{1,0:T(8,128)S(1)}, f32[256,128]{1,0:T(8,128)S(1)}, u32[]{:S(2)}, u32[]{:S(2)}) %collective-permute-start.29) | collective-permute-done | bytes 131104 | tf_op jit(solution)/shard_map/ppermute | solution.py:470
  110.9 1.9 %unpack_heads.1 = (f32[2,64,1024]{2,1,0:T(8,128)}, f32[2,64,1024]{2,1,0:T(8,128)}, f32[2,64,1024]{2,1,0:T(8,128)}, f32[2,64,1024]{2,1,0:T(8,128)}) custom-call(f32[256,128]{1,0:T(8,128)S(1)} %get-tuple-element.52.refs_0_, f32[256,128]{1,0:T(8,128)S(1)} %collective-permute-done.15.refs_1_, f32[256,128]{1,0:T(8,128)S(1)} %collective-permute-done.16.refs_2_, ...), custom_call_target="tpu_custom_call" | custom-call | tf_op jit(solution)/shard_map/unpack_heads/pallas_call | solution.py:527
  (33 shorter events, 1.8 us)
Async XLA Ops:
  3.8 15.1 %collective-permute-start = (f32[264,128]{1,0:T(8,128)}, f32[264,128]{1,0:T(8,128)S(1)}, u32[]{:S(2)}, u32[]{:S(2)}) collective-permute-start(f32[264,128]{1,0:T(8,128)} %get-tuple-element.37), channel_id=1, source_target_pairs={{0,2},{1,3},{2,0},{3,1},{4,6},{5,7},{6,4},{7,5},{8,10},{9,11},{10,... | collective-permute-start | bytes 405512 | tf_op jit(solution)/shard_map/ppermute | solution.py:470
  7.9 11.0 %collective-permute-start.1 = (f32[264,128]{1,0:T(8,128)}, f32[264,128]{1,0:T(8,128)S(1)}, u32[]{:S(2)}, u32[]{:S(2)}) collective-permute-start(f32[264,128]{1,0:T(8,128)} %get-tuple-element.38), channel_id=1, source_target_pairs={{0,3},{1,2},{2,1},{3,0},{4,7},{5,6},{6,5},{7,4},{8,11},{9,10},{10,... | collective-permute-start | bytes 405512 | tf_op jit(solution)/shard_map/ppermute | solution.py:470
  9.2 12.5 %collective-permute-start.2 = (f32[264,128]{1,0:T(8,128)}, f32[264,128]{1,0:T(8,128)S(1)}, u32[]{:S(2)}, u32[]{:S(2)}) collective-permute-start(f32[264,128]{1,0:T(8,128)} %get-tuple-element.39), channel_id=1, source_target_pairs={{0,1},{1,0},{2,3},{3,2},{4,5},{5,4},{6,7},{7,6},{8,9},{9,8},{10,11... | collective-permute-start | bytes 405512 | tf_op jit(solution)/shard_map/ppermute | solution.py:470
  9.5 13.8 %collective-permute-start.3 = (f32[264,128]{1,0:T(8,128)}, f32[264,128]{1,0:T(8,128)S(1)}, u32[]{:S(2)}, u32[]{:S(2)}) collective-permute-start(f32[264,128]{1,0:T(8,128)} %get-tuple-element.40), channel_id=1, source_target_pairs={{0,4},{1,5},{2,6},{3,7},{4,0},{5,1},{6,2},{7,3},{8,12},{9,13},{10,... | collective-permute-start | bytes 405512 | tf_op jit(solution)/shard_map/ppermute | solution.py:470
  9.5 18.1 %collective-permute-start.4 = (f32[264,128]{1,0:T(8,128)}, f32[264,128]{1,0:T(8,128)S(1)}, u32[]{:S(2)}, u32[]{:S(2)}) collective-permute-start(f32[264,128]{1,0:T(8,128)} %get-tuple-element.41), channel_id=1, source_target_pairs={{0,6},{1,7},{2,4},{3,5},{4,2},{5,3},{6,0},{7,1},{8,14},{9,15},{10,... | collective-permute-start | bytes 405512 | tf_op jit(solution)/shard_map/ppermute | solution.py:470
  18.9 12.1 %collective-permute-start.5 = (f32[264,128]{1,0:T(8,128)}, f32[264,128]{1,0:T(8,128)S(1)}, u32[]{:S(2)}, u32[]{:S(2)}) collective-permute-start(f32[264,128]{1,0:T(8,128)} %get-tuple-element.42), channel_id=1, source_target_pairs={{0,5},{1,4},{2,7},{3,6},{4,1},{5,0},{6,3},{7,2},{8,13},{9,12},{10,... | collective-permute-start | bytes 405512 | tf_op jit(solution)/shard_map/ppermute | solution.py:470
  18.9 17.1 %collective-permute-start.6 = (f32[264,128]{1,0:T(8,128)}, f32[264,128]{1,0:T(8,128)S(1)}, u32[]{:S(2)}, u32[]{:S(2)}) collective-permute-start(f32[264,128]{1,0:T(8,128)} %get-tuple-element.43), channel_id=1, source_target_pairs={{0,7},{1,6},{2,5},{3,4},{4,3},{5,2},{6,1},{7,0},{8,15},{9,14},{10,... | collective-permute-start | bytes 405512 | tf_op jit(solution)/shard_map/ppermute | solution.py:470
  21.7 14.7 %collective-permute-start.7 = (f32[264,128]{1,0:T(8,128)}, f32[264,128]{1,0:T(8,128)S(1)}, u32[]{:S(2)}, u32[]{:S(2)}) collective-permute-start(f32[264,128]{1,0:T(8,128)} %get-tuple-element.44), channel_id=1, source_target_pairs={{0,8},{1,9},{2,10},{3,11},{4,12},{5,13},{6,14},{7,15},{8,0},{9,1},... | collective-permute-start | bytes 405512 | tf_op jit(solution)/shard_map/ppermute | solution.py:470
  23.3 15.6 %collective-permute-start.8 = (f32[264,128]{1,0:T(8,128)}, f32[264,128]{1,0:T(8,128)S(1)}, u32[]{:S(2)}, u32[]{:S(2)}) collective-permute-start(f32[264,128]{1,0:T(8,128)} %get-tuple-element.45), channel_id=1, source_target_pairs={{0,10},{1,11},{2,8},{3,9},{4,14},{5,15},{6,12},{7,13},{8,2},{9,3},... | collective-permute-start | bytes 405512 | tf_op jit(solution)/shard_map/ppermute | solution.py:470
  27.5 17.5 %collective-permute-start.9 = (f32[264,128]{1,0:T(8,128)}, f32[264,128]{1,0:T(8,128)S(1)}, u32[]{:S(2)}, u32[]{:S(2)}) collective-permute-start(f32[264,128]{1,0:T(8,128)} %get-tuple-element.46), channel_id=1, source_target_pairs={{0,9},{1,8},{2,11},{3,10},{4,13},{5,12},{6,15},{7,14},{8,1},{9,0},... | collective-permute-start | bytes 405512 | tf_op jit(solution)/shard_map/ppermute | solution.py:470
  31.0 16.8 %collective-permute-start.10 = (f32[264,128]{1,0:T(8,128)}, f32[264,128]{1,0:T(8,128)S(1)}, u32[]{:S(2)}, u32[]{:S(2)}) collective-permute-start(f32[264,128]{1,0:T(8,128)} %get-tuple-element.47), channel_id=1, source_target_pairs={{0,11},{1,10},{2,9},{3,8},{4,15},{5,14},{6,13},{7,12},{8,3},{9,2},... | collective-permute-start | bytes 405512 | tf_op jit(solution)/shard_map/ppermute | solution.py:470
  36.0 11.8 %collective-permute-start.11 = (f32[264,128]{1,0:T(8,128)}, f32[264,128]{1,0:T(8,128)S(1)}, u32[]{:S(2)}, u32[]{:S(2)}) collective-permute-start(f32[264,128]{1,0:T(8,128)} %get-tuple-element.48), channel_id=1, source_target_pairs={{0,12},{1,13},{2,14},{3,15},{4,8},{5,9},{6,10},{7,11},{8,4},{9,5},... | collective-permute-start | bytes 405512 | tf_op jit(solution)/shard_map/ppermute | solution.py:470
  36.4 14.1 %collective-permute-start.12 = (f32[264,128]{1,0:T(8,128)}, f32[264,128]{1,0:T(8,128)S(1)}, u32[]{:S(2)}, u32[]{:S(2)}) collective-permute-start(f32[264,128]{1,0:T(8,128)} %get-tuple-element.49), channel_id=1, source_target_pairs={{0,14},{1,15},{2,12},{3,13},{4,10},{5,11},{6,8},{7,9},{8,6},{9,7},... | collective-permute-start | bytes 405512 | tf_op jit(solution)/shard_map/ppermute | solution.py:470
  38.9 12.5 %collective-permute-start.13 = (f32[264,128]{1,0:T(8,128)}, f32[264,128]{1,0:T(8,128)S(1)}, u32[]{:S(2)}, u32[]{:S(2)}) collective-permute-start(f32[264,128]{1,0:T(8,128)} %get-tuple-element.50), channel_id=1, source_target_pairs={{0,13},{1,12},{2,15},{3,14},{4,9},{5,8},{6,11},{7,10},{8,5},{9,4},... | collective-permute-start | bytes 405512 | tf_op jit(solution)/shard_map/ppermute | solution.py:470
  45.0 9.8 %collective-permute-start.14 = (f32[264,128]{1,0:T(8,128)}, f32[264,128]{1,0:T(8,128)S(1)}, u32[]{:S(2)}, u32[]{:S(2)}) collective-permute-start(f32[264,128]{1,0:T(8,128)} %get-tuple-element.51), channel_id=1, source_target_pairs={{0,15},{1,14},{2,13},{3,12},{4,11},{5,10},{6,9},{7,8},{8,7},{9,6},... | collective-permute-start | bytes 405512 | tf_op jit(solution)/shard_map/ppermute | solution.py:470
  54.8 0.9 copy-start
  61.6 14.0 %collective-permute-start.15 = (f32[256,128]{1,0:T(8,128)S(1)}, f32[256,128]{1,0:T(8,128)S(1)}, u32[]{:S(2)}, u32[]{:S(2)}) collective-permute-start(f32[256,128]{1,0:T(8,128)S(1)} %get-tuple-element.53), channel_id=1, source_target_pairs={{0,2},{1,3},{2,0},{3,1},{4,6},{5,7},{6,4},{7,5},{8,10},{9,11},{10,... | collective-permute-start | bytes 393224 | tf_op jit(solution)/shard_map/ppermute | solution.py:470
  65.7 10.1 %collective-permute-start.16 = (f32[256,128]{1,0:T(8,128)S(1)}, f32[256,128]{1,0:T(8,128)S(1)}, u32[]{:S(2)}, u32[]{:S(2)}) collective-permute-start(f32[256,128]{1,0:T(8,128)S(1)} %get-tuple-element.54), channel_id=1, source_target_pairs={{0,3},{1,2},{2,1},{3,0},{4,7},{5,6},{6,5},{7,4},{8,11},{9,10},{10,... | collective-permute-start | bytes 393224 | tf_op jit(solution)/shard_map/ppermute | solution.py:470
  66.8 12.2 %collective-permute-start.17 = (f32[256,128]{1,0:T(8,128)S(1)}, f32[256,128]{1,0:T(8,128)S(1)}, u32[]{:S(2)}, u32[]{:S(2)}) collective-permute-start(f32[256,128]{1,0:T(8,128)S(1)} %get-tuple-element.55), channel_id=1, source_target_pairs={{0,1},{1,0},{2,3},{3,2},{4,5},{5,4},{6,7},{7,6},{8,9},{9,8},{10,11... | collective-permute-start | bytes 393224 | tf_op jit(solution)/shard_map/ppermute | solution.py:470
  67.3 11.9 %collective-permute-start.18 = (f32[256,128]{1,0:T(8,128)S(1)}, f32[256,128]{1,0:T(8,128)S(1)}, u32[]{:S(2)}, u32[]{:S(2)}) collective-permute-start(f32[256,128]{1,0:T(8,128)S(1)} %get-tuple-element.56), channel_id=1, source_target_pairs={{0,4},{1,5},{2,6},{3,7},{4,0},{5,1},{6,2},{7,3},{8,12},{9,13},{10,... | collective-permute-start | bytes 393224 | tf_op jit(solution)/shard_map/ppermute | solution.py:470
  67.3 17.6 %collective-permute-start.19 = (f32[256,128]{1,0:T(8,128)S(1)}, f32[256,128]{1,0:T(8,128)S(1)}, u32[]{:S(2)}, u32[]{:S(2)}) collective-permute-start(f32[256,128]{1,0:T(8,128)S(1)} %get-tuple-element.57), channel_id=1, source_target_pairs={{0,6},{1,7},{2,4},{3,5},{4,2},{5,3},{6,0},{7,1},{8,14},{9,15},{10,... | collective-permute-start | bytes 393224 | tf_op jit(solution)/shard_map/ppermute | solution.py:470
  75.6 14.5 %collective-permute-start.20 = (f32[256,128]{1,0:T(8,128)S(1)}, f32[256,128]{1,0:T(8,128)S(1)}, u32[]{:S(2)}, u32[]{:S(2)}) collective-permute-start(f32[256,128]{1,0:T(8,128)S(1)} %get-tuple-element.58), channel_id=1, source_target_pairs={{0,5},{1,4},{2,7},{3,6},{4,1},{5,0},{6,3},{7,2},{8,13},{9,12},{10,... | collective-permute-start | bytes 393224 | tf_op jit(solution)/shard_map/ppermute | solution.py:470
  75.7 16.8 %collective-permute-start.21 = (f32[256,128]{1,0:T(8,128)S(1)}, f32[256,128]{1,0:T(8,128)S(1)}, u32[]{:S(2)}, u32[]{:S(2)}) collective-permute-start(f32[256,128]{1,0:T(8,128)S(1)} %get-tuple-element.59), channel_id=1, source_target_pairs={{0,7},{1,6},{2,5},{3,4},{4,3},{5,2},{6,1},{7,0},{8,15},{9,14},{10,... | collective-permute-start | bytes 393224 | tf_op jit(solution)/shard_map/ppermute | solution.py:470
  79.1 14.5 %collective-permute-start.22 = (f32[256,128]{1,0:T(8,128)S(1)}, f32[256,128]{1,0:T(8,128)S(1)}, u32[]{:S(2)}, u32[]{:S(2)}) collective-permute-start(f32[256,128]{1,0:T(8,128)S(1)} %get-tuple-element.60), channel_id=1, source_target_pairs={{0,8},{1,9},{2,10},{3,11},{4,12},{5,13},{6,14},{7,15},{8,0},{9,1},... | collective-permute-start | bytes 393224 | tf_op jit(solution)/shard_map/ppermute | solution.py:470
  79.2 16.6 %collective-permute-start.23 = (f32[256,128]{1,0:T(8,128)S(1)}, f32[256,128]{1,0:T(8,128)S(1)}, u32[]{:S(2)}, u32[]{:S(2)}) collective-permute-start(f32[256,128]{1,0:T(8,128)S(1)} %get-tuple-element.61), channel_id=1, source_target_pairs={{0,10},{1,11},{2,8},{3,9},{4,14},{5,15},{6,12},{7,13},{8,2},{9,3},... | collective-permute-start | bytes 393224 | tf_op jit(solution)/shard_map/ppermute | solution.py:470
  84.9 11.0 %collective-permute-start.24 = (f32[256,128]{1,0:T(8,128)S(1)}, f32[256,128]{1,0:T(8,128)S(1)}, u32[]{:S(2)}, u32[]{:S(2)}) collective-permute-start(f32[256,128]{1,0:T(8,128)S(1)} %get-tuple-element.62), channel_id=1, source_target_pairs={{0,9},{1,8},{2,11},{3,10},{4,13},{5,12},{6,15},{7,14},{8,1},{9,0},... | collective-permute-start | bytes 393224 | tf_op jit(solution)/shard_map/ppermute | solution.py:470
  90.1 14.5 %collective-permute-start.25 = (f32[256,128]{1,0:T(8,128)S(1)}, f32[256,128]{1,0:T(8,128)S(1)}, u32[]{:S(2)}, u32[]{:S(2)}) collective-permute-start(f32[256,128]{1,0:T(8,128)S(1)} %get-tuple-element.63), channel_id=1, source_target_pairs={{0,11},{1,10},{2,9},{3,8},{4,15},{5,14},{6,13},{7,12},{8,3},{9,2},... | collective-permute-start | bytes 393224 | tf_op jit(solution)/shard_map/ppermute | solution.py:470
  92.6 12.0 %collective-permute-start.26 = (f32[256,128]{1,0:T(8,128)S(1)}, f32[256,128]{1,0:T(8,128)S(1)}, u32[]{:S(2)}, u32[]{:S(2)}) collective-permute-start(f32[256,128]{1,0:T(8,128)S(1)} %get-tuple-element.64), channel_id=1, source_target_pairs={{0,12},{1,13},{2,14},{3,15},{4,8},{5,9},{6,10},{7,11},{8,4},{9,5},... | collective-permute-start | bytes 393224 | tf_op jit(solution)/shard_map/ppermute | solution.py:470
  93.6 12.4 %collective-permute-start.27 = (f32[256,128]{1,0:T(8,128)S(1)}, f32[256,128]{1,0:T(8,128)S(1)}, u32[]{:S(2)}, u32[]{:S(2)}) collective-permute-start(f32[256,128]{1,0:T(8,128)S(1)} %get-tuple-element.65), channel_id=1, source_target_pairs={{0,14},{1,15},{2,12},{3,13},{4,10},{5,11},{6,8},{7,9},{8,6},{9,7},... | collective-permute-start | bytes 393224 | tf_op jit(solution)/shard_map/ppermute | solution.py:470
  95.8 10.2 %collective-permute-start.28 = (f32[256,128]{1,0:T(8,128)S(1)}, f32[256,128]{1,0:T(8,128)S(1)}, u32[]{:S(2)}, u32[]{:S(2)}) collective-permute-start(f32[256,128]{1,0:T(8,128)S(1)} %get-tuple-element.66), channel_id=1, source_target_pairs={{0,13},{1,12},{2,15},{3,14},{4,9},{5,8},{6,11},{7,10},{8,5},{9,4},... | collective-permute-start | bytes 393224 | tf_op jit(solution)/shard_map/ppermute | solution.py:470
  96.0 14.9 %collective-permute-start.29 = (f32[256,128]{1,0:T(8,128)S(1)}, f32[256,128]{1,0:T(8,128)S(1)}, u32[]{:S(2)}, u32[]{:S(2)}) collective-permute-start(f32[256,128]{1,0:T(8,128)S(1)} %get-tuple-element.67), channel_id=1, source_target_pairs={{0,15},{1,14},{2,13},{3,12},{4,11},{5,10},{6,9},{7,8},{8,7},{9,6},... | collective-permute-start | bytes 393224 | tf_op jit(solution)/shard_map/ppermute | solution.py:470

commit v2 on v0

--- a/solution.py
+++ b/solution.py
@@ -184,6 +184,14 @@
 LANES = 128
 SIZE = LANES // 2
 INFO = 8
+OUTWARD = (
+    (0, 0), (3, 3), (0, 1), (1, 0), (1, 2), (1, 1), (1, 3), (2, 2),
+    (2, 1), (2, 3), (3, 0), (3, 2), (3, 1), (0, 2), (2, 0), (0, 3),
+)
+HOMEWARD = (
+    (0, 0), (3, 3), (0, 1), (1, 0), (1, 2), (1, 1), (1, 3), (2, 2),
+    (2, 1), (2, 3), (3, 0), (3, 2), (3, 1), (0, 2), (2, 0), (0, 3),
+)
 NN = ((1,), (0,))
 NT = ((1,), (1,))
 
@@ -217,61 +225,88 @@
     return out[:SIZE] + (out[SIZE:] + dot(both[:SIZE], low, dims))
 
 
-def partners(frame_count, patch_count):
-    return [(frame, patch) for frame in range(frame_count) for patch in range(patch_count)]
-
-
 def place(partner, patch_count):
     frame = lax.bitwise_xor(lax.axis_index("frame"), partner[0])
     return frame * patch_count + lax.bitwise_xor(lax.axis_index("patch"), partner[1])
 
 
-def pack_kernel(order, patch_count, window, lookback, *refs):
-    arrays, out_refs = refs[:4], refs[4 : 4 + H]
-    held, (packed, window_ref, lookback_ref, sems) = refs[4 + H : 8 + H], refs[8 + H :]
-    moves = list(zip((*arrays, window, lookback), (*held, window_ref, lookback_ref)))
-    copies = [pltpu.make_async_copy(a, b, sems.at[n]) for n, (a, b) in enumerate(moves)]
-    for copy in copies:
-        copy.start()
-    rows = held[0].shape[1]
-    for number, (copy, ref) in enumerate(zip(copies, held)):
-        copy.wait()
-        for pair in range(H // 2):
-            cols = rows_of(pair, LANES)
-            packed[2 * pair, rows_of(number, rows)], packed[2 * pair + 1, rows_of(number, rows)] = (
-                interleave(ref[0, :, cols], ref[1, :, cols])
-            )
-    copies[4].wait()
-    copies[5].wait()
+def columns_of(head):
+    return pl.ds(pl.multiple_of(head // 2 * LANES, LANES), LANES)
+
+
+def low_lanes(rows):
+    return lax.broadcasted_iota(jnp.int32, (rows, LANES), 1) < SIZE
+
+
+def side_by_side(ref, head, cols):
+    odd = head % 2
+    kept, moved = ref[odd, :, cols], ref[1 - odd, :, cols]
+    low = low_lanes(kept.shape[0]).astype(jnp.int32)
+    return jnp.where(low != odd, kept, pltpu.roll(moved, SIZE, 1))
+
+
+def whole_numbers(window, lookback, rows):
     row = lax.broadcasted_iota(jnp.int32, (INFO, LANES), 0)
     lane = lax.broadcasted_iota(jnp.int32, (INFO, LANES), 1)
     info = jnp.zeros((INFO, LANES), jnp.int32)
     for block in range(rows // BLK):
-        for column in range(window_ref.shape[1]):
+        for column in range(window.shape[1]):
             at = block * BLK + (column // INFO) * SIZE
             here = (row == column % INFO) & (lane >= at) & (lane < at + BLK)
-            info = jnp.where(here, window_ref[block, column], info)
+            info = jnp.where(here, window[block, column], info)
     for frame in range(2):
         here = (row == INFO - 2 + frame) & (lane >= SIZE)
-        info = jnp.where(here, lookback_ref[frame], info)
-    info = info.astype(jnp.float32)
-    for partner, ref in zip(order, out_refs):
-        ref[: 4 * rows] = packed[place(partner, patch_count)]
+        info = jnp.where(here, lookback[frame], info)
+    return info.astype(jnp.float32)
+
+
+def fetch(moves, sems):
+    copies = [pltpu.make_async_copy(a, b, sems.at[n]) for n, (a, b) in enumerate(moves)]
+    for copy in copies:
+        copy.start()
+    return copies
+
+
+def pack_kernel(order, parts, window, lookback, *refs):
+    arrays, out_refs = refs[:4], refs[4 : 3 + H]
+    held, window_ref, lookback_ref, sems = refs[3 + H : 7 + H], *refs[7 + H :]
+    moves = [(window, window_ref), (lookback, lookback_ref)]
+    moves += [(a.at[frame], b.at[frame]) for a, b in zip(arrays, held) for frame in range(2)]
+    copies = fetch(moves, sems)
+    copies[0].wait()
+    copies[1].wait()
+    rows = held[0].shape[1]
+    info = whole_numbers(window_ref, lookback_ref, rows)
+    for ref in out_refs:
         ref[4 * rows :] = info
-
-
-def unpack_kernel(order, patch_count, *refs):
-    in_refs, out_refs, packed = refs[:H], refs[H:-1], refs[-1]
-    rows = out_refs[0].shape[1]
-    for partner, ref in zip(order, in_refs):
-        packed[place(partner, patch_count)] = ref[...]
-    for pair in range(H // 2):
-        cols = rows_of(pair, LANES)
-        for number, ref in enumerate(out_refs):
-            at = rows_of(number, rows)
-            ref[0, :, cols], ref[1, :, cols] = interleave(
-                packed[2 * pair, at], packed[2 * pair + 1, at]
-            )
+    for number, ref in enumerate(held):
+        copies[2 + 2 * number].wait()
+        copies[3 + 2 * number].wait()
+        for partner, out_ref in zip(order, out_refs):
+            head = place(partner, parts)
+            out_ref[rows_of(number, rows)] = side_by_side(ref, head, columns_of(head))
+
+
+def unpack_kernel(order, groups, parts, *refs):
+    in_refs, out_refs, held, sems = refs[:H], refs[H : H + 4], refs[H + 4 : H + 8], refs[H + 8]
+    rows = held[0].shape[1]
+    copies = []
+    for number, ref in enumerate(held):
+        at = rows_of(number, rows)
+        for frame in range(groups):
+            for patch in range(0, parts, 2):
+                head = place((frame, patch), parts)
+                odd = jnp.full((rows, LANES), head % 2, jnp.int32) == 1
+                here = in_refs[order.index((frame, patch))][at]
+                there = in_refs[order.index((frame, patch + 1))][at]
+                first, second = interleave(jnp.where(odd, there, here), jnp.where(odd, here, there))
+                cols = columns_of(head)
+                ref[0, :, cols] = first
+                ref[1, :, cols] = second
+        copies.append(pltpu.make_async_copy(ref, out_refs[number], sems.at[number]))
+        copies[-1].start()
+    for copy in copies:
+        copy.wait()
 
 
 def visible_keys(frame):
@@ -282,43 +317,69 @@
     return slice(index * count, (index + 1) * count)
 
 
-def head_kernel(order, parts, columns, *refs):
-    in_refs, out_refs = refs[:H], refs[H : 2 * H]
-    held, done, qt, kt, vt, ct, tt, gt, gq, gk, gv, wts, bias = refs[2 * H :]
-    rows = done.shape[1] // 4
+def head_kernel(order, back, groups, parts, window, lookback, *refs):
+    arrays, in_refs, out_refs = refs[:4], refs[4 : 3 + H], refs[3 + H : 3 + 2 * H]
+    held, own_ref, window_ref, lookback_ref, lookbacks, sems = refs[3 + 2 * H : 12 + 2 * H][:4], *refs[
+        7 + 2 * H : 12 + 2 * H
+    ]
+    qt, kt, vt, ct, tt, mt, gt, gq, gk, gv, wts, bias = refs[12 + 2 * H :]
+    rows = own_ref.shape[0] // 4
     frames, _, patches = wts.shape
-    pairs = frames // 2
     scale = 1.0 / math.sqrt(SIZE)
 
-    for partner, ref in zip(order, in_refs):
-        held[place(partner, parts)] = ref[...]
-
-    def natural(number, pair):
-        return held[rows_of(pair, parts), rows_of(number, rows)].reshape(patches, LANES)
-
-    info = [held[part, 4 * rows : 4 * rows + INFO] for part in range(parts)]
-    sides = [interleave(info[part], info[part + 1]) for part in range(0, parts, 2)]
+    head = place((0, 0), parts)
+    moves = [(window, window_ref), (lookback, lookback_ref)]
+    moves += [(a.at[:, :, columns_of(head)], b) for a, b in zip(arrays, held)]
+    copies = fetch(moves, sems)
+
+    def natural(number, group):
+        at = rows_of(number, rows)
+        found = [in_refs[order.index((group, part)) - 1][at] if group or part else own_ref[at] for part in range(parts)]
+        return jnp.concatenate(found, axis=0)
+
+    def tile(group, part):
+        return in_refs[order.index((group, part)) - 1][4 * rows :] if group or part else info
+
+    def pair_rows(group):
+        at = lax.bitwise_xor(lax.axis_index("frame"), group) * LANES
+        return pl.ds(pl.multiple_of(at, LANES), LANES)
+
+    def turn(group):
+        at = pair_rows(group)
+        qt[at] = natural(0, group).T * scale
+        kt[at] = natural(1, group).T
+        vt[at] = natural(2, group).T
+        ct[at] = natural(3, group).T
+        lookbacks[lax.bitwise_xor(lax.axis_index("frame"), group)] = tile(group, 0)
+
+    for group in range(1, groups):
+        turn(group)
+    for copy in copies:
+        copy.wait()
+    for number, ref in enumerate(held):
+        own_ref[rows_of(number, rows)] = side_by_side(ref, head, slice(None))
+    info = whole_numbers(window_ref, lookback_ref, rows)
+    turn(0)
+
+    sides = [interleave(tile(0, part), tile(0, part + 1)) for part in range(0, parts, 2)]
     first = jnp.concatenate([side[0] for side in sides], axis=1)
     last = jnp.concatenate([side[1] for side in sides], axis=1)
-    key_block = (lax.broadcasted_iota(jnp.int32, (patches, patches), 0) // BLK).astype(jnp.float32)
-    seen = key_block == first[0:1]
-    for column in range(1, columns):
+    count = rows // BLK
+    block = lax.broadcasted_iota(jnp.int32, (parts * count, patches), 0)
+    block = lax.bitwise_xor(block // count, lax.axis_index("patch")) * count + block % count
+    block = block.astype(jnp.float32)
+    seen = block == first[0:1]
+    for column in range(1, window.shape[1]):
         of = first if column < INFO else last
-        seen = seen | (key_block == of[column % INFO : column % INFO + 1])
-    bias[...] = jnp.where(seen, 0.0, -jnp.inf)
-
-    for pair in range(pairs):
-        at = rows_of(pair, LANES)
-        qt[at] = natural(0, pair).T * scale
-        kt[at] = natural(1, pair).T
-        vt[at] = natural(2, pair).T
-        ct[at] = natural(3, pair).T
+        seen = seen | (block == of[column % INFO : column % INFO + 1])
+    mask = jnp.where(seen, 0.0, -jnp.inf)
+    for number in range(parts * count):
+        bias[rows_of(number, BLK)] = jnp.broadcast_to(mask[number : number + 1], (BLK, patches))
 
     for frame in range(frames):
-        tile = held[(frame // 2) * parts, 4 * rows : 4 * rows + INFO]
-        _, tile = interleave(tile, tile)
+        _, given = interleave(lookbacks[frame // 2], lookbacks[frame // 2])
         at = INFO - 2 + frame % 2
-        lookback = tile[at : at + 1]
+        seen_frames = given[at : at + 1]
         for chunk in range(patches // LANES):
             cols = rows_of(chunk, LANES)
             query = qt[rows_of(frame, SIZE), cols]
@@ -326,7 +387,7 @@
             scores = []
             for key in keys:
                 score = jnp.sum(query * kt[rows_of(key, SIZE), cols], axis=0, keepdims=True)
-                scores.append(jnp.where(lookback > float(frame - key), score, -jnp.inf))
+                scores.append(jnp.where(seen_frames > float(frame - key), score, -jnp.inf))
             top = scores[0]
             for score in scores[1:]:
                 top = jnp.maximum(top, score)
@@ -341,9 +402,9 @@
                 value = value + weight * vt[rows_of(key, SIZE), cols]
             tt[rows_of(frame, SIZE), cols] = value
 
-    for pair in range(pairs):
+    for pair in range(frames // 2):
         at = rows_of(pair, LANES)
-        keys = natural(1, pair)
+        keys = kt[at].T
         high = keys.astype(jnp.bfloat16).astype(jnp.float32)
         low = keys - high
         mid = low.astype(jnp.bfloat16).astype(jnp.float32)
@@ -352,7 +413,6 @@
         value = tt[at].T
         high = value.astype(jnp.bfloat16).astype(jnp.float32)
         values = [x.astype(jnp.bfloat16) for x in interleave(high, value - high)]
-        mixed = []
         for half in range(2):
             mine = rows_of(2 * pair + half, SIZE)
             query, grad = qt[mine], ct[mine]
@@ -372,14 +432,12 @@
             share = 1.0 / jnp.sum(exps, axis=0, keepdims=True)
             high, low = split(exps)
             mix = heads_dot(tt[mine], high, low, NN) * share
-            mixed.append(mix)
+            mt[mine] = mix
             gt[mine] = heads_dot(grad * share, high, low, NT)
             delta = jnp.sum(grad * mix, axis=0, keepdims=True)
             high, low = split(exps * (grad_weights - delta))
             gq[mine] = heads_dot(kt[mine], high, low, NN) * share
             gk[mine] = heads_dot(query * share, high, low, NT)
-        mixed = jnp.concatenate(mixed, axis=0).T.reshape(parts, rows, LANES)
-        done[rows_of(pair, parts), rows_of(0, rows)] = mixed
 
     gv[...] = jnp.zeros(gv.shape, jnp.float32)
     for frame in range(frames):
@@ -404,94 +462,93 @@
                 gv[of, cols] = gv[of, cols] + weight * grad
             gq[mine, cols] = grad_query * scale
 
-    for pair in range(pairs):
-        at = rows_of(pair, LANES)
-        for number, ref in enumerate((gq, gk, gv)):
-            done[rows_of(pair, parts), rows_of(number + 1, rows)] = ref[at].T.reshape(
-                parts, rows, LANES
-            )
-    for partner, ref in zip(order, out_refs):
-        ref[...] = done[place(partner, parts)]
+    for group in range(groups):
+        for number, ref in enumerate((mt, gq, gk, gv)):
+            turned = ref[pair_rows(group)].T
+            for part in range(parts):
+                at = rows_of(number, rows)
+                out_refs[back.index((group, part))][at] = turned[rows_of(part, rows)]
 
 
 def exchange(blocks, order, patch_count):
-    out = []
-    for block, (frame, patch) in zip(blocks, order):
-        pairs = [
-            (i * patch_count + j, (i ^ frame) * patch_count + (j ^ patch))
-            for i in range(H // patch_count)
-            for j in range(patch_count)
-        ]
-        out.append(block if frame == patch == 0 else lax.ppermute(block, ("frame", "patch"), pairs))
-    return out
+    return [
+        lax.ppermute(
+            block,
+            ("frame", "patch"),
+            [
+                (i * patch_count + j, (i ^ frame) * patch_count + (j ^ patch))
+                for i in range(H // patch_count)
+                for j in range(patch_count)
+            ],
+        )
+        for block, (frame, patch) in zip(blocks, order)
+    ]
 
 
 def shards_by_head(queries, key_rows, value_rows, cotangent, lookback, window):
     frames_here, patches_here, model_width = queries.shape
-    parts = lax.axis_size("patch")
-    frames = frames_here * lax.axis_size("frame")
-    patches = patches_here * parts
-    order = partners(lax.axis_size("frame"), parts)
+    groups, parts = lax.axis_size("frame"), lax.axis_size("patch")
+    frames, patches = frames_here * groups, patches_here * parts
+    order = OUTWARD
+    back = HOMEWARD
     vmem = pl.BlockSpec(memory_space=pltpu.VMEM)
     anywhere = pl.BlockSpec(memory_space=pl.ANY)
-
-    def blocks(rows):
-        return [jax.ShapeDtypeStruct((rows, LANES), jnp.float32)] * H
+    dma = pltpu.SemaphoreType.DMA
+    held = pltpu.VMEM(queries.shape, jnp.float32)
+    smem = [pltpu.SMEM(window.shape, jnp.int32), pltpu.SMEM(lookback.shape, jnp.int32)]
+    across = pltpu.VMEM((frames * SIZE, patches), jnp.float32)
+
+    def blocks(count, rows):
+        return [jax.ShapeDtypeStruct((rows, LANES), jnp.float32)] * count
 
     def params(mebibytes):
         return pltpu.CompilerParams(vmem_limit_bytes=mebibytes * 1024 * 1024)
 
+    given = (window, lookback, queries, key_rows, value_rows, cotangent)
     packed = pl.pallas_call(
-        lambda *refs: pack_kernel(order, parts, *refs),
-        out_shape=blocks(4 * patches_here + INFO),
+        lambda *refs: pack_kernel(order[1:], parts, *refs),
+        out_shape=blocks(H - 1, 4 * patches_here + INFO),
         in_specs=[anywhere] * 6,
-        out_specs=[vmem] * H,
-        scratch_shapes=[pltpu.VMEM(queries.shape, jnp.float32)] * 4
-        + [
-            pltpu.VMEM((H, 4 * patches_here, LANES), jnp.float32),
-            pltpu.SMEM(window.shape, jnp.int32),
-            pltpu.SMEM(lookback.shape, jnp.int32),
-            pltpu.SemaphoreType.DMA((6,)),
-        ],
+        out_specs=[vmem] * (H - 1),
+        scratch_shapes=[held] * 4 + smem + [dma((10,))],
         compiler_params=params(56),
         name="pack_heads",
-    )(window, lookback, queries, key_rows, value_rows, cotangent)
-    across = pltpu.VMEM((frames * SIZE, patches), jnp.float32)
+    )(*given)
     done = pl.pallas_call(
-        lambda *refs: head_kernel(order, parts, window.shape[1], *refs),
-        out_shape=blocks(4 * patches_here),
-        in_specs=[vmem] * H,
+        lambda *refs: head_kernel(order, back, groups, parts, *refs),
+        out_shape=blocks(H, 4 * patches_here),
+        in_specs=[anywhere] * 6 + [vmem] * (H - 1),
         out_specs=[vmem] * H,
-        scratch_shapes=[
-            pltpu.VMEM((H, 4 * patches_here + INFO, LANES), jnp.float32),
-            pltpu.VMEM((H, 4 * patches_here, LANES), jnp.float32),
-        ]
-        + [across] * 9
+        scratch_shapes=[pltpu.VMEM((2, patches_here, LANES), jnp.float32)] * 4
+        + [pltpu.VMEM((4 * patches_here, LANES), jnp.float32)]
+        + smem
+        + [pltpu.VMEM((groups, INFO, LANES), jnp.float32), dma((6,))]
+        + [across] * 10
         + [
             pltpu.VMEM((frames, 8, patches), jnp.float32),
             pltpu.VMEM((patches, patches), jnp.float32),
         ],
-        compiler_params=params(40),
+        compiler_params=params(24),
         name="one_head",
-    )(*exchange(packed, order, parts))
+    )(*given, *exchange(packed, order[1:], parts))
     return pl.pallas_call(
-        lambda *refs: unpack_kernel(order, parts, *refs),
+        lambda *refs: unpack_kernel(back, groups, parts, *refs),
         out_shape=[jax.ShapeDtypeStruct(queries.shape, jnp.float32)] * 4,
         in_specs=[vmem] * H,
-        out_specs=[vmem] * 4,
-        scratch_shapes=[pltpu.VMEM((H, 4 * patches_here, LANES), jnp.float32)],
+        out_specs=[anywhere] * 4,
+        scratch_shapes=[held] * 4 + [dma((4,))],
         compiler_params=params(40),
         name="unpack_heads",
-    )(*exchange(done, order, parts))
+    )(done[0], *exchange(done[1:], back[1:], parts))
 
 
 def shards(queries, key_rows, value_rows, cotangent, lookback, window):
     frames_here, patches_here, model_width = queries.shape
     fits = (
         lax.axis_size("frame") * lax.axis_size("patch") == H
+        and lax.axis_size("patch") == 4
         and frames_here == 2
         and patches_here == SIZE
-        and lax.axis_size("patch") in (2, 4, 8)
         and model_width == H * SIZE
     )
     form = shards_by_head if fits else shards_general

time: 116 us -> 110 us (0.948)
  waiting for transfers between devices: 49.2 us -> 39.2 us
  starting transfers between devices: 54 us -> 58.1 us
    ppermute x30, waiting for transfers between devices: 49.2 us -> 39.2 us  [exchange(): lax.ppermute(block, ('frame', 'patch'), [(i * patch_count + j, (i ^ frame...]
    ppermute x30, starting transfers between devices: 54 us -> 58.1 us  [exchange(): lax.ppermute(block, ('frame', 'patch'), [(i * patch_count + j, (i ^ frame...]
  transfers between devices with their start and end apart: 30 -> 30, of which waited for: 10 -> 13; matrix products, arithmetic and copies ran while one was open for 0% -> 0% of each run, Pallas kernels for 0% -> 0%
where the time goes in v2:
time: 110 us; the launch traced here: 109 us
  starting transfers between devices  58.1 us (53%)
  waiting for transfers between devices  39.2 us (36%)
  Pallas kernels  11.4 us (10%)
    ppermute x30, starting transfers between devices, exchange(): lax.ppermute(block, ('frame', 'patch'), [(i * patch_count + j, (i ^ frame...  58.1 us
    ppermute x30, waiting for transfers between devices, exchange(): lax.ppermute(block, ('frame', 'patch'), [(i * patch_count + j, (i ^ frame...  39.2 us
    pallas_call x1, Pallas kernels, shards_by_head(): pl.pallas_call(lambda *refs: head_kernel(order, back, groups, parts, *ref...  6.24 us
    pallas_call x1, Pallas kernels, shards_by_head(): pl.pallas_call(lambda *refs: pack_kernel(order[1:], parts, *refs), out_sh...  3.27 us
  transfers between devices with their start and end apart: 30, of which 13 were waited for; matrix products, arithmetic and copies ran while one was open for 0% of the time, Pallas kernels for 0%

profile of v2, /device:TPU:0, one launch (start us, length us, event | category | flops | bytes accessed | tf_op | source)
XLA Modules:
  0.0 109.4 jit_solution(13087628019447463006)
XLA Ops:
  0.7 3.3 %pack_heads.1 = (f32[264,128]{1,0:T(8,128)}, f32[264,128]{1,0:T(8,128)}, f32[264,128]{1,0:T(8,128)}, f32[264,128]{1,0:T(8,128)}, f32[264,128]{1,0:T(8,128)}, /*i...) custom-call(s32[4,12]{1,0:T(4,128)} %refs_0_.3, ...), custom_call_target="tpu_custom_call" | custom-call | tf_op jit(solution)/shard_map/pack_heads/pallas_call | solution.py:508
  4.0 5.5 %collective-permute-start = (f32[264,128]{1,0:T(8,128)}, f32[264,128]{1,0:T(8,128)S(1)}, u32[]{:S(2)}, u32[]{:S(2)}) collective-permute-start(f32[264,128]{1,0:T(8,128)} %get-tuple-element.35), channel_id=1, source_target_pairs={{0,15},{1,14},{2,13},{3,12},{4,11},{5,10},{6,9},{7,8},{8,7},{9,6},... | collective-permute-start | bytes 405512 | tf_op jit(solution)/shard_map/ppermute | solution.py:475
  10.4 1.2 %collective-permute-start.4 = (f32[264,128]{1,0:T(8,128)}, f32[264,128]{1,0:T(8,128)S(1)}, u32[]{:S(2)}, u32[]{:S(2)}) collective-permute-start(f32[264,128]{1,0:T(8,128)} %get-tuple-element.39), channel_id=1, source_target_pairs={{0,5},{1,4},{2,7},{3,6},{4,1},{5,0},{6,3},{7,2},{8,13},{9,12},{10,... | collective-permute-start | bytes 405512 | tf_op jit(solution)/shard_map/ppermute | solution.py:475
  11.6 2.2 %collective-permute-done.refs_6_ = f32[264,128]{1,0:T(8,128)S(1)} collective-permute-done((f32[264,128]{1,0:T(8,128)}, f32[264,128]{1,0:T(8,128)S(1)}, u32[]{:S(2)}, u32[]{:S(2)}) %collective-permute-start) | collective-permute-done | bytes 135200 | tf_op jit(solution)/shard_map/ppermute | solution.py:475
  13.8 3.8 %collective-permute-start.5 = (f32[264,128]{1,0:T(8,128)}, f32[264,128]{1,0:T(8,128)S(1)}, u32[]{:S(2)}, u32[]{:S(2)}) collective-permute-start(f32[264,128]{1,0:T(8,128)} %get-tuple-element.40), channel_id=1, source_target_pairs={{0,7},{1,6},{2,5},{3,4},{4,3},{5,2},{6,1},{7,0},{8,15},{9,14},{10,... | collective-permute-start | bytes 405512 | tf_op jit(solution)/shard_map/ppermute | solution.py:475
  19.1 3.6 %collective-permute-start.7 = (f32[264,128]{1,0:T(8,128)}, f32[264,128]{1,0:T(8,128)S(1)}, u32[]{:S(2)}, u32[]{:S(2)}) collective-permute-start(f32[264,128]{1,0:T(8,128)} %get-tuple-element.42), channel_id=1, source_target_pairs={{0,9},{1,8},{2,11},{3,10},{4,13},{5,12},{6,15},{7,14},{8,1},{9,0},... | collective-permute-start | bytes 405512 | tf_op jit(solution)/shard_map/ppermute | solution.py:475
  22.7 1.9 %collective-permute-start.8 = (f32[264,128]{1,0:T(8,128)}, f32[264,128]{1,0:T(8,128)S(1)}, u32[]{:S(2)}, u32[]{:S(2)}) collective-permute-start(f32[264,128]{1,0:T(8,128)} %get-tuple-element.43), channel_id=1, source_target_pairs={{0,11},{1,10},{2,9},{3,8},{4,15},{5,14},{6,13},{7,12},{8,3},{9,2},... | collective-permute-start | bytes 405512 | tf_op jit(solution)/shard_map/ppermute | solution.py:475
  24.7 1.0 collective-permute-start.9
  26.1 5.5 %collective-permute-start.10 = (f32[264,128]{1,0:T(8,128)}, f32[264,128]{1,0:T(8,128)S(1)}, u32[]{:S(2)}, u32[]{:S(2)}) collective-permute-start(f32[264,128]{1,0:T(8,128)} %get-tuple-element.45), channel_id=1, source_target_pairs={{0,14},{1,15},{2,12},{3,13},{4,10},{5,11},{6,8},{7,9},{8,6},{9,7},... | collective-permute-start | bytes 405512 | tf_op jit(solution)/shard_map/ppermute | solution.py:475
  31.5 8.2 %collective-permute-done.6.refs_12_ = f32[264,128]{1,0:T(8,128)S(1)} collective-permute-done((f32[264,128]{1,0:T(8,128)}, f32[264,128]{1,0:T(8,128)S(1)}, u32[]{:S(2)}, u32[]{:S(2)}) %collective-permute-start.6) | collective-permute-done | bytes 135200 | tf_op jit(solution)/shard_map/ppermute | solution.py:475
  39.8 3.5 %collective-permute-start.12 = (f32[264,128]{1,0:T(8,128)}, f32[264,128]{1,0:T(8,128)S(1)}, u32[]{:S(2)}, u32[]{:S(2)}) collective-permute-start(f32[264,128]{1,0:T(8,128)} %get-tuple-element.47), channel_id=1, source_target_pairs={{0,2},{1,3},{2,0},{3,1},{4,6},{5,7},{6,4},{7,5},{8,10},{9,11},{10,... | collective-permute-start | bytes 405512 | tf_op jit(solution)/shard_map/ppermute | solution.py:475
  43.8 1.2 %collective-permute-start.14 = (f32[264,128]{1,0:T(8,128)}, f32[264,128]{1,0:T(8,128)S(1)}, u32[]{:S(2)}, u32[]{:S(2)}) collective-permute-start(f32[264,128]{1,0:T(8,128)} %get-tuple-element.49), channel_id=1, source_target_pairs={{0,3},{1,2},{2,1},{3,0},{4,7},{5,6},{6,5},{7,4},{8,11},{9,10},{10,... | collective-permute-start | bytes 405512 | tf_op jit(solution)/shard_map/ppermute | solution.py:475
  45.3 5.2 %collective-permute-done.11.refs_17_ = f32[264,128]{1,0:T(8,128)S(1)} collective-permute-done((f32[264,128]{1,0:T(8,128)}, f32[264,128]{1,0:T(8,128)S(1)}, u32[]{:S(2)}, u32[]{:S(2)}) %collective-permute-start.11) | collective-permute-done | bytes 135200 | tf_op jit(solution)/shard_map/ppermute | solution.py:475
  50.5 3.7 %collective-permute-done.12.refs_18_ = f32[264,128]{1,0:T(8,128)S(1)} collective-permute-done((f32[264,128]{1,0:T(8,128)}, f32[264,128]{1,0:T(8,128)S(1)}, u32[]{:S(2)}, u32[]{:S(2)}) %collective-permute-start.12) | collective-permute-done | bytes 135200 | tf_op jit(solution)/shard_map/ppermute | solution.py:475
  54.2 6.2 %one_head.1 = (f32[256,128]{1,0:T(8,128)S(1)}, f32[256,128]{1,0:T(8,128)S(1)}, f32[256,128]{1,0:T(8,128)S(1)}, f32[256,128]{1,0:T(8,128)S(1)}, f32[256,128]{1,0:...) custom-call(s32[4,12]{1,0:T(4,128)S(1)} %copy-done.4, ...), custom_call_target="tpu_custom_call" | custom-call | tf_op jit(solution)/shard_map/one_head/pallas_call | solution.py:517
  60.5 2.2 %collective-permute-start.15 = (f32[256,128]{1,0:T(8,128)S(1)}, f32[256,128]{1,0:T(8,128)S(1)}, u32[]{:S(2)}, u32[]{:S(2)}) collective-permute-start(f32[256,128]{1,0:T(8,128)S(1)} %get-tuple-element.51), channel_id=1, source_target_pairs={{0,15},{1,14},{2,13},{3,12},{4,11},{5,10},{6,9},{7,8},{8,7},{9,6},... | collective-permute-start | bytes 393224 | tf_op jit(solution)/shard_map/ppermute | solution.py:475
  62.7 2.5 %collective-permute-start.16 = (f32[256,128]{1,0:T(8,128)S(1)}, f32[256,128]{1,0:T(8,128)S(1)}, u32[]{:S(2)}, u32[]{:S(2)}) collective-permute-start(f32[256,128]{1,0:T(8,128)S(1)} %get-tuple-element.52), channel_id=1, source_target_pairs={{0,1},{1,0},{2,3},{3,2},{4,5},{5,4},{6,7},{7,6},{8,9},{9,8},{10,11... | collective-permute-start | bytes 393224 | tf_op jit(solution)/shard_map/ppermute | solution.py:475
  65.3 1.6 %collective-permute-start.19 = (f32[256,128]{1,0:T(8,128)S(1)}, f32[256,128]{1,0:T(8,128)S(1)}, u32[]{:S(2)}, u32[]{:S(2)}) collective-permute-start(f32[256,128]{1,0:T(8,128)S(1)} %get-tuple-element.55), channel_id=1, source_target_pairs={{0,5},{1,4},{2,7},{3,6},{4,1},{5,0},{6,3},{7,2},{8,13},{9,12},{10,... | collective-permute-start | bytes 393224 | tf_op jit(solution)/shard_map/ppermute | solution.py:475
  67.0 2.0 %collective-permute-done.15.refs_1_ = f32[256,128]{1,0:T(8,128)S(1)} collective-permute-done((f32[256,128]{1,0:T(8,128)S(1)}, f32[256,128]{1,0:T(8,128)S(1)}, u32[]{:S(2)}, u32[]{:S(2)}) %collective-permute-start.15) | collective-permute-done | bytes 131104 | tf_op jit(solution)/shard_map/ppermute | solution.py:475
  69.0 2.2 %collective-permute-start.20 = (f32[256,128]{1,0:T(8,128)S(1)}, f32[256,128]{1,0:T(8,128)S(1)}, u32[]{:S(2)}, u32[]{:S(2)}) collective-permute-start(f32[256,128]{1,0:T(8,128)S(1)} %get-tuple-element.56), channel_id=1, source_target_pairs={{0,7},{1,6},{2,5},{3,4},{4,3},{5,2},{6,1},{7,0},{8,15},{9,14},{10,... | collective-permute-start | bytes 393224 | tf_op jit(solution)/shard_map/ppermute | solution.py:475
  71.2 2.5 %collective-permute-start.21 = (f32[256,128]{1,0:T(8,128)S(1)}, f32[256,128]{1,0:T(8,128)S(1)}, u32[]{:S(2)}, u32[]{:S(2)}) collective-permute-start(f32[256,128]{1,0:T(8,128)S(1)} %get-tuple-element.57), channel_id=1, source_target_pairs={{0,10},{1,11},{2,8},{3,9},{4,14},{5,15},{6,12},{7,13},{8,2},{9,3},... | collective-permute-start | bytes 393224 | tf_op jit(solution)/shard_map/ppermute | solution.py:475
  73.7 1.1 %collective-permute-start.22 = (f32[256,128]{1,0:T(8,128)S(1)}, f32[256,128]{1,0:T(8,128)S(1)}, u32[]{:S(2)}, u32[]{:S(2)}) collective-permute-start(f32[256,128]{1,0:T(8,128)S(1)} %get-tuple-element.58), channel_id=1, source_target_pairs={{0,9},{1,8},{2,11},{3,10},{4,13},{5,12},{6,15},{7,14},{8,1},{9,0},... | collective-permute-start | bytes 393224 | tf_op jit(solution)/shard_map/ppermute | solution.py:475
  74.9 1.7 %collective-permute-done.18.refs_4_ = f32[256,128]{1,0:T(8,128)S(1)} collective-permute-done((f32[256,128]{1,0:T(8,128)S(1)}, f32[256,128]{1,0:T(8,128)S(1)}, u32[]{:S(2)}, u32[]{:S(2)}) %collective-permute-start.18) | collective-permute-done | bytes 131104 | tf_op jit(solution)/shard_map/ppermute | solution.py:475
  76.6 3.5 %collective-permute-start.23 = (f32[256,128]{1,0:T(8,128)S(1)}, f32[256,128]{1,0:T(8,128)S(1)}, u32[]{:S(2)}, u32[]{:S(2)}) collective-permute-start(f32[256,128]{1,0:T(8,128)S(1)} %get-tuple-element.59), channel_id=1, source_target_pairs={{0,11},{1,10},{2,9},{3,8},{4,15},{5,14},{6,13},{7,12},{8,3},{9,2},... | collective-permute-start | bytes 393224 | tf_op jit(solution)/shard_map/ppermute | solution.py:475
  80.2 7.2 %collective-permute-start.25 = (f32[256,128]{1,0:T(8,128)S(1)}, f32[256,128]{1,0:T(8,128)S(1)}, u32[]{:S(2)}, u32[]{:S(2)}) collective-permute-start(f32[256,128]{1,0:T(8,128)S(1)} %get-tuple-element.61), channel_id=1, source_target_pairs={{0,14},{1,15},{2,12},{3,13},{4,10},{5,11},{6,8},{7,9},{8,6},{9,7},... | collective-permute-start | bytes 393224 | tf_op jit(solution)/shard_map/ppermute | solution.py:475
  87.3 7.0 %collective-permute-done.21.refs_7_ = f32[256,128]{1,0:T(8,128)S(1)} collective-permute-done((f32[256,128]{1,0:T(8,128)S(1)}, f32[256,128]{1,0:T(8,128)S(1)}, u32[]{:S(2)}, u32[]{:S(2)}) %collective-permute-start.21) | collective-permute-done | bytes 131104 | tf_op jit(solution)/shard_map/ppermute | solution.py:475
  94.4 2.6 %collective-permute-start.27 = (f32[256,128]{1,0:T(8,128)S(1)}, f32[256,128]{1,0:T(8,128)S(1)}, u32[]{:S(2)}, u32[]{:S(2)}) collective-permute-start(f32[256,128]{1,0:T(8,128)S(1)} %get-tuple-element.63), channel_id=1, source_target_pairs={{0,2},{1,3},{2,0},{3,1},{4,6},{5,7},{6,4},{7,5},{8,10},{9,11},{10,... | collective-permute-start | bytes 393224 | tf_op jit(solution)/shard_map/ppermute | solution.py:475
  97.0 1.5 %collective-permute-start.28 = (f32[256,128]{1,0:T(8,128)S(1)}, f32[256,128]{1,0:T(8,128)S(1)}, u32[]{:S(2)}, u32[]{:S(2)}) collective-permute-start(f32[256,128]{1,0:T(8,128)S(1)} %get-tuple-element.64), channel_id=1, source_target_pairs={{0,8},{1,9},{2,10},{3,11},{4,12},{5,13},{6,14},{7,15},{8,0},{9,1},... | collective-permute-start | bytes 393224 | tf_op jit(solution)/shard_map/ppermute | solution.py:475
  98.5 1.4 %collective-permute-start.29 = (f32[256,128]{1,0:T(8,128)S(1)}, f32[256,128]{1,0:T(8,128)S(1)}, u32[]{:S(2)}, u32[]{:S(2)}) collective-permute-start(f32[256,128]{1,0:T(8,128)S(1)} %get-tuple-element.65), channel_id=1, source_target_pairs={{0,3},{1,2},{2,1},{3,0},{4,7},{5,6},{6,5},{7,4},{8,11},{9,10},{10,... | collective-permute-start | bytes 393224 | tf_op jit(solution)/shard_map/ppermute | solution.py:475
  100.1 4.1 %collective-permute-done.26.refs_12_ = f32[256,128]{1,0:T(8,128)S(1)} collective-permute-done((f32[256,128]{1,0:T(8,128)S(1)}, f32[256,128]{1,0:T(8,128)S(1)}, u32[]{:S(2)}, u32[]{:S(2)}) %collective-permute-start.26) | collective-permute-done | bytes 131104 | tf_op jit(solution)/shard_map/ppermute | solution.py:475
  104.2 3.4 %collective-permute-done.27.refs_13_ = f32[256,128]{1,0:T(8,128)S(1)} collective-permute-done((f32[256,128]{1,0:T(8,128)S(1)}, f32[256,128]{1,0:T(8,128)S(1)}, u32[]{:S(2)}, u32[]{:S(2)}) %collective-permute-start.27) | collective-permute-done | bytes 131104 | tf_op jit(solution)/shard_map/ppermute | solution.py:475
  107.6 1.9 %unpack_heads.1 = (f32[2,64,1024]{2,1,0:T(8,128)}, f32[2,64,1024]{2,1,0:T(8,128)}, f32[2,64,1024]{2,1,0:T(8,128)}, f32[2,64,1024]{2,1,0:T(8,128)}) custom-call(f32[256,128]{1,0:T(8,128)S(1)} %get-tuple-element.50.refs_0_, f32[256,128]{1,0:T(8,128)S(1)} %collective-permute-done.15.refs_1_, f32[256,128]{1,0:T(8,128)S(1)} %collective-permute-done.16.refs_2_, ...), custom_call_target="tpu_custom_call" | custom-call | tf_op jit(solution)/shard_map/unpack_heads/pallas_call | solution.py:534
  (43 shorter events, 4.1 us)
Async XLA Ops:
  0.6 53.6 %copy-start.3 = (f32[2,64,1024]{2,1,0:T(8,128)S(1)}, f32[2,64,1024]{2,1,0:T(8,128)}, u32[]{:S(2)}) copy-start(f32[2,64,1024]{2,1,0:T(8,128)} %refs_5_.3) | copy-start | bytes 1572868
  0.6 53.6 %copy-start.2 = (f32[2,64,1024]{2,1,0:T(8,128)S(1)}, f32[2,64,1024]{2,1,0:T(8,128)}, u32[]{:S(2)}) copy-start(f32[2,64,1024]{2,1,0:T(8,128)} %refs_4_.3) | copy-start | bytes 1572868
  4.0 9.8 %collective-permute-start = (f32[264,128]{1,0:T(8,128)}, f32[264,128]{1,0:T(8,128)S(1)}, u32[]{:S(2)}, u32[]{:S(2)}) collective-permute-start(f32[264,128]{1,0:T(8,128)} %get-tuple-element.35), channel_id=1, source_target_pairs={{0,15},{1,14},{2,13},{3,12},{4,11},{5,10},{6,9},{7,8},{8,7},{9,6},... | collective-permute-start | bytes 405512 | tf_op jit(solution)/shard_map/ppermute | solution.py:475
  9.5 8.8 %collective-permute-start.1 = (f32[264,128]{1,0:T(8,128)}, f32[264,128]{1,0:T(8,128)S(1)}, u32[]{:S(2)}, u32[]{:S(2)}) collective-permute-start(f32[264,128]{1,0:T(8,128)} %get-tuple-element.36), channel_id=1, source_target_pairs={{0,1},{1,0},{2,3},{3,2},{4,5},{5,4},{6,7},{7,6},{8,9},{9,8},{10,11... | collective-permute-start | bytes 405512 | tf_op jit(solution)/shard_map/ppermute | solution.py:475
  9.5 9.6 %collective-permute-start.2 = (f32[264,128]{1,0:T(8,128)}, f32[264,128]{1,0:T(8,128)S(1)}, u32[]{:S(2)}, u32[]{:S(2)}) collective-permute-start(f32[264,128]{1,0:T(8,128)} %get-tuple-element.37), channel_id=1, source_target_pairs={{0,4},{1,5},{2,6},{3,7},{4,0},{5,1},{6,2},{7,3},{8,12},{9,13},{10,... | collective-permute-start | bytes 405512 | tf_op jit(solution)/shard_map/ppermute | solution.py:475
  10.1 12.6 %collective-permute-start.3 = (f32[264,128]{1,0:T(8,128)}, f32[264,128]{1,0:T(8,128)S(1)}, u32[]{:S(2)}, u32[]{:S(2)}) collective-permute-start(f32[264,128]{1,0:T(8,128)} %get-tuple-element.38), channel_id=1, source_target_pairs={{0,6},{1,7},{2,4},{3,5},{4,2},{5,3},{6,0},{7,1},{8,14},{9,15},{10,... | collective-permute-start | bytes 405512 | tf_op jit(solution)/shard_map/ppermute | solution.py:475
  10.4 14.3 %collective-permute-start.4 = (f32[264,128]{1,0:T(8,128)}, f32[264,128]{1,0:T(8,128)S(1)}, u32[]{:S(2)}, u32[]{:S(2)}) collective-permute-start(f32[264,128]{1,0:T(8,128)} %get-tuple-element.39), channel_id=1, source_target_pairs={{0,5},{1,4},{2,7},{3,6},{4,1},{5,0},{6,3},{7,2},{8,13},{9,12},{10,... | collective-permute-start | bytes 405512 | tf_op jit(solution)/shard_map/ppermute | solution.py:475
  13.8 12.3 %collective-permute-start.5 = (f32[264,128]{1,0:T(8,128)}, f32[264,128]{1,0:T(8,128)S(1)}, u32[]{:S(2)}, u32[]{:S(2)}) collective-permute-start(f32[264,128]{1,0:T(8,128)} %get-tuple-element.40), channel_id=1, source_target_pairs={{0,7},{1,6},{2,5},{3,4},{4,3},{5,2},{6,1},{7,0},{8,15},{9,14},{10,... | collective-permute-start | bytes 405512 | tf_op jit(solution)/shard_map/ppermute | solution.py:475
  18.3 21.5 %collective-permute-start.6 = (f32[264,128]{1,0:T(8,128)}, f32[264,128]{1,0:T(8,128)S(1)}, u32[]{:S(2)}, u32[]{:S(2)}) collective-permute-start(f32[264,128]{1,0:T(8,128)} %get-tuple-element.41), channel_id=1, source_target_pairs={{0,10},{1,11},{2,8},{3,9},{4,14},{5,15},{6,12},{7,13},{8,2},{9,3},... | collective-permute-start | bytes 405512 | tf_op jit(solution)/shard_map/ppermute | solution.py:475
  19.1 20.7 %collective-permute-start.7 = (f32[264,128]{1,0:T(8,128)}, f32[264,128]{1,0:T(8,128)S(1)}, u32[]{:S(2)}, u32[]{:S(2)}) collective-permute-start(f32[264,128]{1,0:T(8,128)} %get-tuple-element.42), channel_id=1, source_target_pairs={{0,9},{1,8},{2,11},{3,10},{4,13},{5,12},{6,15},{7,14},{8,1},{9,0},... | collective-permute-start | bytes 405512 | tf_op jit(solution)/shard_map/ppermute | solution.py:475
  22.7 20.6 %collective-permute-start.8 = (f32[264,128]{1,0:T(8,128)}, f32[264,128]{1,0:T(8,128)S(1)}, u32[]{:S(2)}, u32[]{:S(2)}) collective-permute-start(f32[264,128]{1,0:T(8,128)} %get-tuple-element.43), channel_id=1, source_target_pairs={{0,11},{1,10},{2,9},{3,8},{4,15},{5,14},{6,13},{7,12},{8,3},{9,2},... | collective-permute-start | bytes 405512 | tf_op jit(solution)/shard_map/ppermute | solution.py:475
  24.7 19.1 %collective-permute-start.9 = (f32[264,128]{1,0:T(8,128)}, f32[264,128]{1,0:T(8,128)S(1)}, u32[]{:S(2)}, u32[]{:S(2)}) collective-permute-start(f32[264,128]{1,0:T(8,128)} %get-tuple-element.44), channel_id=1, source_target_pairs={{0,12},{1,13},{2,14},{3,15},{4,8},{5,9},{6,10},{7,11},{8,4},{9,5},... | collective-permute-start | bytes 405512 | tf_op jit(solution)/shard_map/ppermute | solution.py:475
  26.1 19.2 %collective-permute-start.10 = (f32[264,128]{1,0:T(8,128)}, f32[264,128]{1,0:T(8,128)S(1)}, u32[]{:S(2)}, u32[]{:S(2)}) collective-permute-start(f32[264,128]{1,0:T(8,128)} %get-tuple-element.45), channel_id=1, source_target_pairs={{0,14},{1,15},{2,12},{3,13},{4,10},{5,11},{6,8},{7,9},{8,6},{9,7},... | collective-permute-start | bytes 405512 | tf_op jit(solution)/shard_map/ppermute | solution.py:475
  39.8 10.8 %collective-permute-start.11 = (f32[264,128]{1,0:T(8,128)}, f32[264,128]{1,0:T(8,128)S(1)}, u32[]{:S(2)}, u32[]{:S(2)}) collective-permute-start(f32[264,128]{1,0:T(8,128)} %get-tuple-element.46), channel_id=1, source_target_pairs={{0,13},{1,12},{2,15},{3,14},{4,9},{5,8},{6,11},{7,10},{8,5},{9,4},... | collective-permute-start | bytes 405512 | tf_op jit(solution)/shard_map/ppermute | solution.py:475
  39.8 14.4 %collective-permute-start.12 = (f32[264,128]{1,0:T(8,128)}, f32[264,128]{1,0:T(8,128)S(1)}, u32[]{:S(2)}, u32[]{:S(2)}) collective-permute-start(f32[264,128]{1,0:T(8,128)} %get-tuple-element.47), channel_id=1, source_target_pairs={{0,2},{1,3},{2,0},{3,1},{4,6},{5,7},{6,4},{7,5},{8,10},{9,11},{10,... | collective-permute-start | bytes 405512 | tf_op jit(solution)/shard_map/ppermute | solution.py:475
  43.3 10.9 %collective-permute-start.13 = (f32[264,128]{1,0:T(8,128)}, f32[264,128]{1,0:T(8,128)S(1)}, u32[]{:S(2)}, u32[]{:S(2)}) collective-permute-start(f32[264,128]{1,0:T(8,128)} %get-tuple-element.48), channel_id=1, source_target_pairs={{0,8},{1,9},{2,10},{3,11},{4,12},{5,13},{6,14},{7,15},{8,0},{9,1},... | collective-permute-start | bytes 405512 | tf_op jit(solution)/shard_map/ppermute | solution.py:475
  43.8 10.4 %collective-permute-start.14 = (f32[264,128]{1,0:T(8,128)}, f32[264,128]{1,0:T(8,128)S(1)}, u32[]{:S(2)}, u32[]{:S(2)}) collective-permute-start(f32[264,128]{1,0:T(8,128)} %get-tuple-element.49), channel_id=1, source_target_pairs={{0,3},{1,2},{2,1},{3,0},{4,7},{5,6},{6,5},{7,4},{8,11},{9,10},{10,... | collective-permute-start | bytes 405512 | tf_op jit(solution)/shard_map/ppermute | solution.py:475
  60.5 8.5 %collective-permute-start.15 = (f32[256,128]{1,0:T(8,128)S(1)}, f32[256,128]{1,0:T(8,128)S(1)}, u32[]{:S(2)}, u32[]{:S(2)}) collective-permute-start(f32[256,128]{1,0:T(8,128)S(1)} %get-tuple-element.51), channel_id=1, source_target_pairs={{0,15},{1,14},{2,13},{3,12},{4,11},{5,10},{6,9},{7,8},{8,7},{9,6},... | collective-permute-start | bytes 393224 | tf_op jit(solution)/shard_map/ppermute | solution.py:475
  62.7 8.5 %collective-permute-start.16 = (f32[256,128]{1,0:T(8,128)S(1)}, f32[256,128]{1,0:T(8,128)S(1)}, u32[]{:S(2)}, u32[]{:S(2)}) collective-permute-start(f32[256,128]{1,0:T(8,128)S(1)} %get-tuple-element.52), channel_id=1, source_target_pairs={{0,1},{1,0},{2,3},{3,2},{4,5},{5,4},{6,7},{7,6},{8,9},{9,8},{10,11... | collective-permute-start | bytes 393224 | tf_op jit(solution)/shard_map/ppermute | solution.py:475
  65.2 8.5 %collective-permute-start.17 = (f32[256,128]{1,0:T(8,128)S(1)}, f32[256,128]{1,0:T(8,128)S(1)}, u32[]{:S(2)}, u32[]{:S(2)}) collective-permute-start(f32[256,128]{1,0:T(8,128)S(1)} %get-tuple-element.53), channel_id=1, source_target_pairs={{0,4},{1,5},{2,6},{3,7},{4,0},{5,1},{6,2},{7,3},{8,12},{9,13},{10,... | collective-permute-start | bytes 393224 | tf_op jit(solution)/shard_map/ppermute | solution.py:475
  65.3 11.2 %collective-permute-start.18 = (f32[256,128]{1,0:T(8,128)S(1)}, f32[256,128]{1,0:T(8,128)S(1)}, u32[]{:S(2)}, u32[]{:S(2)}) collective-permute-start(f32[256,128]{1,0:T(8,128)S(1)} %get-tuple-element.54), channel_id=1, source_target_pairs={{0,6},{1,7},{2,4},{3,5},{4,2},{5,3},{6,0},{7,1},{8,14},{9,15},{10,... | collective-permute-start | bytes 393224 | tf_op jit(solution)/shard_map/ppermute | solution.py:475
  65.3 14.8 %collective-permute-start.19 = (f32[256,128]{1,0:T(8,128)S(1)}, f32[256,128]{1,0:T(8,128)S(1)}, u32[]{:S(2)}, u32[]{:S(2)}) collective-permute-start(f32[256,128]{1,0:T(8,128)S(1)} %get-tuple-element.55), channel_id=1, source_target_pairs={{0,5},{1,4},{2,7},{3,6},{4,1},{5,0},{6,3},{7,2},{8,13},{9,12},{10,... | collective-permute-start | bytes 393224 | tf_op jit(solution)/shard_map/ppermute | solution.py:475
  69.0 11.2 %collective-permute-start.20 = (f32[256,128]{1,0:T(8,128)S(1)}, f32[256,128]{1,0:T(8,128)S(1)}, u32[]{:S(2)}, u32[]{:S(2)}) collective-permute-start(f32[256,128]{1,0:T(8,128)S(1)} %get-tuple-element.56), channel_id=1, source_target_pairs={{0,7},{1,6},{2,5},{3,4},{4,3},{5,2},{6,1},{7,0},{8,15},{9,14},{10,... | collective-permute-start | bytes 393224 | tf_op jit(solution)/shard_map/ppermute | solution.py:475
  71.2 23.2 %collective-permute-start.21 = (f32[256,128]{1,0:T(8,128)S(1)}, f32[256,128]{1,0:T(8,128)S(1)}, u32[]{:S(2)}, u32[]{:S(2)}) collective-permute-start(f32[256,128]{1,0:T(8,128)S(1)} %get-tuple-element.57), channel_id=1, source_target_pairs={{0,10},{1,11},{2,8},{3,9},{4,14},{5,15},{6,12},{7,13},{8,2},{9,3},... | collective-permute-start | bytes 393224 | tf_op jit(solution)/shard_map/ppermute | solution.py:475
  73.7 20.7 %collective-permute-start.22 = (f32[256,128]{1,0:T(8,128)S(1)}, f32[256,128]{1,0:T(8,128)S(1)}, u32[]{:S(2)}, u32[]{:S(2)}) collective-permute-start(f32[256,128]{1,0:T(8,128)S(1)} %get-tuple-element.58), channel_id=1, source_target_pairs={{0,9},{1,8},{2,11},{3,10},{4,13},{5,12},{6,15},{7,14},{8,1},{9,0},... | collective-permute-start | bytes 393224 | tf_op jit(solution)/shard_map/ppermute | solution.py:475
  76.6 20.4 %collective-permute-start.23 = (f32[256,128]{1,0:T(8,128)S(1)}, f32[256,128]{1,0:T(8,128)S(1)}, u32[]{:S(2)}, u32[]{:S(2)}) collective-permute-start(f32[256,128]{1,0:T(8,128)S(1)} %get-tuple-element.59), channel_id=1, source_target_pairs={{0,11},{1,10},{2,9},{3,8},{4,15},{5,14},{6,13},{7,12},{8,3},{9,2},... | collective-permute-start | bytes 393224 | tf_op jit(solution)/shard_map/ppermute | solution.py:475
  80.1 18.4 %collective-permute-start.24 = (f32[256,128]{1,0:T(8,128)S(1)}, f32[256,128]{1,0:T(8,128)S(1)}, u32[]{:S(2)}, u32[]{:S(2)}) collective-permute-start(f32[256,128]{1,0:T(8,128)S(1)} %get-tuple-element.60), channel_id=1, source_target_pairs={{0,12},{1,13},{2,14},{3,15},{4,8},{5,9},{6,10},{7,11},{8,4},{9,5},... | collective-permute-start | bytes 393224 | tf_op jit(solution)/shard_map/ppermute | solution.py:475
  80.2 19.9 %collective-permute-start.25 = (f32[256,128]{1,0:T(8,128)S(1)}, f32[256,128]{1,0:T(8,128)S(1)}, u32[]{:S(2)}, u32[]{:S(2)}) collective-permute-start(f32[256,128]{1,0:T(8,128)S(1)} %get-tuple-element.61), channel_id=1, source_target_pairs={{0,14},{1,15},{2,12},{3,13},{4,10},{5,11},{6,8},{7,9},{8,6},{9,7},... | collective-permute-start | bytes 393224 | tf_op jit(solution)/shard_map/ppermute | solution.py:475
  94.4 9.8 %collective-permute-start.26 = (f32[256,128]{1,0:T(8,128)S(1)}, f32[256,128]{1,0:T(8,128)S(1)}, u32[]{:S(2)}, u32[]{:S(2)}) collective-permute-start(f32[256,128]{1,0:T(8,128)S(1)} %get-tuple-element.62), channel_id=1, source_target_pairs={{0,13},{1,12},{2,15},{3,14},{4,9},{5,8},{6,11},{7,10},{8,5},{9,4},... | collective-permute-start | bytes 393224 | tf_op jit(solution)/shard_map/ppermute | solution.py:475
  94.4 13.2 %collective-permute-start.27 = (f32[256,128]{1,0:T(8,128)S(1)}, f32[256,128]{1,0:T(8,128)S(1)}, u32[]{:S(2)}, u32[]{:S(2)}) collective-permute-start(f32[256,128]{1,0:T(8,128)S(1)} %get-tuple-element.63), channel_id=1, source_target_pairs={{0,2},{1,3},{2,0},{3,1},{4,6},{5,7},{6,4},{7,5},{8,10},{9,11},{10,... | collective-permute-start | bytes 393224 | tf_op jit(solution)/shard_map/ppermute | solution.py:475
  97.0 10.6 %collective-permute-start.28 = (f32[256,128]{1,0:T(8,128)S(1)}, f32[256,128]{1,0:T(8,128)S(1)}, u32[]{:S(2)}, u32[]{:S(2)}) collective-permute-start(f32[256,128]{1,0:T(8,128)S(1)} %get-tuple-element.64), channel_id=1, source_target_pairs={{0,8},{1,9},{2,10},{3,11},{4,12},{5,13},{6,14},{7,15},{8,0},{9,1},... | collective-permute-start | bytes 393224 | tf_op jit(solution)/shard_map/ppermute | solution.py:475
  98.5 9.0 %collective-permute-start.29 = (f32[256,128]{1,0:T(8,128)S(1)}, f32[256,128]{1,0:T(8,128)S(1)}, u32[]{:S(2)}, u32[]{:S(2)}) collective-permute-start(f32[256,128]{1,0:T(8,128)S(1)} %get-tuple-element.65), channel_id=1, source_target_pairs={{0,3},{1,2},{2,1},{3,0},{4,7},{5,6},{6,5},{7,4},{8,11},{9,10},{10,... | collective-permute-start | bytes 393224 | tf_op jit(solution)/shard_map/ppermute | solution.py:475
  (4 other events, 132.5 us)

commit v3 on v2

--- a/solution.py
+++ b/solution.py
@@ -192,6 +192,7 @@
     (0, 0), (3, 3), (0, 1), (1, 0), (1, 2), (1, 1), (1, 3), (2, 2),
     (2, 1), (2, 3), (3, 0), (3, 2), (3, 1), (0, 2), (2, 0), (0, 3),
 )
+HIDDEN = -1e30
 NN = ((1,), (0,))
 NT = ((1,), (1,))
 
@@ -322,7 +323,7 @@
     held, own_ref, window_ref, lookback_ref, lookbacks, sems = refs[3 + 2 * H : 12 + 2 * H][:4], *refs[
         7 + 2 * H : 12 + 2 * H
     ]
-    qt, kt, vt, ct, tt, mt, gt, gq, gk, gv, wts, bias = refs[12 + 2 * H :]
+    qt, kt, vt, ct, tt, mt, gt, gq, gk, gv, wts, bias, blocks = refs[12 + 2 * H :]
     rows = own_ref.shape[0] // 4
     frames, _, patches = wts.shape
     scale = 1.0 / math.sqrt(SIZE)
@@ -372,11 +373,14 @@
     for column in range(1, window.shape[1]):
         of = first if column < INFO else last
         seen = seen | (block == of[column % INFO : column % INFO + 1])
-    mask = jnp.where(seen, 0.0, -jnp.inf)
-    for number in range(parts * count):
-        bias[rows_of(number, BLK)] = jnp.broadcast_to(mask[number : number + 1], (BLK, patches))
-
-    for frame in range(frames):
+    mask = jnp.where(seen, 0.0, HIDDEN).astype(jnp.bfloat16)
+    spare = jnp.zeros((LANES - parts * count, patches), jnp.bfloat16)
+    bias[...] = jnp.concatenate([mask, spare], axis=0)
+    key_block = lax.broadcasted_iota(jnp.int32, (patches, LANES), 0) // BLK
+    lane = lax.broadcasted_iota(jnp.int32, (patches, LANES), 1)
+    blocks[...] = jnp.where(key_block == lane, 1.0, 0.0).astype(jnp.bfloat16)
+
+    def look_back(frame):
         _, given = interleave(lookbacks[frame // 2], lookbacks[frame // 2])
         at = INFO - 2 + frame % 2
         seen_frames = given[at : at + 1]
@@ -402,45 +406,66 @@
                 value = value + weight * vt[rows_of(key, SIZE), cols]
             tt[rows_of(frame, SIZE), cols] = value
 
-    for pair in range(frames // 2):
-        at = rows_of(pair, LANES)
-        keys = kt[at].T
-        high = keys.astype(jnp.bfloat16).astype(jnp.float32)
-        low = keys - high
-        mid = low.astype(jnp.bfloat16).astype(jnp.float32)
-        upper = [x.astype(jnp.bfloat16) for x in interleave(high, mid)]
-        lower = [x.astype(jnp.bfloat16) for x in interleave(high, low - mid)]
-        value = tt[at].T
-        high = value.astype(jnp.bfloat16).astype(jnp.float32)
-        values = [x.astype(jnp.bfloat16) for x in interleave(high, value - high)]
-        for half in range(2):
-            mine = rows_of(2 * pair + half, SIZE)
-            query, grad = qt[mine], ct[mine]
-            high, mid = split(query)
-            low = query - high.astype(jnp.float32) - mid.astype(jnp.float32)
-            low = low.astype(jnp.bfloat16)
-            logits = dot(
-                jnp.concatenate([upper[half]] * 2, axis=1),
-                jnp.concatenate([high, high, mid, mid], axis=0),
-                NN,
-            )
-            logits = logits + dot(lower[half], jnp.concatenate([low, high], axis=0), NN)
-            logits = logits + bias[...]
-            grad_weights = dot(jnp.concatenate([values[half]] * 2, axis=1), stacked(grad, 2), NN)
-            top = jnp.max(logits, axis=0, keepdims=True)
-            exps = jnp.exp(logits - top)
-            share = 1.0 / jnp.sum(exps, axis=0, keepdims=True)
-            high, low = split(exps)
-            mix = heads_dot(tt[mine], high, low, NN) * share
-            mt[mine] = mix
-            gt[mine] = heads_dot(grad * share, high, low, NT)
-            delta = jnp.sum(grad * mix, axis=0, keepdims=True)
-            high, low = split(exps * (grad_weights - delta))
-            gq[mine] = heads_dot(kt[mine], high, low, NN) * share
-            gk[mine] = heads_dot(query * share, high, low, NT)
-
-    gv[...] = jnp.zeros(gv.shape, jnp.float32)
-    for frame in range(frames):
+    state = {}
+
+    def products(frame):
+        mine = rows_of(frame, SIZE)
+        if frame % 2 == 0:
+            at = rows_of(frame // 2, LANES)
+            keys = kt[at].T
+            high = keys.astype(jnp.bfloat16).astype(jnp.float32)
+            low = keys - high
+            mid = low.astype(jnp.bfloat16).astype(jnp.float32)
+            upper = [x.astype(jnp.bfloat16) for x in interleave(high, mid)]
+            lower = [x.astype(jnp.bfloat16) for x in interleave(high, low - mid)]
+            value = tt[at].T
+            high = value.astype(jnp.bfloat16).astype(jnp.float32)
+            values = [x.astype(jnp.bfloat16) for x in interleave(high, value - high)]
+            state["pair"] = list(zip(upper, lower, values))
+        upper, lower, value = state["pair"][frame % 2]
+        query = qt[mine]
+        high, mid = split(query)
+        low = query - high.astype(jnp.float32) - mid.astype(jnp.float32)
+        low = low.astype(jnp.bfloat16)
+        logits = dot(
+            jnp.concatenate([upper] * 2, axis=1),
+            jnp.concatenate([high, high, mid, mid], axis=0),
+            NN,
+        )
+        logits = logits + dot(
+            jnp.concatenate([lower, blocks[...]], axis=1),
+            jnp.concatenate([low, high, bias[...]], axis=0),
+            NN,
+        )
+        grad_weights = dot(jnp.concatenate([value] * 2, axis=1), stacked(ct[mine], 2), NN)
+        state[frame] = logits, grad_weights
+
+    def weigh(frame):
+        logits, grad_weights = state[frame]
+        top = jnp.max(logits, axis=0, keepdims=True)
+        exps = jnp.exp(logits - top)
+        share = 1.0 / jnp.sum(exps, axis=0, keepdims=True)
+        state[frame] = exps, *split(exps), share, grad_weights
+
+    def mix(frame):
+        mine = rows_of(frame, SIZE)
+        exps, high, low, share, grad_weights = state[frame]
+        mt[mine] = heads_dot(tt[mine], high, low, NN) * share
+        gt[mine] = heads_dot(ct[mine] * share, high, low, NT)
+
+    def differ(frame):
+        mine = rows_of(frame, SIZE)
+        exps, _, _, share, grad_weights = state[frame]
+        delta = jnp.sum(ct[mine] * mt[mine], axis=0, keepdims=True)
+        state[frame] = *split(exps * (grad_weights - delta)), share
+
+    def finish(frame):
+        mine = rows_of(frame, SIZE)
+        high, low, share = state.pop(frame)
+        gq[mine] = heads_dot(kt[mine], high, low, NN) * share
+        gk[mine] = heads_dot(qt[mine] * share, high, low, NT)
+
+    def hand_back(frame):
         mine = rows_of(frame, SIZE)
         for chunk in range(patches // LANES):
             cols = rows_of(chunk, LANES)
@@ -459,8 +484,24 @@
                 score = weight * (term - inner)
                 grad_query = grad_query + score * kt[of, cols]
                 gk[of, cols] = gk[of, cols] + score * query
-                gv[of, cols] = gv[of, cols] + weight * grad
+                if key == frame:
+                    gv[of, cols] = weight * grad
+                else:
+                    gv[of, cols] = gv[of, cols] + weight * grad
             gq[mine, cols] = grad_query * scale
+
+    for step in range(frames + 5):
+        for late, does in (
+            (0, look_back),
+            (2, products),
+            (3, weigh),
+            (4, differ),
+            (3, mix),
+            (4, finish),
+            (5, hand_back),
+        ):
+            if 0 <= step - late < frames:
+                does(step - late)
 
     for group in range(groups):
         for number, ref in enumerate((mt, gq, gk, gv)):
@@ -526,7 +567,8 @@
         + [across] * 10
         + [
             pltpu.VMEM((frames, 8, patches), jnp.float32),
-            pltpu.VMEM((patches, patches), jnp.float32),
+            pltpu.VMEM((LANES, patches), jnp.bfloat16),
+            pltpu.VMEM((patches, LANES), jnp.bfloat16),
         ],
         compiler_params=params(24),
         name="one_head",

time: 110 us -> 109 us (level)
  no operation moved by 1% of the time
where the time goes in v3:
time: 109 us; the launch traced here: 108 us
  starting transfers between devices  58.1 us (53%)
  waiting for transfers between devices  39.2 us (36%)
  Pallas kernels  10.3 us (9%)
    ppermute x30, starting transfers between devices, exchange(): lax.ppermute(block, ('frame', 'patch'), [(i * patch_count + j, (i ^ frame...  58.1 us
    ppermute x30, waiting for transfers between devices, exchange(): lax.ppermute(block, ('frame', 'patch'), [(i * patch_count + j, (i ^ frame...  39.2 us
    pallas_call x1, Pallas kernels, shards_by_head(): pl.pallas_call(lambda *refs: head_kernel(order, back, groups, parts, *ref...  5.18 us
    pallas_call x1, Pallas kernels, shards_by_head(): pl.pallas_call(lambda *refs: pack_kernel(order[1:], parts, *refs), out_sh...  3.27 us
  transfers between devices with their start and end apart: 30, of which 13 were waited for; matrix products, arithmetic and copies ran while one was open for 0% of the time, Pallas kernels for 0%

profile of v3, /device:TPU:0, one launch (start us, length us, event | category | flops | bytes accessed | tf_op | source)
XLA Modules:
  0.0 108.4 jit_solution(159014715633746526)
XLA Ops:
  0.7 3.3 %pack_heads.1 = (f32[264,128]{1,0:T(8,128)}, f32[264,128]{1,0:T(8,128)}, f32[264,128]{1,0:T(8,128)}, f32[264,128]{1,0:T(8,128)}, f32[264,128]{1,0:T(8,128)}, /*i...) custom-call(s32[4,12]{1,0:T(4,128)} %refs_0_.3, ...), custom_call_target="tpu_custom_call" | custom-call | tf_op jit(solution)/shard_map/pack_heads/pallas_call | solution.py:549
  4.0 5.5 %collective-permute-start = (f32[264,128]{1,0:T(8,128)}, f32[264,128]{1,0:T(8,128)S(1)}, u32[]{:S(2)}, u32[]{:S(2)}) collective-permute-start(f32[264,128]{1,0:T(8,128)} %get-tuple-element.35), channel_id=1, source_target_pairs={{0,15},{1,14},{2,13},{3,12},{4,11},{5,10},{6,9},{7,8},{8,7},{9,6},... | collective-permute-start | bytes 405512 | tf_op jit(solution)/shard_map/ppermute | solution.py:516
  10.4 1.2 %collective-permute-start.4 = (f32[264,128]{1,0:T(8,128)}, f32[264,128]{1,0:T(8,128)S(1)}, u32[]{:S(2)}, u32[]{:S(2)}) collective-permute-start(f32[264,128]{1,0:T(8,128)} %get-tuple-element.39), channel_id=1, source_target_pairs={{0,5},{1,4},{2,7},{3,6},{4,1},{5,0},{6,3},{7,2},{8,13},{9,12},{10,... | collective-permute-start | bytes 405512 | tf_op jit(solution)/shard_map/ppermute | solution.py:516
  11.6 2.2 %collective-permute-done.refs_6_ = f32[264,128]{1,0:T(8,128)S(1)} collective-permute-done((f32[264,128]{1,0:T(8,128)}, f32[264,128]{1,0:T(8,128)S(1)}, u32[]{:S(2)}, u32[]{:S(2)}) %collective-permute-start) | collective-permute-done | bytes 135200 | tf_op jit(solution)/shard_map/ppermute | solution.py:516
  13.8 3.8 %collective-permute-start.5 = (f32[264,128]{1,0:T(8,128)}, f32[264,128]{1,0:T(8,128)S(1)}, u32[]{:S(2)}, u32[]{:S(2)}) collective-permute-start(f32[264,128]{1,0:T(8,128)} %get-tuple-element.40), channel_id=1, source_target_pairs={{0,7},{1,6},{2,5},{3,4},{4,3},{5,2},{6,1},{7,0},{8,15},{9,14},{10,... | collective-permute-start | bytes 405512 | tf_op jit(solution)/shard_map/ppermute | solution.py:516
  19.1 3.6 %collective-permute-start.7 = (f32[264,128]{1,0:T(8,128)}, f32[264,128]{1,0:T(8,128)S(1)}, u32[]{:S(2)}, u32[]{:S(2)}) collective-permute-start(f32[264,128]{1,0:T(8,128)} %get-tuple-element.42), channel_id=1, source_target_pairs={{0,9},{1,8},{2,11},{3,10},{4,13},{5,12},{6,15},{7,14},{8,1},{9,0},... | collective-permute-start | bytes 405512 | tf_op jit(solution)/shard_map/ppermute | solution.py:516
  22.7 1.9 %collective-permute-start.8 = (f32[264,128]{1,0:T(8,128)}, f32[264,128]{1,0:T(8,128)S(1)}, u32[]{:S(2)}, u32[]{:S(2)}) collective-permute-start(f32[264,128]{1,0:T(8,128)} %get-tuple-element.43), channel_id=1, source_target_pairs={{0,11},{1,10},{2,9},{3,8},{4,15},{5,14},{6,13},{7,12},{8,3},{9,2},... | collective-permute-start | bytes 405512 | tf_op jit(solution)/shard_map/ppermute | solution.py:516
  24.7 1.0 collective-permute-start.9
  26.1 5.5 %collective-permute-start.10 = (f32[264,128]{1,0:T(8,128)}, f32[264,128]{1,0:T(8,128)S(1)}, u32[]{:S(2)}, u32[]{:S(2)}) collective-permute-start(f32[264,128]{1,0:T(8,128)} %get-tuple-element.45), channel_id=1, source_target_pairs={{0,14},{1,15},{2,12},{3,13},{4,10},{5,11},{6,8},{7,9},{8,6},{9,7},... | collective-permute-start | bytes 405512 | tf_op jit(solution)/shard_map/ppermute | solution.py:516
  31.5 8.2 %collective-permute-done.6.refs_12_ = f32[264,128]{1,0:T(8,128)S(1)} collective-permute-done((f32[264,128]{1,0:T(8,128)}, f32[264,128]{1,0:T(8,128)S(1)}, u32[]{:S(2)}, u32[]{:S(2)}) %collective-permute-start.6) | collective-permute-done | bytes 135200 | tf_op jit(solution)/shard_map/ppermute | solution.py:516
  39.8 3.5 %collective-permute-start.12 = (f32[264,128]{1,0:T(8,128)}, f32[264,128]{1,0:T(8,128)S(1)}, u32[]{:S(2)}, u32[]{:S(2)}) collective-permute-start(f32[264,128]{1,0:T(8,128)} %get-tuple-element.47), channel_id=1, source_target_pairs={{0,2},{1,3},{2,0},{3,1},{4,6},{5,7},{6,4},{7,5},{8,10},{9,11},{10,... | collective-permute-start | bytes 405512 | tf_op jit(solution)/shard_map/ppermute | solution.py:516
  43.8 1.2 %collective-permute-start.14 = (f32[264,128]{1,0:T(8,128)}, f32[264,128]{1,0:T(8,128)S(1)}, u32[]{:S(2)}, u32[]{:S(2)}) collective-permute-start(f32[264,128]{1,0:T(8,128)} %get-tuple-element.49), channel_id=1, source_target_pairs={{0,3},{1,2},{2,1},{3,0},{4,7},{5,6},{6,5},{7,4},{8,11},{9,10},{10,... | collective-permute-start | bytes 405512 | tf_op jit(solution)/shard_map/ppermute | solution.py:516
  45.3 5.2 %collective-permute-done.11.refs_17_ = f32[264,128]{1,0:T(8,128)S(1)} collective-permute-done((f32[264,128]{1,0:T(8,128)}, f32[264,128]{1,0:T(8,128)S(1)}, u32[]{:S(2)}, u32[]{:S(2)}) %collective-permute-start.11) | collective-permute-done | bytes 135200 | tf_op jit(solution)/shard_map/ppermute | solution.py:516
  50.5 3.7 %collective-permute-done.12.refs_18_ = f32[264,128]{1,0:T(8,128)S(1)} collective-permute-done((f32[264,128]{1,0:T(8,128)}, f32[264,128]{1,0:T(8,128)S(1)}, u32[]{:S(2)}, u32[]{:S(2)}) %collective-permute-start.12) | collective-permute-done | bytes 135200 | tf_op jit(solution)/shard_map/ppermute | solution.py:516
  54.2 5.2 %one_head.1 = (f32[256,128]{1,0:T(8,128)S(1)}, f32[256,128]{1,0:T(8,128)S(1)}, f32[256,128]{1,0:T(8,128)S(1)}, f32[256,128]{1,0:T(8,128)S(1)}, f32[256,128]{1,0:...) custom-call(s32[4,12]{1,0:T(4,128)S(1)} %copy-done.4, ...), custom_call_target="tpu_custom_call" | custom-call | tf_op jit(solution)/shard_map/one_head/pallas_call | solution.py:558
  59.4 2.2 %collective-permute-start.15 = (f32[256,128]{1,0:T(8,128)S(1)}, f32[256,128]{1,0:T(8,128)S(1)}, u32[]{:S(2)}, u32[]{:S(2)}) collective-permute-start(f32[256,128]{1,0:T(8,128)S(1)} %get-tuple-element.51), channel_id=1, source_target_pairs={{0,15},{1,14},{2,13},{3,12},{4,11},{5,10},{6,9},{7,8},{8,7},{9,6},... | collective-permute-start | bytes 393224 | tf_op jit(solution)/shard_map/ppermute | solution.py:516
  61.6 2.5 %collective-permute-start.16 = (f32[256,128]{1,0:T(8,128)S(1)}, f32[256,128]{1,0:T(8,128)S(1)}, u32[]{:S(2)}, u32[]{:S(2)}) collective-permute-start(f32[256,128]{1,0:T(8,128)S(1)} %get-tuple-element.52), channel_id=1, source_target_pairs={{0,1},{1,0},{2,3},{3,2},{4,5},{5,4},{6,7},{7,6},{8,9},{9,8},{10,11... | collective-permute-start | bytes 393224 | tf_op jit(solution)/shard_map/ppermute | solution.py:516
  64.3 1.6 %collective-permute-start.19 = (f32[256,128]{1,0:T(8,128)S(1)}, f32[256,128]{1,0:T(8,128)S(1)}, u32[]{:S(2)}, u32[]{:S(2)}) collective-permute-start(f32[256,128]{1,0:T(8,128)S(1)} %get-tuple-element.55), channel_id=1, source_target_pairs={{0,5},{1,4},{2,7},{3,6},{4,1},{5,0},{6,3},{7,2},{8,13},{9,12},{10,... | collective-permute-start | bytes 393224 | tf_op jit(solution)/shard_map/ppermute | solution.py:516
  65.9 2.0 %collective-permute-done.15.refs_1_ = f32[256,128]{1,0:T(8,128)S(1)} collective-permute-done((f32[256,128]{1,0:T(8,128)S(1)}, f32[256,128]{1,0:T(8,128)S(1)}, u32[]{:S(2)}, u32[]{:S(2)}) %collective-permute-start.15) | collective-permute-done | bytes 131104 | tf_op jit(solution)/shard_map/ppermute | solution.py:516
  67.9 2.3 %collective-permute-start.20 = (f32[256,128]{1,0:T(8,128)S(1)}, f32[256,128]{1,0:T(8,128)S(1)}, u32[]{:S(2)}, u32[]{:S(2)}) collective-permute-start(f32[256,128]{1,0:T(8,128)S(1)} %get-tuple-element.56), channel_id=1, source_target_pairs={{0,7},{1,6},{2,5},{3,4},{4,3},{5,2},{6,1},{7,0},{8,15},{9,14},{10,... | collective-permute-start | bytes 393224 | tf_op jit(solution)/shard_map/ppermute | solution.py:516
  70.1 2.5 %collective-permute-start.21 = (f32[256,128]{1,0:T(8,128)S(1)}, f32[256,128]{1,0:T(8,128)S(1)}, u32[]{:S(2)}, u32[]{:S(2)}) collective-permute-start(f32[256,128]{1,0:T(8,128)S(1)} %get-tuple-element.57), channel_id=1, source_target_pairs={{0,10},{1,11},{2,8},{3,9},{4,14},{5,15},{6,12},{7,13},{8,2},{9,3},... | collective-permute-start | bytes 393224 | tf_op jit(solution)/shard_map/ppermute | solution.py:516
  72.6 1.1 %collective-permute-start.22 = (f32[256,128]{1,0:T(8,128)S(1)}, f32[256,128]{1,0:T(8,128)S(1)}, u32[]{:S(2)}, u32[]{:S(2)}) collective-permute-start(f32[256,128]{1,0:T(8,128)S(1)} %get-tuple-element.58), channel_id=1, source_target_pairs={{0,9},{1,8},{2,11},{3,10},{4,13},{5,12},{6,15},{7,14},{8,1},{9,0},... | collective-permute-start | bytes 393224 | tf_op jit(solution)/shard_map/ppermute | solution.py:516
  73.8 1.7 %collective-permute-done.18.refs_4_ = f32[256,128]{1,0:T(8,128)S(1)} collective-permute-done((f32[256,128]{1,0:T(8,128)S(1)}, f32[256,128]{1,0:T(8,128)S(1)}, u32[]{:S(2)}, u32[]{:S(2)}) %collective-permute-start.18) | collective-permute-done | bytes 131104 | tf_op jit(solution)/shard_map/ppermute | solution.py:516
  75.5 3.5 %collective-permute-start.23 = (f32[256,128]{1,0:T(8,128)S(1)}, f32[256,128]{1,0:T(8,128)S(1)}, u32[]{:S(2)}, u32[]{:S(2)}) collective-permute-start(f32[256,128]{1,0:T(8,128)S(1)} %get-tuple-element.59), channel_id=1, source_target_pairs={{0,11},{1,10},{2,9},{3,8},{4,15},{5,14},{6,13},{7,12},{8,3},{9,2},... | collective-permute-start | bytes 393224 | tf_op jit(solution)/shard_map/ppermute | solution.py:516
  79.1 7.2 %collective-permute-start.25 = (f32[256,128]{1,0:T(8,128)S(1)}, f32[256,128]{1,0:T(8,128)S(1)}, u32[]{:S(2)}, u32[]{:S(2)}) collective-permute-start(f32[256,128]{1,0:T(8,128)S(1)} %get-tuple-element.61), channel_id=1, source_target_pairs={{0,14},{1,15},{2,12},{3,13},{4,10},{5,11},{6,8},{7,9},{8,6},{9,7},... | collective-permute-start | bytes 393224 | tf_op jit(solution)/shard_map/ppermute | solution.py:516
  86.3 7.0 %collective-permute-done.21.refs_7_ = f32[256,128]{1,0:T(8,128)S(1)} collective-permute-done((f32[256,128]{1,0:T(8,128)S(1)}, f32[256,128]{1,0:T(8,128)S(1)}, u32[]{:S(2)}, u32[]{:S(2)}) %collective-permute-start.21) | collective-permute-done | bytes 131104 | tf_op jit(solution)/shard_map/ppermute | solution.py:516
  93.3 2.6 %collective-permute-start.27 = (f32[256,128]{1,0:T(8,128)S(1)}, f32[256,128]{1,0:T(8,128)S(1)}, u32[]{:S(2)}, u32[]{:S(2)}) collective-permute-start(f32[256,128]{1,0:T(8,128)S(1)} %get-tuple-element.63), channel_id=1, source_target_pairs={{0,2},{1,3},{2,0},{3,1},{4,6},{5,7},{6,4},{7,5},{8,10},{9,11},{10,... | collective-permute-start | bytes 393224 | tf_op jit(solution)/shard_map/ppermute | solution.py:516
  95.9 1.5 %collective-permute-start.28 = (f32[256,128]{1,0:T(8,128)S(1)}, f32[256,128]{1,0:T(8,128)S(1)}, u32[]{:S(2)}, u32[]{:S(2)}) collective-permute-start(f32[256,128]{1,0:T(8,128)S(1)} %get-tuple-element.64), channel_id=1, source_target_pairs={{0,8},{1,9},{2,10},{3,11},{4,12},{5,13},{6,14},{7,15},{8,0},{9,1},... | collective-permute-start | bytes 393224 | tf_op jit(solution)/shard_map/ppermute | solution.py:516
  97.5 1.4 %collective-permute-start.29 = (f32[256,128]{1,0:T(8,128)S(1)}, f32[256,128]{1,0:T(8,128)S(1)}, u32[]{:S(2)}, u32[]{:S(2)}) collective-permute-start(f32[256,128]{1,0:T(8,128)S(1)} %get-tuple-element.65), channel_id=1, source_target_pairs={{0,3},{1,2},{2,1},{3,0},{4,7},{5,6},{6,5},{7,4},{8,11},{9,10},{10,... | collective-permute-start | bytes 393224 | tf_op jit(solution)/shard_map/ppermute | solution.py:516
  99.0 4.1 %collective-permute-done.26.refs_12_ = f32[256,128]{1,0:T(8,128)S(1)} collective-permute-done((f32[256,128]{1,0:T(8,128)S(1)}, f32[256,128]{1,0:T(8,128)S(1)}, u32[]{:S(2)}, u32[]{:S(2)}) %collective-permute-start.26) | collective-permute-done | bytes 131104 | tf_op jit(solution)/shard_map/ppermute | solution.py:516
  103.1 3.4 %collective-permute-done.27.refs_13_ = f32[256,128]{1,0:T(8,128)S(1)} collective-permute-done((f32[256,128]{1,0:T(8,128)S(1)}, f32[256,128]{1,0:T(8,128)S(1)}, u32[]{:S(2)}, u32[]{:S(2)}) %collective-permute-start.27) | collective-permute-done | bytes 131104 | tf_op jit(solution)/shard_map/ppermute | solution.py:516
  106.5 1.9 %unpack_heads.1 = (f32[2,64,1024]{2,1,0:T(8,128)}, f32[2,64,1024]{2,1,0:T(8,128)}, f32[2,64,1024]{2,1,0:T(8,128)}, f32[2,64,1024]{2,1,0:T(8,128)}) custom-call(f32[256,128]{1,0:T(8,128)S(1)} %get-tuple-element.50.refs_0_, f32[256,128]{1,0:T(8,128)S(1)} %collective-permute-done.15.refs_1_, f32[256,128]{1,0:T(8,128)S(1)} %collective-permute-done.16.refs_2_, ...), custom_call_target="tpu_custom_call" | custom-call | tf_op jit(solution)/shard_map/unpack_heads/pallas_call | solution.py:576
  (43 shorter events, 4.0 us)
Async XLA Ops:
  0.6 53.6 %copy-start.3 = (f32[2,64,1024]{2,1,0:T(8,128)S(1)}, f32[2,64,1024]{2,1,0:T(8,128)}, u32[]{:S(2)}) copy-start(f32[2,64,1024]{2,1,0:T(8,128)} %refs_5_.3) | copy-start | bytes 1572868
  0.6 53.6 %copy-start.2 = (f32[2,64,1024]{2,1,0:T(8,128)S(1)}, f32[2,64,1024]{2,1,0:T(8,128)}, u32[]{:S(2)}) copy-start(f32[2,64,1024]{2,1,0:T(8,128)} %refs_4_.3) | copy-start | bytes 1572868
  4.0 9.8 %collective-permute-start = (f32[264,128]{1,0:T(8,128)}, f32[264,128]{1,0:T(8,128)S(1)}, u32[]{:S(2)}, u32[]{:S(2)}) collective-permute-start(f32[264,128]{1,0:T(8,128)} %get-tuple-element.35), channel_id=1, source_target_pairs={{0,15},{1,14},{2,13},{3,12},{4,11},{5,10},{6,9},{7,8},{8,7},{9,6},... | collective-permute-start | bytes 405512 | tf_op jit(solution)/shard_map/ppermute | solution.py:516
  9.5 8.8 %collective-permute-start.1 = (f32[264,128]{1,0:T(8,128)}, f32[264,128]{1,0:T(8,128)S(1)}, u32[]{:S(2)}, u32[]{:S(2)}) collective-permute-start(f32[264,128]{1,0:T(8,128)} %get-tuple-element.36), channel_id=1, source_target_pairs={{0,1},{1,0},{2,3},{3,2},{4,5},{5,4},{6,7},{7,6},{8,9},{9,8},{10,11... | collective-permute-start | bytes 405512 | tf_op jit(solution)/shard_map/ppermute | solution.py:516
  9.5 9.6 %collective-permute-start.2 = (f32[264,128]{1,0:T(8,128)}, f32[264,128]{1,0:T(8,128)S(1)}, u32[]{:S(2)}, u32[]{:S(2)}) collective-permute-start(f32[264,128]{1,0:T(8,128)} %get-tuple-element.37), channel_id=1, source_target_pairs={{0,4},{1,5},{2,6},{3,7},{4,0},{5,1},{6,2},{7,3},{8,12},{9,13},{10,... | collective-permute-start | bytes 405512 | tf_op jit(solution)/shard_map/ppermute | solution.py:516
  10.1 12.6 %collective-permute-start.3 = (f32[264,128]{1,0:T(8,128)}, f32[264,128]{1,0:T(8,128)S(1)}, u32[]{:S(2)}, u32[]{:S(2)}) collective-permute-start(f32[264,128]{1,0:T(8,128)} %get-tuple-element.38), channel_id=1, source_target_pairs={{0,6},{1,7},{2,4},{3,5},{4,2},{5,3},{6,0},{7,1},{8,14},{9,15},{10,... | collective-permute-start | bytes 405512 | tf_op jit(solution)/shard_map/ppermute | solution.py:516
  10.4 14.3 %collective-permute-start.4 = (f32[264,128]{1,0:T(8,128)}, f32[264,128]{1,0:T(8,128)S(1)}, u32[]{:S(2)}, u32[]{:S(2)}) collective-permute-start(f32[264,128]{1,0:T(8,128)} %get-tuple-element.39), channel_id=1, source_target_pairs={{0,5},{1,4},{2,7},{3,6},{4,1},{5,0},{6,3},{7,2},{8,13},{9,12},{10,... | collective-permute-start | bytes 405512 | tf_op jit(solution)/shard_map/ppermute | solution.py:516
  13.8 12.3 %collective-permute-start.5 = (f32[264,128]{1,0:T(8,128)}, f32[264,128]{1,0:T(8,128)S(1)}, u32[]{:S(2)}, u32[]{:S(2)}) collective-permute-start(f32[264,128]{1,0:T(8,128)} %get-tuple-element.40), channel_id=1, source_target_pairs={{0,7},{1,6},{2,5},{3,4},{4,3},{5,2},{6,1},{7,0},{8,15},{9,14},{10,... | collective-permute-start | bytes 405512 | tf_op jit(solution)/shard_map/ppermute | solution.py:516
  18.3 21.5 %collective-permute-start.6 = (f32[264,128]{1,0:T(8,128)}, f32[264,128]{1,0:T(8,128)S(1)}, u32[]{:S(2)}, u32[]{:S(2)}) collective-permute-start(f32[264,128]{1,0:T(8,128)} %get-tuple-element.41), channel_id=1, source_target_pairs={{0,10},{1,11},{2,8},{3,9},{4,14},{5,15},{6,12},{7,13},{8,2},{9,3},... | collective-permute-start | bytes 405512 | tf_op jit(solution)/shard_map/ppermute | solution.py:516
  19.1 20.7 %collective-permute-start.7 = (f32[264,128]{1,0:T(8,128)}, f32[264,128]{1,0:T(8,128)S(1)}, u32[]{:S(2)}, u32[]{:S(2)}) collective-permute-start(f32[264,128]{1,0:T(8,128)} %get-tuple-element.42), channel_id=1, source_target_pairs={{0,9},{1,8},{2,11},{3,10},{4,13},{5,12},{6,15},{7,14},{8,1},{9,0},... | collective-permute-start | bytes 405512 | tf_op jit(solution)/shard_map/ppermute | solution.py:516
  22.7 20.6 %collective-permute-start.8 = (f32[264,128]{1,0:T(8,128)}, f32[264,128]{1,0:T(8,128)S(1)}, u32[]{:S(2)}, u32[]{:S(2)}) collective-permute-start(f32[264,128]{1,0:T(8,128)} %get-tuple-element.43), channel_id=1, source_target_pairs={{0,11},{1,10},{2,9},{3,8},{4,15},{5,14},{6,13},{7,12},{8,3},{9,2},... | collective-permute-start | bytes 405512 | tf_op jit(solution)/shard_map/ppermute | solution.py:516
  24.7 19.1 %collective-permute-start.9 = (f32[264,128]{1,0:T(8,128)}, f32[264,128]{1,0:T(8,128)S(1)}, u32[]{:S(2)}, u32[]{:S(2)}) collective-permute-start(f32[264,128]{1,0:T(8,128)} %get-tuple-element.44), channel_id=1, source_target_pairs={{0,12},{1,13},{2,14},{3,15},{4,8},{5,9},{6,10},{7,11},{8,4},{9,5},... | collective-permute-start | bytes 405512 | tf_op jit(solution)/shard_map/ppermute | solution.py:516
  26.1 19.2 %collective-permute-start.10 = (f32[264,128]{1,0:T(8,128)}, f32[264,128]{1,0:T(8,128)S(1)}, u32[]{:S(2)}, u32[]{:S(2)}) collective-permute-start(f32[264,128]{1,0:T(8,128)} %get-tuple-element.45), channel_id=1, source_target_pairs={{0,14},{1,15},{2,12},{3,13},{4,10},{5,11},{6,8},{7,9},{8,6},{9,7},... | collective-permute-start | bytes 405512 | tf_op jit(solution)/shard_map/ppermute | solution.py:516
  39.8 10.8 %collective-permute-start.11 = (f32[264,128]{1,0:T(8,128)}, f32[264,128]{1,0:T(8,128)S(1)}, u32[]{:S(2)}, u32[]{:S(2)}) collective-permute-start(f32[264,128]{1,0:T(8,128)} %get-tuple-element.46), channel_id=1, source_target_pairs={{0,13},{1,12},{2,15},{3,14},{4,9},{5,8},{6,11},{7,10},{8,5},{9,4},... | collective-permute-start | bytes 405512 | tf_op jit(solution)/shard_map/ppermute | solution.py:516
  39.8 14.4 %collective-permute-start.12 = (f32[264,128]{1,0:T(8,128)}, f32[264,128]{1,0:T(8,128)S(1)}, u32[]{:S(2)}, u32[]{:S(2)}) collective-permute-start(f32[264,128]{1,0:T(8,128)} %get-tuple-element.47), channel_id=1, source_target_pairs={{0,2},{1,3},{2,0},{3,1},{4,6},{5,7},{6,4},{7,5},{8,10},{9,11},{10,... | collective-permute-start | bytes 405512 | tf_op jit(solution)/shard_map/ppermute | solution.py:516
  43.3 10.9 %collective-permute-start.13 = (f32[264,128]{1,0:T(8,128)}, f32[264,128]{1,0:T(8,128)S(1)}, u32[]{:S(2)}, u32[]{:S(2)}) collective-permute-start(f32[264,128]{1,0:T(8,128)} %get-tuple-element.48), channel_id=1, source_target_pairs={{0,8},{1,9},{2,10},{3,11},{4,12},{5,13},{6,14},{7,15},{8,0},{9,1},... | collective-permute-start | bytes 405512 | tf_op jit(solution)/shard_map/ppermute | solution.py:516
  43.8 10.4 %collective-permute-start.14 = (f32[264,128]{1,0:T(8,128)}, f32[264,128]{1,0:T(8,128)S(1)}, u32[]{:S(2)}, u32[]{:S(2)}) collective-permute-start(f32[264,128]{1,0:T(8,128)} %get-tuple-element.49), channel_id=1, source_target_pairs={{0,3},{1,2},{2,1},{3,0},{4,7},{5,6},{6,5},{7,4},{8,11},{9,10},{10,... | collective-permute-start | bytes 405512 | tf_op jit(solution)/shard_map/ppermute | solution.py:516
  59.4 8.4 %collective-permute-start.15 = (f32[256,128]{1,0:T(8,128)S(1)}, f32[256,128]{1,0:T(8,128)S(1)}, u32[]{:S(2)}, u32[]{:S(2)}) collective-permute-start(f32[256,128]{1,0:T(8,128)S(1)} %get-tuple-element.51), channel_id=1, source_target_pairs={{0,15},{1,14},{2,13},{3,12},{4,11},{5,10},{6,9},{7,8},{8,7},{9,6},... | collective-permute-start | bytes 393224 | tf_op jit(solution)/shard_map/ppermute | solution.py:516
  61.6 8.5 %collective-permute-start.16 = (f32[256,128]{1,0:T(8,128)S(1)}, f32[256,128]{1,0:T(8,128)S(1)}, u32[]{:S(2)}, u32[]{:S(2)}) collective-permute-start(f32[256,128]{1,0:T(8,128)S(1)} %get-tuple-element.52), channel_id=1, source_target_pairs={{0,1},{1,0},{2,3},{3,2},{4,5},{5,4},{6,7},{7,6},{8,9},{9,8},{10,11... | collective-permute-start | bytes 393224 | tf_op jit(solution)/shard_map/ppermute | solution.py:516
  64.1 8.5 %collective-permute-start.17 = (f32[256,128]{1,0:T(8,128)S(1)}, f32[256,128]{1,0:T(8,128)S(1)}, u32[]{:S(2)}, u32[]{:S(2)}) collective-permute-start(f32[256,128]{1,0:T(8,128)S(1)} %get-tuple-element.53), channel_id=1, source_target_pairs={{0,4},{1,5},{2,6},{3,7},{4,0},{5,1},{6,2},{7,3},{8,12},{9,13},{10,... | collective-permute-start | bytes 393224 | tf_op jit(solution)/shard_map/ppermute | solution.py:516
  64.3 11.2 %collective-permute-start.18 = (f32[256,128]{1,0:T(8,128)S(1)}, f32[256,128]{1,0:T(8,128)S(1)}, u32[]{:S(2)}, u32[]{:S(2)}) collective-permute-start(f32[256,128]{1,0:T(8,128)S(1)} %get-tuple-element.54), channel_id=1, source_target_pairs={{0,6},{1,7},{2,4},{3,5},{4,2},{5,3},{6,0},{7,1},{8,14},{9,15},{10,... | collective-permute-start | bytes 393224 | tf_op jit(solution)/shard_map/ppermute | solution.py:516
  64.3 14.8 %collective-permute-start.19 = (f32[256,128]{1,0:T(8,128)S(1)}, f32[256,128]{1,0:T(8,128)S(1)}, u32[]{:S(2)}, u32[]{:S(2)}) collective-permute-start(f32[256,128]{1,0:T(8,128)S(1)} %get-tuple-element.55), channel_id=1, source_target_pairs={{0,5},{1,4},{2,7},{3,6},{4,1},{5,0},{6,3},{7,2},{8,13},{9,12},{10,... | collective-permute-start | bytes 393224 | tf_op jit(solution)/shard_map/ppermute | solution.py:516
  67.9 11.2 %collective-permute-start.20 = (f32[256,128]{1,0:T(8,128)S(1)}, f32[256,128]{1,0:T(8,128)S(1)}, u32[]{:S(2)}, u32[]{:S(2)}) collective-permute-start(f32[256,128]{1,0:T(8,128)S(1)} %get-tuple-element.56), channel_id=1, source_target_pairs={{0,7},{1,6},{2,5},{3,4},{4,3},{5,2},{6,1},{7,0},{8,15},{9,14},{10,... | collective-permute-start | bytes 393224 | tf_op jit(solution)/shard_map/ppermute | solution.py:516
  70.1 23.1 %collective-permute-start.21 = (f32[256,128]{1,0:T(8,128)S(1)}, f32[256,128]{1,0:T(8,128)S(1)}, u32[]{:S(2)}, u32[]{:S(2)}) collective-permute-start(f32[256,128]{1,0:T(8,128)S(1)} %get-tuple-element.57), channel_id=1, source_target_pairs={{0,10},{1,11},{2,8},{3,9},{4,14},{5,15},{6,12},{7,13},{8,2},{9,3},... | collective-permute-start | bytes 393224 | tf_op jit(solution)/shard_map/ppermute | solution.py:516
  72.6 20.6 %collective-permute-start.22 = (f32[256,128]{1,0:T(8,128)S(1)}, f32[256,128]{1,0:T(8,128)S(1)}, u32[]{:S(2)}, u32[]{:S(2)}) collective-permute-start(f32[256,128]{1,0:T(8,128)S(1)} %get-tuple-element.58), channel_id=1, source_target_pairs={{0,9},{1,8},{2,11},{3,10},{4,13},{5,12},{6,15},{7,14},{8,1},{9,0},... | collective-permute-start | bytes 393224 | tf_op jit(solution)/shard_map/ppermute | solution.py:516
  75.5 20.4 %collective-permute-start.23 = (f32[256,128]{1,0:T(8,128)S(1)}, f32[256,128]{1,0:T(8,128)S(1)}, u32[]{:S(2)}, u32[]{:S(2)}) collective-permute-start(f32[256,128]{1,0:T(8,128)S(1)} %get-tuple-element.59), channel_id=1, source_target_pairs={{0,11},{1,10},{2,9},{3,8},{4,15},{5,14},{6,13},{7,12},{8,3},{9,2},... | collective-permute-start | bytes 393224 | tf_op jit(solution)/shard_map/ppermute | solution.py:516
  79.1 18.4 %collective-permute-start.24 = (f32[256,128]{1,0:T(8,128)S(1)}, f32[256,128]{1,0:T(8,128)S(1)}, u32[]{:S(2)}, u32[]{:S(2)}) collective-permute-start(f32[256,128]{1,0:T(8,128)S(1)} %get-tuple-element.60), channel_id=1, source_target_pairs={{0,12},{1,13},{2,14},{3,15},{4,8},{5,9},{6,10},{7,11},{8,4},{9,5},... | collective-permute-start | bytes 393224 | tf_op jit(solution)/shard_map/ppermute | solution.py:516
  79.1 19.9 %collective-permute-start.25 = (f32[256,128]{1,0:T(8,128)S(1)}, f32[256,128]{1,0:T(8,128)S(1)}, u32[]{:S(2)}, u32[]{:S(2)}) collective-permute-start(f32[256,128]{1,0:T(8,128)S(1)} %get-tuple-element.61), channel_id=1, source_target_pairs={{0,14},{1,15},{2,12},{3,13},{4,10},{5,11},{6,8},{7,9},{8,6},{9,7},... | collective-permute-start | bytes 393224 | tf_op jit(solution)/shard_map/ppermute | solution.py:516
  93.3 9.8 %collective-permute-start.26 = (f32[256,128]{1,0:T(8,128)S(1)}, f32[256,128]{1,0:T(8,128)S(1)}, u32[]{:S(2)}, u32[]{:S(2)}) collective-permute-start(f32[256,128]{1,0:T(8,128)S(1)} %get-tuple-element.62), channel_id=1, source_target_pairs={{0,13},{1,12},{2,15},{3,14},{4,9},{5,8},{6,11},{7,10},{8,5},{9,4},... | collective-permute-start | bytes 393224 | tf_op jit(solution)/shard_map/ppermute | solution.py:516
  93.3 13.2 %collective-permute-start.27 = (f32[256,128]{1,0:T(8,128)S(1)}, f32[256,128]{1,0:T(8,128)S(1)}, u32[]{:S(2)}, u32[]{:S(2)}) collective-permute-start(f32[256,128]{1,0:T(8,128)S(1)} %get-tuple-element.63), channel_id=1, source_target_pairs={{0,2},{1,3},{2,0},{3,1},{4,6},{5,7},{6,4},{7,5},{8,10},{9,11},{10,... | collective-permute-start | bytes 393224 | tf_op jit(solution)/shard_map/ppermute | solution.py:516
  95.9 10.6 %collective-permute-start.28 = (f32[256,128]{1,0:T(8,128)S(1)}, f32[256,128]{1,0:T(8,128)S(1)}, u32[]{:S(2)}, u32[]{:S(2)}) collective-permute-start(f32[256,128]{1,0:T(8,128)S(1)} %get-tuple-element.64), channel_id=1, source_target_pairs={{0,8},{1,9},{2,10},{3,11},{4,12},{5,13},{6,14},{7,15},{8,0},{9,1},... | collective-permute-start | bytes 393224 | tf_op jit(solution)/shard_map/ppermute | solution.py:516
  97.5 9.0 %collective-permute-start.29 = (f32[256,128]{1,0:T(8,128)S(1)}, f32[256,128]{1,0:T(8,128)S(1)}, u32[]{:S(2)}, u32[]{:S(2)}) collective-permute-start(f32[256,128]{1,0:T(8,128)S(1)} %get-tuple-element.65), channel_id=1, source_target_pairs={{0,3},{1,2},{2,1},{3,0},{4,7},{5,6},{6,5},{7,4},{8,11},{9,10},{10,... | collective-permute-start | bytes 393224 | tf_op jit(solution)/shard_map/ppermute | solution.py:516
  (4 other events, 132.5 us)

commit v4 on v3

--- a/solution.py
+++ b/solution.py
@@ -185,13 +185,14 @@
 SIZE = LANES // 2
 INFO = 8
 OUTWARD = (
-    (0, 0), (3, 3), (0, 1), (1, 0), (1, 2), (1, 1), (1, 3), (2, 2),
-    (2, 1), (2, 3), (3, 0), (3, 2), (3, 1), (0, 2), (2, 0), (0, 3),
+    (0, 0), (2, 3), (1, 1), (1, 0), (0, 2), (0, 1), (0, 3), (3, 2),
+    (3, 1), (1, 2), (2, 1), (2, 0), (2, 2), (3, 3), (3, 0), (1, 3),
 )
 HOMEWARD = (
-    (0, 0), (3, 3), (0, 1), (1, 0), (1, 2), (1, 1), (1, 3), (2, 2),
-    (2, 1), (2, 3), (3, 0), (3, 2), (3, 1), (0, 2), (2, 0), (0, 3),
+    (0, 0), (2, 3), (1, 1), (1, 0), (0, 2), (0, 1), (0, 3), (3, 2),
+    (3, 1), (3, 3), (2, 0), (2, 2), (2, 1), (1, 2), (3, 0), (1, 3),
 )
+FIRST = 5
 HIDDEN = -1e30
 NN = ((1,), (0,))
 NT = ((1,), (1,))
@@ -269,8 +270,8 @@
 
 
 def pack_kernel(order, parts, window, lookback, *refs):
-    arrays, out_refs = refs[:4], refs[4 : 3 + H]
-    held, window_ref, lookback_ref, sems = refs[3 + H : 7 + H], *refs[7 + H :]
+    arrays, out_refs, refs = refs[:4], refs[4 : 4 + len(order)], refs[4 + len(order) :]
+    held, window_ref, lookback_ref, sems = refs[:4], *refs[4:]
     moves = [(window, window_ref), (lookback, lookback_ref)]
     moves += [(a.at[frame], b.at[frame]) for a, b in zip(arrays, held) for frame in range(2)]
     copies = fetch(moves, sems)
@@ -289,23 +290,26 @@
 
 
 def unpack_kernel(order, groups, parts, *refs):
-    in_refs, out_refs, held, sems = refs[:H], refs[H : H + 4], refs[H + 4 : H + 8], refs[H + 8]
-    rows = held[0].shape[1]
+    in_refs, out_refs, held, sems = refs[:H], refs[H : H + 4], refs[H + 4], refs[H + 5]
+    rows = held.shape[3]
+    pairs = [(frame, patch) for frame in range(groups) for patch in range(0, parts, 2)]
     copies = []
-    for number, ref in enumerate(held):
-        at = rows_of(number, rows)
-        for frame in range(groups):
-            for patch in range(0, parts, 2):
-                head = place((frame, patch), parts)
-                odd = jnp.full((rows, LANES), head % 2, jnp.int32) == 1
-                here = in_refs[order.index((frame, patch))][at]
-                there = in_refs[order.index((frame, patch + 1))][at]
-                first, second = interleave(jnp.where(odd, there, here), jnp.where(odd, here, there))
-                cols = columns_of(head)
-                ref[0, :, cols] = first
-                ref[1, :, cols] = second
-        copies.append(pltpu.make_async_copy(ref, out_refs[number], sems.at[number]))
-        copies[-1].start()
+    for n, (frame, patch) in enumerate(pairs):
+        head = place((frame, patch), parts)
+        odd = jnp.full((rows, LANES), head % 2, jnp.int32) == 1
+        for m, out_ref in enumerate(out_refs):
+            at = rows_of(m, rows)
+            here = in_refs[order.index((frame, patch))][at]
+            there = in_refs[order.index((frame, patch + 1))][at]
+            held[n, m, 0], held[n, m, 1] = interleave(
+                jnp.where(odd, there, here), jnp.where(odd, here, there)
+            )
+            copies.append(
+                pltpu.make_async_copy(
+                    held.at[n, m], out_ref.at[:, :, columns_of(head)], sems.at[4 * n + m]
+                )
+            )
+            copies[-1].start()
     for copy in copies:
         copy.wait()
 
@@ -546,15 +550,20 @@
         return pltpu.CompilerParams(vmem_limit_bytes=mebibytes * 1024 * 1024)
 
     given = (window, lookback, queries, key_rows, value_rows, cotangent)
-    packed = pl.pallas_call(
-        lambda *refs: pack_kernel(order[1:], parts, *refs),
-        out_shape=blocks(H - 1, 4 * patches_here + INFO),
-        in_specs=[anywhere] * 6,
-        out_specs=[vmem] * (H - 1),
-        scratch_shapes=[held] * 4 + smem + [dma((10,))],
-        compiler_params=params(56),
-        name="pack_heads",
-    )(*given)
+
+    def pack(some, name):
+        return pl.pallas_call(
+            lambda *refs: pack_kernel(some, parts, *refs),
+            out_shape=blocks(len(some), 4 * patches_here + INFO),
+            in_specs=[anywhere] * 6,
+            out_specs=[vmem] * len(some),
+            scratch_shapes=[held] * 4 + smem + [dma((10,))],
+            compiler_params=params(56),
+            name=name,
+        )(*given)
+
+    packed = pack(order[1 : 1 + FIRST], "pack_heads")
+    packed = *packed, *pack(order[1 + FIRST :], "pack_rest")
     done = pl.pallas_call(
         lambda *refs: head_kernel(order, back, groups, parts, *refs),
         out_shape=blocks(H, 4 * patches_here),
@@ -578,7 +587,10 @@
         out_shape=[jax.ShapeDtypeStruct(queries.shape, jnp.float32)] * 4,
         in_specs=[vmem] * H,
         out_specs=[anywhere] * 4,
-        scratch_shapes=[held] * 4 + [dma((4,))],
+        scratch_shapes=[
+            pltpu.VMEM((H // 2, 4, 2, patches_here, LANES), jnp.float32),
+            dma((2 * H,)),
+        ],
         compiler_params=params(40),
         name="unpack_heads",
     )(done[0], *exchange(done[1:], back[1:], parts))

time: 109 us -> 106 us (0.972)
  waiting for transfers between devices: 39.2 us -> 35.3 us
  Pallas kernels: 10.3 us -> 12.1 us
  starting transfers between devices: 58.1 us -> 56.7 us
    ppermute x30, waiting for transfers between devices: 39.2 us -> 35.3 us  [exchange(): lax.ppermute(block, ('frame', 'patch'), [(i * patch_count + j, (i ^ frame...]
    pallas_call x1 -> x2, Pallas kernels: 3.27 us -> 5.3 us  [pack(): pl.pallas_call(lambda *refs: pack_kernel(some, parts, *refs), out_shape=b...]
    ppermute x30, starting transfers between devices: 58.1 us -> 56.7 us  [exchange(): lax.ppermute(block, ('frame', 'patch'), [(i * patch_count + j, (i ^ frame...]
  transfers between devices with their start and end apart: 30 -> 30, of which waited for: 13 -> 9; matrix products, arithmetic and copies ran while one was open for 0% -> 0% of each run, Pallas kernels for 0% -> 3%
where the time goes in v4:
time: 106 us; the launch traced here: 105 us
  starting transfers between devices  56.7 us (53%)
  waiting for transfers between devices  35.3 us (33%)
  Pallas kernels  12.1 us (11%)
    ppermute x30, starting transfers between devices, exchange(): lax.ppermute(block, ('frame', 'patch'), [(i * patch_count + j, (i ^ frame...  56.7 us
    ppermute x30, waiting for transfers between devices, exchange(): lax.ppermute(block, ('frame', 'patch'), [(i * patch_count + j, (i ^ frame...  35.3 us
    pallas_call x2, Pallas kernels, pack(): pl.pallas_call(lambda *refs: pack_kernel(some, parts, *refs), out_shape=b...  5.3 us
    pallas_call x1, Pallas kernels, shards_by_head(): pl.pallas_call(lambda *refs: head_kernel(order, back, groups, parts, *ref...  5.18 us
  transfers between devices with their start and end apart: 30, of which 9 were waited for; matrix products, arithmetic and copies ran while one was open for 0% of the time, Pallas kernels for 3%

profile of v4, /device:TPU:0, one launch (start us, length us, event | category | flops | bytes accessed | tf_op | source)
XLA Modules:
  0.0 105.0 jit_solution(2625408391212680699)
XLA Ops:
  0.6 2.5 %pack_heads.1 = (f32[264,128]{1,0:T(8,128)}, f32[264,128]{1,0:T(8,128)}, f32[264,128]{1,0:T(8,128)}, f32[264,128]{1,0:T(8,128)}, f32[264,128]{1,0:T(8,128)}) custom-call(s32[4,12]{1,0:T(4,128)} %refs_0_.5, s32[2]{0:T(128)} %refs_1_.5, f32[2,64,1024]{2,1,0:T(8,128)} %refs_2_.5, f32[2,64,1024]{2,1,0:T(8,128)} %refs_3_.5, f32[2,64,1024]{2,1,0:T(8,128)} %refs_4_.5, ...), custom_call_target="tpu_custom_call" | custom-call | tf_op jit(solution)/shard_map/pack_heads/pallas_call | solution.py:555
  3.1 6.1 %collective-permute-start = (f32[264,128]{1,0:T(8,128)}, f32[264,128]{1,0:T(8,128)S(1)}, u32[]{:S(2)}, u32[]{:S(2)}) collective-permute-start(f32[264,128]{1,0:T(8,128)} %get-tuple-element.35), channel_id=1, source_target_pairs={{0,11},{1,10},{2,9},{3,8},{4,15},{5,14},{6,13},{7,12},{8,3},{9,2},... | collective-permute-start | bytes 405512 | tf_op jit(solution)/shard_map/ppermute | solution.py:520
  9.2 0.9 collective-permute-start.3
  10.1 1.3 %collective-permute-start.4 = (f32[264,128]{1,0:T(8,128)}, f32[264,128]{1,0:T(8,128)S(1)}, u32[]{:S(2)}, u32[]{:S(2)}) collective-permute-start(f32[264,128]{1,0:T(8,128)} %get-tuple-element.39), channel_id=1, source_target_pairs={{0,1},{1,0},{2,3},{3,2},{4,5},{5,4},{6,7},{7,6},{8,9},{9,8},{10,11... | collective-permute-start | bytes 405512 | tf_op jit(solution)/shard_map/ppermute | solution.py:520
  11.4 2.8 %pack_rest.1 = (f32[264,128]{1,0:T(8,128)}, f32[264,128]{1,0:T(8,128)}, f32[264,128]{1,0:T(8,128)}, f32[264,128]{1,0:T(8,128)}, f32[264,128]{1,0:T(8,128)}, /*in...) custom-call(s32[4,12]{1,0:T(4,128)} %refs_0_.5, ...), custom_call_target="tpu_custom_call" | custom-call | tf_op jit(solution)/shard_map/pack_rest/pallas_call | solution.py:555
  14.3 3.4 %collective-permute-start.5 = (f32[264,128]{1,0:T(8,128)}, f32[264,128]{1,0:T(8,128)S(1)}, u32[]{:S(2)}, u32[]{:S(2)}) collective-permute-start(f32[264,128]{1,0:T(8,128)} %get-tuple-element.40), channel_id=1, source_target_pairs={{0,3},{1,2},{2,1},{3,0},{4,7},{5,6},{6,5},{7,4},{8,11},{9,10},{10,... | collective-permute-start | bytes 405512 | tf_op jit(solution)/shard_map/ppermute | solution.py:520
  17.6 3.7 %collective-permute-start.7 = (f32[264,128]{1,0:T(8,128)}, f32[264,128]{1,0:T(8,128)S(1)}, u32[]{:S(2)}, u32[]{:S(2)}) collective-permute-start(f32[264,128]{1,0:T(8,128)} %get-tuple-element.42), channel_id=1, source_target_pairs={{0,13},{1,12},{2,15},{3,14},{4,9},{5,8},{6,11},{7,10},{8,5},{9,4},... | collective-permute-start | bytes 405512 | tf_op jit(solution)/shard_map/ppermute | solution.py:520
  21.4 1.5 %collective-permute-done.3.refs_9_ = f32[264,128]{1,0:T(8,128)S(1)} collective-permute-done((f32[264,128]{1,0:T(8,128)}, f32[264,128]{1,0:T(8,128)S(1)}, u32[]{:S(2)}, u32[]{:S(2)}) %collective-permute-start.3) | collective-permute-done | bytes 135200 | tf_op jit(solution)/shard_map/ppermute | solution.py:520
  22.9 1.7 %collective-permute-start.9 = (f32[264,128]{1,0:T(8,128)}, f32[264,128]{1,0:T(8,128)S(1)}, u32[]{:S(2)}, u32[]{:S(2)}) collective-permute-start(f32[264,128]{1,0:T(8,128)} %get-tuple-element.44), channel_id=1, source_target_pairs={{0,9},{1,8},{2,11},{3,10},{4,13},{5,12},{6,15},{7,14},{8,1},{9,0},... | collective-permute-start | bytes 405512 | tf_op jit(solution)/shard_map/ppermute | solution.py:520
  24.5 1.3 %collective-permute-done.5.refs_11_ = f32[264,128]{1,0:T(8,128)S(1)} collective-permute-done((f32[264,128]{1,0:T(8,128)}, f32[264,128]{1,0:T(8,128)S(1)}, u32[]{:S(2)}, u32[]{:S(2)}) %collective-permute-start.5) | collective-permute-done | bytes 135200 | tf_op jit(solution)/shard_map/ppermute | solution.py:520
  26.2 7.6 %collective-permute-done.6.refs_12_ = f32[264,128]{1,0:T(8,128)S(1)} collective-permute-done((f32[264,128]{1,0:T(8,128)}, f32[264,128]{1,0:T(8,128)S(1)}, u32[]{:S(2)}, u32[]{:S(2)}) %collective-permute-start.6) | collective-permute-done | bytes 135200 | tf_op jit(solution)/shard_map/ppermute | solution.py:520
  33.7 2.2 %collective-permute-start.11 = (f32[264,128]{1,0:T(8,128)}, f32[264,128]{1,0:T(8,128)S(1)}, u32[]{:S(2)}, u32[]{:S(2)}) collective-permute-start(f32[264,128]{1,0:T(8,128)} %get-tuple-element.46), channel_id=1, source_target_pairs={{0,10},{1,11},{2,8},{3,9},{4,14},{5,15},{6,12},{7,13},{8,2},{9,3},... | collective-permute-start | bytes 405512 | tf_op jit(solution)/shard_map/ppermute | solution.py:520
  35.9 3.1 %collective-permute-start.12 = (f32[264,128]{1,0:T(8,128)}, f32[264,128]{1,0:T(8,128)S(1)}, u32[]{:S(2)}, u32[]{:S(2)}) collective-permute-start(f32[264,128]{1,0:T(8,128)} %get-tuple-element.47), channel_id=1, source_target_pairs={{0,15},{1,14},{2,13},{3,12},{4,11},{5,10},{6,9},{7,8},{8,7},{9,6},... | collective-permute-start | bytes 405512 | tf_op jit(solution)/shard_map/ppermute | solution.py:520
  39.3 1.5 %collective-permute-start.14 = (f32[264,128]{1,0:T(8,128)}, f32[264,128]{1,0:T(8,128)S(1)}, u32[]{:S(2)}, u32[]{:S(2)}) collective-permute-start(f32[264,128]{1,0:T(8,128)} %get-tuple-element.49), channel_id=1, source_target_pairs={{0,7},{1,6},{2,5},{3,4},{4,3},{5,2},{6,1},{7,0},{8,15},{9,14},{10,... | collective-permute-start | bytes 405512 | tf_op jit(solution)/shard_map/ppermute | solution.py:520
  40.8 8.9 %collective-permute-done.11.refs_17_ = f32[264,128]{1,0:T(8,128)S(1)} collective-permute-done((f32[264,128]{1,0:T(8,128)}, f32[264,128]{1,0:T(8,128)S(1)}, u32[]{:S(2)}, u32[]{:S(2)}) %collective-permute-start.11) | collective-permute-done | bytes 135200 | tf_op jit(solution)/shard_map/ppermute | solution.py:520
  49.8 5.2 %one_head.1 = (f32[256,128]{1,0:T(8,128)S(1)}, f32[256,128]{1,0:T(8,128)S(1)}, f32[256,128]{1,0:T(8,128)S(1)}, f32[256,128]{1,0:T(8,128)S(1)}, f32[256,128]{1,0:...) custom-call(s32[4,12]{1,0:T(4,128)S(1)} %copy-done.4, ...), custom_call_target="tpu_custom_call" | custom-call | tf_op jit(solution)/shard_map/one_head/pallas_call | solution.py:567
  54.9 3.5 %collective-permute-start.15 = (f32[256,128]{1,0:T(8,128)S(1)}, f32[256,128]{1,0:T(8,128)S(1)}, u32[]{:S(2)}, u32[]{:S(2)}) collective-permute-start(f32[256,128]{1,0:T(8,128)S(1)} %get-tuple-element.51), channel_id=1, source_target_pairs={{0,11},{1,10},{2,9},{3,8},{4,15},{5,14},{6,13},{7,12},{8,3},{9,2},... | collective-permute-start | bytes 393224 | tf_op jit(solution)/shard_map/ppermute | solution.py:520
  58.4 4.0 %collective-permute-start.16 = (f32[256,128]{1,0:T(8,128)S(1)}, f32[256,128]{1,0:T(8,128)S(1)}, u32[]{:S(2)}, u32[]{:S(2)}) collective-permute-start(f32[256,128]{1,0:T(8,128)S(1)} %get-tuple-element.52), channel_id=1, source_target_pairs={{0,5},{1,4},{2,7},{3,6},{4,1},{5,0},{6,3},{7,2},{8,13},{9,12},{10,... | collective-permute-start | bytes 393224 | tf_op jit(solution)/shard_map/ppermute | solution.py:520
  62.4 0.8 collective-permute-start.17
  63.2 0.8 collective-permute-start.18
  64.0 2.1 %collective-permute-start.19 = (f32[256,128]{1,0:T(8,128)S(1)}, f32[256,128]{1,0:T(8,128)S(1)}, u32[]{:S(2)}, u32[]{:S(2)}) collective-permute-start(f32[256,128]{1,0:T(8,128)S(1)} %get-tuple-element.55), channel_id=1, source_target_pairs={{0,1},{1,0},{2,3},{3,2},{4,5},{5,4},{6,7},{7,6},{8,9},{9,8},{10,11... | collective-permute-start | bytes 393224 | tf_op jit(solution)/shard_map/ppermute | solution.py:520
  66.1 1.5 %collective-permute-start.20 = (f32[256,128]{1,0:T(8,128)S(1)}, f32[256,128]{1,0:T(8,128)S(1)}, u32[]{:S(2)}, u32[]{:S(2)}) collective-permute-start(f32[256,128]{1,0:T(8,128)S(1)} %get-tuple-element.56), channel_id=1, source_target_pairs={{0,3},{1,2},{2,1},{3,0},{4,7},{5,6},{6,5},{7,4},{8,11},{9,10},{10,... | collective-permute-start | bytes 393224 | tf_op jit(solution)/shard_map/ppermute | solution.py:520
  67.6 2.8 %collective-permute-start.21 = (f32[256,128]{1,0:T(8,128)S(1)}, f32[256,128]{1,0:T(8,128)S(1)}, u32[]{:S(2)}, u32[]{:S(2)}) collective-permute-start(f32[256,128]{1,0:T(8,128)S(1)} %get-tuple-element.57), channel_id=1, source_target_pairs={{0,14},{1,15},{2,12},{3,13},{4,10},{5,11},{6,8},{7,9},{8,6},{9,7},... | collective-permute-start | bytes 393224 | tf_op jit(solution)/shard_map/ppermute | solution.py:520
  70.4 0.7 collective-permute-start.22
  71.2 3.2 %collective-permute-done.18.refs_4_ = f32[256,128]{1,0:T(8,128)S(1)} collective-permute-done((f32[256,128]{1,0:T(8,128)S(1)}, f32[256,128]{1,0:T(8,128)S(1)}, u32[]{:S(2)}, u32[]{:S(2)}) %collective-permute-start.18) | collective-permute-done | bytes 131104 | tf_op jit(solution)/shard_map/ppermute | solution.py:520
  74.5 0.9 collective-permute-start.24
  75.6 8.7 %collective-permute-start.25 = (f32[256,128]{1,0:T(8,128)S(1)}, f32[256,128]{1,0:T(8,128)S(1)}, u32[]{:S(2)}, u32[]{:S(2)}) collective-permute-start(f32[256,128]{1,0:T(8,128)S(1)} %get-tuple-element.61), channel_id=1, source_target_pairs={{0,10},{1,11},{2,8},{3,9},{4,14},{5,15},{6,12},{7,13},{8,2},{9,3},... | collective-permute-start | bytes 393224 | tf_op jit(solution)/shard_map/ppermute | solution.py:520
  84.3 5.9 %collective-permute-done.21.refs_7_ = f32[256,128]{1,0:T(8,128)S(1)} collective-permute-done((f32[256,128]{1,0:T(8,128)S(1)}, f32[256,128]{1,0:T(8,128)S(1)}, u32[]{:S(2)}, u32[]{:S(2)}) %collective-permute-start.21) | collective-permute-done | bytes 131104 | tf_op jit(solution)/shard_map/ppermute | solution.py:520
  90.8 2.4 %collective-permute-start.27 = (f32[256,128]{1,0:T(8,128)S(1)}, f32[256,128]{1,0:T(8,128)S(1)}, u32[]{:S(2)}, u32[]{:S(2)}) collective-permute-start(f32[256,128]{1,0:T(8,128)S(1)} %get-tuple-element.63), channel_id=1, source_target_pairs={{0,6},{1,7},{2,4},{3,5},{4,2},{5,3},{6,0},{7,1},{8,14},{9,15},{10,... | collective-permute-start | bytes 393224 | tf_op jit(solution)/shard_map/ppermute | solution.py:520
  93.2 3.3 %collective-permute-start.29 = (f32[256,128]{1,0:T(8,128)S(1)}, f32[256,128]{1,0:T(8,128)S(1)}, u32[]{:S(2)}, u32[]{:S(2)}) collective-permute-start(f32[256,128]{1,0:T(8,128)S(1)} %get-tuple-element.65), channel_id=1, source_target_pairs={{0,7},{1,6},{2,5},{3,4},{4,3},{5,2},{6,1},{7,0},{8,15},{9,14},{10,... | collective-permute-start | bytes 393224 | tf_op jit(solution)/shard_map/ppermute | solution.py:520
  96.4 6.6 %collective-permute-done.25.refs_11_ = f32[256,128]{1,0:T(8,128)S(1)} collective-permute-done((f32[256,128]{1,0:T(8,128)S(1)}, f32[256,128]{1,0:T(8,128)S(1)}, u32[]{:S(2)}, u32[]{:S(2)}) %collective-permute-start.25) | collective-permute-done | bytes 131104 | tf_op jit(solution)/shard_map/ppermute | solution.py:520
  103.3 1.7 %unpack_heads.1 = (f32[2,64,1024]{2,1,0:T(8,128)}, f32[2,64,1024]{2,1,0:T(8,128)}, f32[2,64,1024]{2,1,0:T(8,128)}, f32[2,64,1024]{2,1,0:T(8,128)}) custom-call(f32[256,128]{1,0:T(8,128)S(1)} %get-tuple-element.50.refs_0_, f32[256,128]{1,0:T(8,128)S(1)} %collective-permute-done.15.refs_1_, f32[256,128]{1,0:T(8,128)S(1)} %collective-permute-done.16.refs_2_, ...), custom_call_target="tpu_custom_call" | custom-call | tf_op jit(solution)/shard_map/unpack_heads/pallas_call | solution.py:585
  (44 shorter events, 2.1 us)
Async XLA Ops:
  3.1 11.1 %collective-permute-start = (f32[264,128]{1,0:T(8,128)}, f32[264,128]{1,0:T(8,128)S(1)}, u32[]{:S(2)}, u32[]{:S(2)}) collective-permute-start(f32[264,128]{1,0:T(8,128)} %get-tuple-element.35), channel_id=1, source_target_pairs={{0,11},{1,10},{2,9},{3,8},{4,15},{5,14},{6,13},{7,12},{8,3},{9,2},... | collective-permute-start | bytes 405512 | tf_op jit(solution)/shard_map/ppermute | solution.py:520
  9.2 8.4 %collective-permute-start.1 = (f32[264,128]{1,0:T(8,128)}, f32[264,128]{1,0:T(8,128)S(1)}, u32[]{:S(2)}, u32[]{:S(2)}) collective-permute-start(f32[264,128]{1,0:T(8,128)} %get-tuple-element.36), channel_id=1, source_target_pairs={{0,5},{1,4},{2,7},{3,6},{4,1},{5,0},{6,3},{7,2},{8,13},{9,12},{10,... | collective-permute-start | bytes 405512 | tf_op jit(solution)/shard_map/ppermute | solution.py:520
  9.2 8.4 %collective-permute-start.2 = (f32[264,128]{1,0:T(8,128)}, f32[264,128]{1,0:T(8,128)S(1)}, u32[]{:S(2)}, u32[]{:S(2)}) collective-permute-start(f32[264,128]{1,0:T(8,128)} %get-tuple-element.37), channel_id=1, source_target_pairs={{0,4},{1,5},{2,6},{3,7},{4,0},{5,1},{6,2},{7,3},{8,12},{9,13},{10,... | collective-permute-start | bytes 405512 | tf_op jit(solution)/shard_map/ppermute | solution.py:520
  9.2 13.6 %collective-permute-start.3 = (f32[264,128]{1,0:T(8,128)}, f32[264,128]{1,0:T(8,128)S(1)}, u32[]{:S(2)}, u32[]{:S(2)}) collective-permute-start(f32[264,128]{1,0:T(8,128)} %get-tuple-element.38), channel_id=1, source_target_pairs={{0,2},{1,3},{2,0},{3,1},{4,6},{5,7},{6,4},{7,5},{8,10},{9,11},{10,... | collective-permute-start | bytes 405512 | tf_op jit(solution)/shard_map/ppermute | solution.py:520
  10.1 39.6 %copy-start.2 = (f32[2,64,1024]{2,1,0:T(8,128)S(1)}, f32[2,64,1024]{2,1,0:T(8,128)}, u32[]{:S(2)}) copy-start(f32[2,64,1024]{2,1,0:T(8,128)} %refs_4_.5) | copy-start | bytes 1572868
  10.1 39.6 %copy-start.3 = (f32[2,64,1024]{2,1,0:T(8,128)S(1)}, f32[2,64,1024]{2,1,0:T(8,128)}, u32[]{:S(2)}) copy-start(f32[2,64,1024]{2,1,0:T(8,128)} %refs_5_.5) | copy-start | bytes 1572868
  10.1 12.7 %collective-permute-start.4 = (f32[264,128]{1,0:T(8,128)}, f32[264,128]{1,0:T(8,128)S(1)}, u32[]{:S(2)}, u32[]{:S(2)}) collective-permute-start(f32[264,128]{1,0:T(8,128)} %get-tuple-element.39), channel_id=1, source_target_pairs={{0,1},{1,0},{2,3},{3,2},{4,5},{5,4},{6,7},{7,6},{8,9},{9,8},{10,11... | collective-permute-start | bytes 405512 | tf_op jit(solution)/shard_map/ppermute | solution.py:520
  14.3 11.5 %collective-permute-start.5 = (f32[264,128]{1,0:T(8,128)}, f32[264,128]{1,0:T(8,128)S(1)}, u32[]{:S(2)}, u32[]{:S(2)}) collective-permute-start(f32[264,128]{1,0:T(8,128)} %get-tuple-element.40), channel_id=1, source_target_pairs={{0,3},{1,2},{2,1},{3,0},{4,7},{5,6},{6,5},{7,4},{8,11},{9,10},{10,... | collective-permute-start | bytes 405512 | tf_op jit(solution)/shard_map/ppermute | solution.py:520
  17.6 16.1 %collective-permute-start.6 = (f32[264,128]{1,0:T(8,128)}, f32[264,128]{1,0:T(8,128)S(1)}, u32[]{:S(2)}, u32[]{:S(2)}) collective-permute-start(f32[264,128]{1,0:T(8,128)} %get-tuple-element.41), channel_id=1, source_target_pairs={{0,14},{1,15},{2,12},{3,13},{4,10},{5,11},{6,8},{7,9},{8,6},{9,7},... | collective-permute-start | bytes 405512 | tf_op jit(solution)/shard_map/ppermute | solution.py:520
  17.6 18.3 %collective-permute-start.7 = (f32[264,128]{1,0:T(8,128)}, f32[264,128]{1,0:T(8,128)S(1)}, u32[]{:S(2)}, u32[]{:S(2)}) collective-permute-start(f32[264,128]{1,0:T(8,128)} %get-tuple-element.42), channel_id=1, source_target_pairs={{0,13},{1,12},{2,15},{3,14},{4,9},{5,8},{6,11},{7,10},{8,5},{9,4},... | collective-permute-start | bytes 405512 | tf_op jit(solution)/shard_map/ppermute | solution.py:520
  22.9 16.2 %collective-permute-start.8 = (f32[264,128]{1,0:T(8,128)}, f32[264,128]{1,0:T(8,128)S(1)}, u32[]{:S(2)}, u32[]{:S(2)}) collective-permute-start(f32[264,128]{1,0:T(8,128)} %get-tuple-element.43), channel_id=1, source_target_pairs={{0,6},{1,7},{2,4},{3,5},{4,2},{5,3},{6,0},{7,1},{8,14},{9,15},{10,... | collective-permute-start | bytes 405512 | tf_op jit(solution)/shard_map/ppermute | solution.py:520
  22.9 16.4 %collective-permute-start.9 = (f32[264,128]{1,0:T(8,128)}, f32[264,128]{1,0:T(8,128)S(1)}, u32[]{:S(2)}, u32[]{:S(2)}) collective-permute-start(f32[264,128]{1,0:T(8,128)} %get-tuple-element.44), channel_id=1, source_target_pairs={{0,9},{1,8},{2,11},{3,10},{4,13},{5,12},{6,15},{7,14},{8,1},{9,0},... | collective-permute-start | bytes 405512 | tf_op jit(solution)/shard_map/ppermute | solution.py:520
  25.8 15.0 %collective-permute-start.10 = (f32[264,128]{1,0:T(8,128)}, f32[264,128]{1,0:T(8,128)S(1)}, u32[]{:S(2)}, u32[]{:S(2)}) collective-permute-start(f32[264,128]{1,0:T(8,128)} %get-tuple-element.45), channel_id=1, source_target_pairs={{0,8},{1,9},{2,10},{3,11},{4,12},{5,13},{6,14},{7,15},{8,0},{9,1},... | collective-permute-start | bytes 405512 | tf_op jit(solution)/shard_map/ppermute | solution.py:520
  33.7 16.0 %collective-permute-start.11 = (f32[264,128]{1,0:T(8,128)}, f32[264,128]{1,0:T(8,128)S(1)}, u32[]{:S(2)}, u32[]{:S(2)}) collective-permute-start(f32[264,128]{1,0:T(8,128)} %get-tuple-element.46), channel_id=1, source_target_pairs={{0,10},{1,11},{2,8},{3,9},{4,14},{5,15},{6,12},{7,13},{8,2},{9,3},... | collective-permute-start | bytes 405512 | tf_op jit(solution)/shard_map/ppermute | solution.py:520
  35.9 13.7 %collective-permute-start.12 = (f32[264,128]{1,0:T(8,128)}, f32[264,128]{1,0:T(8,128)S(1)}, u32[]{:S(2)}, u32[]{:S(2)}) collective-permute-start(f32[264,128]{1,0:T(8,128)} %get-tuple-element.47), channel_id=1, source_target_pairs={{0,15},{1,14},{2,13},{3,12},{4,11},{5,10},{6,9},{7,8},{8,7},{9,6},... | collective-permute-start | bytes 405512 | tf_op jit(solution)/shard_map/ppermute | solution.py:520
  39.0 10.7 %collective-permute-start.13 = (f32[264,128]{1,0:T(8,128)}, f32[264,128]{1,0:T(8,128)S(1)}, u32[]{:S(2)}, u32[]{:S(2)}) collective-permute-start(f32[264,128]{1,0:T(8,128)} %get-tuple-element.48), channel_id=1, source_target_pairs={{0,12},{1,13},{2,14},{3,15},{4,8},{5,9},{6,10},{7,11},{8,4},{9,5},... | collective-permute-start | bytes 405512 | tf_op jit(solution)/shard_map/ppermute | solution.py:520
  39.3 10.4 %collective-permute-start.14 = (f32[264,128]{1,0:T(8,128)}, f32[264,128]{1,0:T(8,128)S(1)}, u32[]{:S(2)}, u32[]{:S(2)}) collective-permute-start(f32[264,128]{1,0:T(8,128)} %get-tuple-element.49), channel_id=1, source_target_pairs={{0,7},{1,6},{2,5},{3,4},{4,3},{5,2},{6,1},{7,0},{8,15},{9,14},{10,... | collective-permute-start | bytes 405512 | tf_op jit(solution)/shard_map/ppermute | solution.py:520
  54.9 11.2 %collective-permute-start.15 = (f32[256,128]{1,0:T(8,128)S(1)}, f32[256,128]{1,0:T(8,128)S(1)}, u32[]{:S(2)}, u32[]{:S(2)}) collective-permute-start(f32[256,128]{1,0:T(8,128)S(1)} %get-tuple-element.51), channel_id=1, source_target_pairs={{0,11},{1,10},{2,9},{3,8},{4,15},{5,14},{6,13},{7,12},{8,3},{9,2},... | collective-permute-start | bytes 393224 | tf_op jit(solution)/shard_map/ppermute | solution.py:520
  58.4 9.2 %collective-permute-start.16 = (f32[256,128]{1,0:T(8,128)S(1)}, f32[256,128]{1,0:T(8,128)S(1)}, u32[]{:S(2)}, u32[]{:S(2)}) collective-permute-start(f32[256,128]{1,0:T(8,128)S(1)} %get-tuple-element.52), channel_id=1, source_target_pairs={{0,5},{1,4},{2,7},{3,6},{4,1},{5,0},{6,3},{7,2},{8,13},{9,12},{10,... | collective-permute-start | bytes 393224 | tf_op jit(solution)/shard_map/ppermute | solution.py:520
  62.4 8.0 %collective-permute-start.17 = (f32[256,128]{1,0:T(8,128)S(1)}, f32[256,128]{1,0:T(8,128)S(1)}, u32[]{:S(2)}, u32[]{:S(2)}) collective-permute-start(f32[256,128]{1,0:T(8,128)S(1)} %get-tuple-element.53), channel_id=1, source_target_pairs={{0,4},{1,5},{2,6},{3,7},{4,0},{5,1},{6,2},{7,3},{8,12},{9,13},{10,... | collective-permute-start | bytes 393224 | tf_op jit(solution)/shard_map/ppermute | solution.py:520
  63.2 11.1 %collective-permute-start.18 = (f32[256,128]{1,0:T(8,128)S(1)}, f32[256,128]{1,0:T(8,128)S(1)}, u32[]{:S(2)}, u32[]{:S(2)}) collective-permute-start(f32[256,128]{1,0:T(8,128)S(1)} %get-tuple-element.54), channel_id=1, source_target_pairs={{0,2},{1,3},{2,0},{3,1},{4,6},{5,7},{6,4},{7,5},{8,10},{9,11},{10,... | collective-permute-start | bytes 393224 | tf_op jit(solution)/shard_map/ppermute | solution.py:520
  64.0 10.5 %collective-permute-start.19 = (f32[256,128]{1,0:T(8,128)S(1)}, f32[256,128]{1,0:T(8,128)S(1)}, u32[]{:S(2)}, u32[]{:S(2)}) collective-permute-start(f32[256,128]{1,0:T(8,128)S(1)} %get-tuple-element.55), channel_id=1, source_target_pairs={{0,1},{1,0},{2,3},{3,2},{4,5},{5,4},{6,7},{7,6},{8,9},{9,8},{10,11... | collective-permute-start | bytes 393224 | tf_op jit(solution)/shard_map/ppermute | solution.py:520
  66.1 9.5 %collective-permute-start.20 = (f32[256,128]{1,0:T(8,128)S(1)}, f32[256,128]{1,0:T(8,128)S(1)}, u32[]{:S(2)}, u32[]{:S(2)}) collective-permute-start(f32[256,128]{1,0:T(8,128)S(1)} %get-tuple-element.56), channel_id=1, source_target_pairs={{0,3},{1,2},{2,1},{3,0},{4,7},{5,6},{6,5},{7,4},{8,11},{9,10},{10,... | collective-permute-start | bytes 393224 | tf_op jit(solution)/shard_map/ppermute | solution.py:520
  67.6 22.6 %collective-permute-start.21 = (f32[256,128]{1,0:T(8,128)S(1)}, f32[256,128]{1,0:T(8,128)S(1)}, u32[]{:S(2)}, u32[]{:S(2)}) collective-permute-start(f32[256,128]{1,0:T(8,128)S(1)} %get-tuple-element.57), channel_id=1, source_target_pairs={{0,14},{1,15},{2,12},{3,13},{4,10},{5,11},{6,8},{7,9},{8,6},{9,7},... | collective-permute-start | bytes 393224 | tf_op jit(solution)/shard_map/ppermute | solution.py:520
  70.4 20.3 %collective-permute-start.22 = (f32[256,128]{1,0:T(8,128)S(1)}, f32[256,128]{1,0:T(8,128)S(1)}, u32[]{:S(2)}, u32[]{:S(2)}) collective-permute-start(f32[256,128]{1,0:T(8,128)S(1)} %get-tuple-element.58), channel_id=1, source_target_pairs={{0,13},{1,12},{2,15},{3,14},{4,9},{5,8},{6,11},{7,10},{8,5},{9,4},... | collective-permute-start | bytes 393224 | tf_op jit(solution)/shard_map/ppermute | solution.py:520
  74.3 18.8 %collective-permute-start.23 = (f32[256,128]{1,0:T(8,128)S(1)}, f32[256,128]{1,0:T(8,128)S(1)}, u32[]{:S(2)}, u32[]{:S(2)}) collective-permute-start(f32[256,128]{1,0:T(8,128)S(1)} %get-tuple-element.59), channel_id=1, source_target_pairs={{0,15},{1,14},{2,13},{3,12},{4,11},{5,10},{6,9},{7,8},{8,7},{9,6},... | collective-permute-start | bytes 393224 | tf_op jit(solution)/shard_map/ppermute | solution.py:520
  74.5 18.6 %collective-permute-start.24 = (f32[256,128]{1,0:T(8,128)S(1)}, f32[256,128]{1,0:T(8,128)S(1)}, u32[]{:S(2)}, u32[]{:S(2)}) collective-permute-start(f32[256,128]{1,0:T(8,128)S(1)} %get-tuple-element.60), channel_id=1, source_target_pairs={{0,8},{1,9},{2,10},{3,11},{4,12},{5,13},{6,14},{7,15},{8,0},{9,1},... | collective-permute-start | bytes 393224 | tf_op jit(solution)/shard_map/ppermute | solution.py:520
  75.6 27.4 %collective-permute-start.25 = (f32[256,128]{1,0:T(8,128)S(1)}, f32[256,128]{1,0:T(8,128)S(1)}, u32[]{:S(2)}, u32[]{:S(2)}) collective-permute-start(f32[256,128]{1,0:T(8,128)S(1)} %get-tuple-element.61), channel_id=1, source_target_pairs={{0,10},{1,11},{2,8},{3,9},{4,14},{5,15},{6,12},{7,13},{8,2},{9,3},... | collective-permute-start | bytes 393224 | tf_op jit(solution)/shard_map/ppermute | solution.py:520
  90.2 12.8 %collective-permute-start.26 = (f32[256,128]{1,0:T(8,128)S(1)}, f32[256,128]{1,0:T(8,128)S(1)}, u32[]{:S(2)}, u32[]{:S(2)}) collective-permute-start(f32[256,128]{1,0:T(8,128)S(1)} %get-tuple-element.62), channel_id=1, source_target_pairs={{0,9},{1,8},{2,11},{3,10},{4,13},{5,12},{6,15},{7,14},{8,1},{9,0},... | collective-permute-start | bytes 393224 | tf_op jit(solution)/shard_map/ppermute | solution.py:520
  90.8 12.5 %collective-permute-start.27 = (f32[256,128]{1,0:T(8,128)S(1)}, f32[256,128]{1,0:T(8,128)S(1)}, u32[]{:S(2)}, u32[]{:S(2)}) collective-permute-start(f32[256,128]{1,0:T(8,128)S(1)} %get-tuple-element.63), channel_id=1, source_target_pairs={{0,6},{1,7},{2,4},{3,5},{4,2},{5,3},{6,0},{7,1},{8,14},{9,15},{10,... | collective-permute-start | bytes 393224 | tf_op jit(solution)/shard_map/ppermute | solution.py:520
  93.2 10.1 %collective-permute-start.28 = (f32[256,128]{1,0:T(8,128)S(1)}, f32[256,128]{1,0:T(8,128)S(1)}, u32[]{:S(2)}, u32[]{:S(2)}) collective-permute-start(f32[256,128]{1,0:T(8,128)S(1)} %get-tuple-element.64), channel_id=1, source_target_pairs={{0,12},{1,13},{2,14},{3,15},{4,8},{5,9},{6,10},{7,11},{8,4},{9,5},... | collective-permute-start | bytes 393224 | tf_op jit(solution)/shard_map/ppermute | solution.py:520
  93.2 10.1 %collective-permute-start.29 = (f32[256,128]{1,0:T(8,128)S(1)}, f32[256,128]{1,0:T(8,128)S(1)}, u32[]{:S(2)}, u32[]{:S(2)}) collective-permute-start(f32[256,128]{1,0:T(8,128)S(1)} %get-tuple-element.65), channel_id=1, source_target_pairs={{0,7},{1,6},{2,5},{3,4},{4,3},{5,2},{6,1},{7,0},{8,15},{9,14},{10,... | collective-permute-start | bytes 393224 | tf_op jit(solution)/shard_map/ppermute | solution.py:520
  (4 other events, 103.7 us)

commit v5 on v4

--- a/solution.py
+++ b/solution.py
@@ -185,12 +185,12 @@
 SIZE = LANES // 2
 INFO = 8
 OUTWARD = (
-    (0, 0), (2, 3), (1, 1), (1, 0), (0, 2), (0, 1), (0, 3), (3, 2),
-    (3, 1), (1, 2), (2, 1), (2, 0), (2, 2), (3, 3), (3, 0), (1, 3),
+    (0, 0), (0, 3), (3, 0), (2, 2), (2, 1), (1, 0), (1, 2), (1, 1),
+    (1, 3), (2, 0), (3, 2), (0, 1), (0, 2), (3, 1), (2, 3), (3, 3),
 )
 HOMEWARD = (
-    (0, 0), (2, 3), (1, 1), (1, 0), (0, 2), (0, 1), (0, 3), (3, 2),
-    (3, 1), (3, 3), (2, 0), (2, 2), (2, 1), (1, 2), (3, 0), (1, 3),
+    (0, 0), (0, 3), (3, 0), (2, 2), (2, 1), (1, 0), (1, 2), (1, 1),
+    (1, 3), (2, 0), (3, 2), (0, 1), (0, 2), (3, 1), (2, 3), (3, 3),
 )
 FIRST = 5
 HIDDEN = -1e30

time: 106 us -> 105 us (level)
  the two profiles are of different devices: /device:TPU:0 before, /device:TPU:19 now
where the time goes in v5:
time: 105 us
  waiting for transfers between devices  46.5 us (44%)
  starting transfers between devices  45.3 us (43%)
  Pallas kernels  12.2 us (12%)
    ppermute x30, waiting for transfers between devices, exchange(): lax.ppermute(block, ('frame', 'patch'), [(i * patch_count + j, (i ^ frame...  46.5 us
    ppermute x30, starting transfers between devices, exchange(): lax.ppermute(block, ('frame', 'patch'), [(i * patch_count + j, (i ^ frame...  45.3 us
    pallas_call x2, Pallas kernels, pack(): pl.pallas_call(lambda *refs: pack_kernel(some, parts, *refs), out_shape=b...  5.41 us
    pallas_call x1, Pallas kernels, shards_by_head(): pl.pallas_call(lambda *refs: head_kernel(order, back, groups, parts, *ref...  5.17 us
  transfers between devices with their start and end apart: 30, of which 12 were waited for; matrix products, arithmetic and copies ran while one was open for 0% of the time, Pallas kernels for 3%

profile of v5, /device:TPU:19, one launch (start us, length us, event | category | flops | bytes accessed | tf_op | source)
XLA Modules:
  0.0 104.8 jit_solution(1210810392434243458)
XLA Ops:
  0.6 2.5 %pack_heads.1 = (f32[264,128]{1,0:T(8,128)}, f32[264,128]{1,0:T(8,128)}, f32[264,128]{1,0:T(8,128)}, f32[264,128]{1,0:T(8,128)}, f32[264,128]{1,0:T(8,128)}) custom-call(s32[4,12]{1,0:T(4,128)} %refs_0_.5, s32[2]{0:T(128)} %refs_1_.5, f32[2,64,1024]{2,1,0:T(8,128)} %refs_2_.5, f32[2,64,1024]{2,1,0:T(8,128)} %refs_3_.5, f32[2,64,1024]{2,1,0:T(8,128)} %refs_4_.5, ...), custom_call_target="tpu_custom_call" | custom-call | tf_op jit(solution)/shard_map/pack_heads/pallas_call | solution.py:555
  3.4 2.1 %collective-permute-start.1 = (f32[264,128]{1,0:T(8,128)}, f32[264,128]{1,0:T(8,128)S(1)}, u32[]{:S(2)}, u32[]{:S(2)}) collective-permute-start(f32[264,128]{1,0:T(8,128)} %get-tuple-element.36), channel_id=1, source_target_pairs={{0,12},{1,13},{2,14},{3,15},{4,8},{5,9},{6,10},{7,11},{8,4},{9,5},... | collective-permute-start | bytes 405512 | tf_op jit(solution)/shard_map/ppermute | solution.py:520
  5.5 3.2 %collective-permute-start.2 = (f32[264,128]{1,0:T(8,128)}, f32[264,128]{1,0:T(8,128)S(1)}, u32[]{:S(2)}, u32[]{:S(2)}) collective-permute-start(f32[264,128]{1,0:T(8,128)} %get-tuple-element.37), channel_id=1, source_target_pairs={{0,10},{1,11},{2,8},{3,9},{4,14},{5,15},{6,12},{7,13},{8,2},{9,3},... | collective-permute-start | bytes 405512 | tf_op jit(solution)/shard_map/ppermute | solution.py:520
  9.0 2.9 %pack_rest.1 = (f32[264,128]{1,0:T(8,128)}, f32[264,128]{1,0:T(8,128)}, f32[264,128]{1,0:T(8,128)}, f32[264,128]{1,0:T(8,128)}, f32[264,128]{1,0:T(8,128)}, /*in...) custom-call(s32[4,12]{1,0:T(4,128)} %refs_0_.5, ...), custom_call_target="tpu_custom_call" | custom-call | tf_op jit(solution)/shard_map/pack_rest/pallas_call | solution.py:555
  12.0 1.4 %collective-permute-start.5 = (f32[264,128]{1,0:T(8,128)}, f32[264,128]{1,0:T(8,128)S(1)}, u32[]{:S(2)}, u32[]{:S(2)}) collective-permute-start(f32[264,128]{1,0:T(8,128)} %get-tuple-element.40), channel_id=1, source_target_pairs={{0,6},{1,7},{2,4},{3,5},{4,2},{5,3},{6,0},{7,1},{8,14},{9,15},{10,... | collective-permute-start | bytes 405512 | tf_op jit(solution)/shard_map/ppermute | solution.py:520
  13.3 2.2 %collective-permute-start.6 = (f32[264,128]{1,0:T(8,128)}, f32[264,128]{1,0:T(8,128)S(1)}, u32[]{:S(2)}, u32[]{:S(2)}) collective-permute-start(f32[264,128]{1,0:T(8,128)} %get-tuple-element.41), channel_id=1, source_target_pairs={{0,5},{1,4},{2,7},{3,6},{4,1},{5,0},{6,3},{7,2},{8,13},{9,12},{10,... | collective-permute-start | bytes 405512 | tf_op jit(solution)/shard_map/ppermute | solution.py:520
  15.5 4.1 %collective-permute-start.7 = (f32[264,128]{1,0:T(8,128)}, f32[264,128]{1,0:T(8,128)S(1)}, u32[]{:S(2)}, u32[]{:S(2)}) collective-permute-start(f32[264,128]{1,0:T(8,128)} %get-tuple-element.42), channel_id=1, source_target_pairs={{0,7},{1,6},{2,5},{3,4},{4,3},{5,2},{6,1},{7,0},{8,15},{9,14},{10,... | collective-permute-start | bytes 405512 | tf_op jit(solution)/shard_map/ppermute | solution.py:520
  19.6 1.2 %collective-permute-start.8 = (f32[264,128]{1,0:T(8,128)}, f32[264,128]{1,0:T(8,128)S(1)}, u32[]{:S(2)}, u32[]{:S(2)}) collective-permute-start(f32[264,128]{1,0:T(8,128)} %get-tuple-element.43), channel_id=1, source_target_pairs={{0,8},{1,9},{2,10},{3,11},{4,12},{5,13},{6,14},{7,15},{8,0},{9,1},... | collective-permute-start | bytes 405512 | tf_op jit(solution)/shard_map/ppermute | solution.py:520
  20.8 3.5 %collective-permute-start.9 = (f32[264,128]{1,0:T(8,128)}, f32[264,128]{1,0:T(8,128)S(1)}, u32[]{:S(2)}, u32[]{:S(2)}) collective-permute-start(f32[264,128]{1,0:T(8,128)} %get-tuple-element.44), channel_id=1, source_target_pairs={{0,14},{1,15},{2,12},{3,13},{4,10},{5,11},{6,8},{7,9},{8,6},{9,7},... | collective-permute-start | bytes 405512 | tf_op jit(solution)/shard_map/ppermute | solution.py:520
  24.3 0.9 collective-permute-start.10
  25.3 1.4 %collective-permute-start.11 = (f32[264,128]{1,0:T(8,128)}, f32[264,128]{1,0:T(8,128)S(1)}, u32[]{:S(2)}, u32[]{:S(2)}) collective-permute-start(f32[264,128]{1,0:T(8,128)} %get-tuple-element.46), channel_id=1, source_target_pairs={{0,2},{1,3},{2,0},{3,1},{4,6},{5,7},{6,4},{7,5},{8,10},{9,11},{10,... | collective-permute-start | bytes 405512 | tf_op jit(solution)/shard_map/ppermute | solution.py:520
  26.7 6.8 %collective-permute-done.7.refs_13_ = f32[264,128]{1,0:T(8,128)S(1)} collective-permute-done((f32[264,128]{1,0:T(8,128)}, f32[264,128]{1,0:T(8,128)S(1)}, u32[]{:S(2)}, u32[]{:S(2)}) %collective-permute-start.7) | collective-permute-done | bytes 135200 | tf_op jit(solution)/shard_map/ppermute | solution.py:520
  34.3 5.3 %collective-permute-start.14 = (f32[264,128]{1,0:T(8,128)}, f32[264,128]{1,0:T(8,128)S(1)}, u32[]{:S(2)}, u32[]{:S(2)}) collective-permute-start(f32[264,128]{1,0:T(8,128)} %get-tuple-element.49), channel_id=1, source_target_pairs={{0,15},{1,14},{2,13},{3,12},{4,11},{5,10},{6,9},{7,8},{8,7},{9,6},... | collective-permute-start | bytes 405512 | tf_op jit(solution)/shard_map/ppermute | solution.py:520
  39.6 7.3 %collective-permute-done.12.refs_18_ = f32[264,128]{1,0:T(8,128)S(1)} collective-permute-done((f32[264,128]{1,0:T(8,128)}, f32[264,128]{1,0:T(8,128)S(1)}, u32[]{:S(2)}, u32[]{:S(2)}) %collective-permute-start.12) | collective-permute-done | bytes 135200 | tf_op jit(solution)/shard_map/ppermute | solution.py:520
  46.9 3.0 %collective-permute-done.13.refs_19_ = f32[264,128]{1,0:T(8,128)S(1)} collective-permute-done((f32[264,128]{1,0:T(8,128)}, f32[264,128]{1,0:T(8,128)S(1)}, u32[]{:S(2)}, u32[]{:S(2)}) %collective-permute-start.13) | collective-permute-done | bytes 135200 | tf_op jit(solution)/shard_map/ppermute | solution.py:520
  49.8 3.4 %collective-permute-done.14.refs_20_ = f32[264,128]{1,0:T(8,128)S(1)} collective-permute-done((f32[264,128]{1,0:T(8,128)}, f32[264,128]{1,0:T(8,128)S(1)}, u32[]{:S(2)}, u32[]{:S(2)}) %collective-permute-start.14) | collective-permute-done | bytes 135200 | tf_op jit(solution)/shard_map/ppermute | solution.py:520
  53.3 5.2 %one_head.1 = (f32[256,128]{1,0:T(8,128)S(1)}, f32[256,128]{1,0:T(8,128)S(1)}, f32[256,128]{1,0:T(8,128)S(1)}, f32[256,128]{1,0:T(8,128)S(1)}, f32[256,128]{1,0:...) custom-call(s32[4,12]{1,0:T(4,128)S(1)} %copy-done.4, ...), custom_call_target="tpu_custom_call" | custom-call | tf_op jit(solution)/shard_map/one_head/pallas_call | solution.py:567
  59.3 3.0 %collective-permute-start.18 = (f32[256,128]{1,0:T(8,128)S(1)}, f32[256,128]{1,0:T(8,128)S(1)}, u32[]{:S(2)}, u32[]{:S(2)}) collective-permute-start(f32[256,128]{1,0:T(8,128)S(1)} %get-tuple-element.54), channel_id=1, source_target_pairs={{0,9},{1,8},{2,11},{3,10},{4,13},{5,12},{6,15},{7,14},{8,1},{9,0},... | collective-permute-start | bytes 393224 | tf_op jit(solution)/shard_map/ppermute | solution.py:520
  63.2 2.7 %collective-permute-done.15.refs_1_ = f32[256,128]{1,0:T(8,128)S(1)} collective-permute-done((f32[256,128]{1,0:T(8,128)S(1)}, f32[256,128]{1,0:T(8,128)S(1)}, u32[]{:S(2)}, u32[]{:S(2)}) %collective-permute-start.15) | collective-permute-done | bytes 131104 | tf_op jit(solution)/shard_map/ppermute | solution.py:520
  66.0 3.8 %collective-permute-done.16.refs_2_ = f32[256,128]{1,0:T(8,128)S(1)} collective-permute-done((f32[256,128]{1,0:T(8,128)S(1)}, f32[256,128]{1,0:T(8,128)S(1)}, u32[]{:S(2)}, u32[]{:S(2)}) %collective-permute-start.16) | collective-permute-done | bytes 131104 | tf_op jit(solution)/shard_map/ppermute | solution.py:520
  69.8 1.3 %collective-permute-start.22 = (f32[256,128]{1,0:T(8,128)S(1)}, f32[256,128]{1,0:T(8,128)S(1)}, u32[]{:S(2)}, u32[]{:S(2)}) collective-permute-start(f32[256,128]{1,0:T(8,128)S(1)} %get-tuple-element.58), channel_id=1, source_target_pairs={{0,7},{1,6},{2,5},{3,4},{4,3},{5,2},{6,1},{7,0},{8,15},{9,14},{10,... | collective-permute-start | bytes 393224 | tf_op jit(solution)/shard_map/ppermute | solution.py:520
  71.0 3.3 %collective-permute-start.24 = (f32[256,128]{1,0:T(8,128)S(1)}, f32[256,128]{1,0:T(8,128)S(1)}, u32[]{:S(2)}, u32[]{:S(2)}) collective-permute-start(f32[256,128]{1,0:T(8,128)S(1)} %get-tuple-element.60), channel_id=1, source_target_pairs={{0,14},{1,15},{2,12},{3,13},{4,10},{5,11},{6,8},{7,9},{8,6},{9,7},... | collective-permute-start | bytes 393224 | tf_op jit(solution)/shard_map/ppermute | solution.py:520
  74.3 2.6 %collective-permute-start.25 = (f32[256,128]{1,0:T(8,128)S(1)}, f32[256,128]{1,0:T(8,128)S(1)}, u32[]{:S(2)}, u32[]{:S(2)}) collective-permute-start(f32[256,128]{1,0:T(8,128)S(1)} %get-tuple-element.61), channel_id=1, source_target_pairs={{0,1},{1,0},{2,3},{3,2},{4,5},{5,4},{6,7},{7,6},{8,9},{9,8},{10,11... | collective-permute-start | bytes 393224 | tf_op jit(solution)/shard_map/ppermute | solution.py:520
  76.9 4.2 %collective-permute-start.26 = (f32[256,128]{1,0:T(8,128)S(1)}, f32[256,128]{1,0:T(8,128)S(1)}, u32[]{:S(2)}, u32[]{:S(2)}) collective-permute-start(f32[256,128]{1,0:T(8,128)S(1)} %get-tuple-element.62), channel_id=1, source_target_pairs={{0,2},{1,3},{2,0},{3,1},{4,6},{5,7},{6,4},{7,5},{8,10},{9,11},{10,... | collective-permute-start | bytes 393224 | tf_op jit(solution)/shard_map/ppermute | solution.py:520
  81.1 2.7 %collective-permute-done.22.refs_8_ = f32[256,128]{1,0:T(8,128)S(1)} collective-permute-done((f32[256,128]{1,0:T(8,128)S(1)}, f32[256,128]{1,0:T(8,128)S(1)}, u32[]{:S(2)}, u32[]{:S(2)}) %collective-permute-start.22) | collective-permute-done | bytes 131104 | tf_op jit(solution)/shard_map/ppermute | solution.py:520
  84.2 2.6 %collective-permute-done.24.refs_10_ = f32[256,128]{1,0:T(8,128)S(1)} collective-permute-done((f32[256,128]{1,0:T(8,128)S(1)}, f32[256,128]{1,0:T(8,128)S(1)}, u32[]{:S(2)}, u32[]{:S(2)}) %collective-permute-start.24) | collective-permute-done | bytes 131104 | tf_op jit(solution)/shard_map/ppermute | solution.py:520
  86.8 2.4 %collective-permute-start.29 = (f32[256,128]{1,0:T(8,128)S(1)}, f32[256,128]{1,0:T(8,128)S(1)}, u32[]{:S(2)}, u32[]{:S(2)}) collective-permute-start(f32[256,128]{1,0:T(8,128)S(1)} %get-tuple-element.65), channel_id=1, source_target_pairs={{0,15},{1,14},{2,13},{3,12},{4,11},{5,10},{6,9},{7,8},{8,7},{9,6},... | collective-permute-start | bytes 393224 | tf_op jit(solution)/shard_map/ppermute | solution.py:520
  89.1 3.2 %collective-permute-done.26.refs_12_ = f32[256,128]{1,0:T(8,128)S(1)} collective-permute-done((f32[256,128]{1,0:T(8,128)S(1)}, f32[256,128]{1,0:T(8,128)S(1)}, u32[]{:S(2)}, u32[]{:S(2)}) %collective-permute-start.26) | collective-permute-done | bytes 131104 | tf_op jit(solution)/shard_map/ppermute | solution.py:520
  92.4 4.7 %collective-permute-done.27.refs_13_ = f32[256,128]{1,0:T(8,128)S(1)} collective-permute-done((f32[256,128]{1,0:T(8,128)S(1)}, f32[256,128]{1,0:T(8,128)S(1)}, u32[]{:S(2)}, u32[]{:S(2)}) %collective-permute-start.27) | collective-permute-done | bytes 131104 | tf_op jit(solution)/shard_map/ppermute | solution.py:520
  97.1 3.2 %collective-permute-done.28.refs_14_ = f32[256,128]{1,0:T(8,128)S(1)} collective-permute-done((f32[256,128]{1,0:T(8,128)S(1)}, f32[256,128]{1,0:T(8,128)S(1)}, u32[]{:S(2)}, u32[]{:S(2)}) %collective-permute-start.28) | collective-permute-done | bytes 131104 | tf_op jit(solution)/shard_map/ppermute | solution.py:520
  100.3 2.8 %collective-permute-done.29.refs_15_ = f32[256,128]{1,0:T(8,128)S(1)} collective-permute-done((f32[256,128]{1,0:T(8,128)S(1)}, f32[256,128]{1,0:T(8,128)S(1)}, u32[]{:S(2)}, u32[]{:S(2)}) %collective-permute-start.29) | collective-permute-done | bytes 131104 | tf_op jit(solution)/shard_map/ppermute | solution.py:520
  103.1 1.7 %unpack_heads.1 = (f32[2,64,1024]{2,1,0:T(8,128)}, f32[2,64,1024]{2,1,0:T(8,128)}, f32[2,64,1024]{2,1,0:T(8,128)}, f32[2,64,1024]{2,1,0:T(8,128)}) custom-call(f32[256,128]{1,0:T(8,128)S(1)} %get-tuple-element.50.refs_0_, f32[256,128]{1,0:T(8,128)S(1)} %collective-permute-done.15.refs_1_, f32[256,128]{1,0:T(8,128)S(1)} %collective-permute-done.16.refs_2_, ...), custom_call_target="tpu_custom_call" | custom-call | tf_op jit(solution)/shard_map/unpack_heads/pallas_call | solution.py:585
  (44 shorter events, 3.5 us)
Async XLA Ops:
  3.1 8.8 %collective-permute-start = (f32[264,128]{1,0:T(8,128)}, f32[264,128]{1,0:T(8,128)S(1)}, u32[]{:S(2)}, u32[]{:S(2)}) collective-permute-start(f32[264,128]{1,0:T(8,128)} %get-tuple-element.35), channel_id=1, source_target_pairs={{0,3},{1,2},{2,1},{3,0},{4,7},{5,6},{6,5},{7,4},{8,11},{9,10},{10,... | collective-permute-start | bytes 405512 | tf_op jit(solution)/shard_map/ppermute | solution.py:520
  3.4 9.9 %collective-permute-start.1 = (f32[264,128]{1,0:T(8,128)}, f32[264,128]{1,0:T(8,128)S(1)}, u32[]{:S(2)}, u32[]{:S(2)}) collective-permute-start(f32[264,128]{1,0:T(8,128)} %get-tuple-element.36), channel_id=1, source_target_pairs={{0,12},{1,13},{2,14},{3,15},{4,8},{5,9},{6,10},{7,11},{8,4},{9,5},... | collective-permute-start | bytes 405512 | tf_op jit(solution)/shard_map/ppermute | solution.py:520
  5.5 10.0 %collective-permute-start.2 = (f32[264,128]{1,0:T(8,128)}, f32[264,128]{1,0:T(8,128)S(1)}, u32[]{:S(2)}, u32[]{:S(2)}) collective-permute-start(f32[264,128]{1,0:T(8,128)} %get-tuple-element.37), channel_id=1, source_target_pairs={{0,10},{1,11},{2,8},{3,9},{4,14},{5,15},{6,12},{7,13},{8,2},{9,3},... | collective-permute-start | bytes 405512 | tf_op jit(solution)/shard_map/ppermute | solution.py:520
  8.6 11.0 %collective-permute-start.3 = (f32[264,128]{1,0:T(8,128)}, f32[264,128]{1,0:T(8,128)S(1)}, u32[]{:S(2)}, u32[]{:S(2)}) collective-permute-start(f32[264,128]{1,0:T(8,128)} %get-tuple-element.38), channel_id=1, source_target_pairs={{0,9},{1,8},{2,11},{3,10},{4,13},{5,12},{6,15},{7,14},{8,1},{9,0},... | collective-permute-start | bytes 405512 | tf_op jit(solution)/shard_map/ppermute | solution.py:520
  8.8 44.4 %copy-start.2 = (f32[2,64,1024]{2,1,0:T(8,128)S(1)}, f32[2,64,1024]{2,1,0:T(8,128)}, u32[]{:S(2)}) copy-start(f32[2,64,1024]{2,1,0:T(8,128)} %refs_4_.5) | copy-start | bytes 1572868
  8.8 44.4 %copy-start.3 = (f32[2,64,1024]{2,1,0:T(8,128)S(1)}, f32[2,64,1024]{2,1,0:T(8,128)}, u32[]{:S(2)}) copy-start(f32[2,64,1024]{2,1,0:T(8,128)} %refs_5_.5) | copy-start | bytes 1572868
  8.8 12.0 %collective-permute-start.4 = (f32[264,128]{1,0:T(8,128)}, f32[264,128]{1,0:T(8,128)S(1)}, u32[]{:S(2)}, u32[]{:S(2)}) collective-permute-start(f32[264,128]{1,0:T(8,128)} %get-tuple-element.39), channel_id=1, source_target_pairs={{0,4},{1,5},{2,6},{3,7},{4,0},{5,1},{6,2},{7,3},{8,12},{9,13},{10,... | collective-permute-start | bytes 405512 | tf_op jit(solution)/shard_map/ppermute | solution.py:520
  12.0 12.4 %collective-permute-start.5 = (f32[264,128]{1,0:T(8,128)}, f32[264,128]{1,0:T(8,128)S(1)}, u32[]{:S(2)}, u32[]{:S(2)}) collective-permute-start(f32[264,128]{1,0:T(8,128)} %get-tuple-element.40), channel_id=1, source_target_pairs={{0,6},{1,7},{2,4},{3,5},{4,2},{5,3},{6,0},{7,1},{8,14},{9,15},{10,... | collective-permute-start | bytes 405512 | tf_op jit(solution)/shard_map/ppermute | solution.py:520
  13.3 11.9 %collective-permute-start.6 = (f32[264,128]{1,0:T(8,128)}, f32[264,128]{1,0:T(8,128)S(1)}, u32[]{:S(2)}, u32[]{:S(2)}) collective-permute-start(f32[264,128]{1,0:T(8,128)} %get-tuple-element.41), channel_id=1, source_target_pairs={{0,5},{1,4},{2,7},{3,6},{4,1},{5,0},{6,3},{7,2},{8,13},{9,12},{10,... | collective-permute-start | bytes 405512 | tf_op jit(solution)/shard_map/ppermute | solution.py:520
  15.5 18.0 %collective-permute-start.7 = (f32[264,128]{1,0:T(8,128)}, f32[264,128]{1,0:T(8,128)S(1)}, u32[]{:S(2)}, u32[]{:S(2)}) collective-permute-start(f32[264,128]{1,0:T(8,128)} %get-tuple-element.42), channel_id=1, source_target_pairs={{0,7},{1,6},{2,5},{3,4},{4,3},{5,2},{6,1},{7,0},{8,15},{9,14},{10,... | collective-permute-start | bytes 405512 | tf_op jit(solution)/shard_map/ppermute | solution.py:520
  19.6 13.9 %collective-permute-start.8 = (f32[264,128]{1,0:T(8,128)}, f32[264,128]{1,0:T(8,128)S(1)}, u32[]{:S(2)}, u32[]{:S(2)}) collective-permute-start(f32[264,128]{1,0:T(8,128)} %get-tuple-element.43), channel_id=1, source_target_pairs={{0,8},{1,9},{2,10},{3,11},{4,12},{5,13},{6,14},{7,15},{8,0},{9,1},... | collective-permute-start | bytes 405512 | tf_op jit(solution)/shard_map/ppermute | solution.py:520
  20.8 13.4 %collective-permute-start.9 = (f32[264,128]{1,0:T(8,128)}, f32[264,128]{1,0:T(8,128)S(1)}, u32[]{:S(2)}, u32[]{:S(2)}) collective-permute-start(f32[264,128]{1,0:T(8,128)} %get-tuple-element.44), channel_id=1, source_target_pairs={{0,14},{1,15},{2,12},{3,13},{4,10},{5,11},{6,8},{7,9},{8,6},{9,7},... | collective-permute-start | bytes 405512 | tf_op jit(solution)/shard_map/ppermute | solution.py:520
  24.3 15.2 %collective-permute-start.10 = (f32[264,128]{1,0:T(8,128)}, f32[264,128]{1,0:T(8,128)S(1)}, u32[]{:S(2)}, u32[]{:S(2)}) collective-permute-start(f32[264,128]{1,0:T(8,128)} %get-tuple-element.45), channel_id=1, source_target_pairs={{0,1},{1,0},{2,3},{3,2},{4,5},{5,4},{6,7},{7,6},{8,9},{9,8},{10,11... | collective-permute-start | bytes 405512 | tf_op jit(solution)/shard_map/ppermute | solution.py:520
  25.3 14.3 %collective-permute-start.11 = (f32[264,128]{1,0:T(8,128)}, f32[264,128]{1,0:T(8,128)S(1)}, u32[]{:S(2)}, u32[]{:S(2)}) collective-permute-start(f32[264,128]{1,0:T(8,128)} %get-tuple-element.46), channel_id=1, source_target_pairs={{0,2},{1,3},{2,0},{3,1},{4,6},{5,7},{6,4},{7,5},{8,10},{9,11},{10,... | collective-permute-start | bytes 405512 | tf_op jit(solution)/shard_map/ppermute | solution.py:520
  33.5 13.4 %collective-permute-start.12 = (f32[264,128]{1,0:T(8,128)}, f32[264,128]{1,0:T(8,128)S(1)}, u32[]{:S(2)}, u32[]{:S(2)}) collective-permute-start(f32[264,128]{1,0:T(8,128)} %get-tuple-element.47), channel_id=1, source_target_pairs={{0,13},{1,12},{2,15},{3,14},{4,9},{5,8},{6,11},{7,10},{8,5},{9,4},... | collective-permute-start | bytes 405512 | tf_op jit(solution)/shard_map/ppermute | solution.py:520
  33.5 16.3 %collective-permute-start.13 = (f32[264,128]{1,0:T(8,128)}, f32[264,128]{1,0:T(8,128)S(1)}, u32[]{:S(2)}, u32[]{:S(2)}) collective-permute-start(f32[264,128]{1,0:T(8,128)} %get-tuple-element.48), channel_id=1, source_target_pairs={{0,11},{1,10},{2,9},{3,8},{4,15},{5,14},{6,13},{7,12},{8,3},{9,2},... | collective-permute-start | bytes 405512 | tf_op jit(solution)/shard_map/ppermute | solution.py:520
  34.3 19.0 %collective-permute-start.14 = (f32[264,128]{1,0:T(8,128)}, f32[264,128]{1,0:T(8,128)S(1)}, u32[]{:S(2)}, u32[]{:S(2)}) collective-permute-start(f32[264,128]{1,0:T(8,128)} %get-tuple-element.49), channel_id=1, source_target_pairs={{0,15},{1,14},{2,13},{3,12},{4,11},{5,10},{6,9},{7,8},{8,7},{9,6},... | collective-permute-start | bytes 405512 | tf_op jit(solution)/shard_map/ppermute | solution.py:520
  58.5 7.5 %collective-permute-start.15 = (f32[256,128]{1,0:T(8,128)S(1)}, f32[256,128]{1,0:T(8,128)S(1)}, u32[]{:S(2)}, u32[]{:S(2)}) collective-permute-start(f32[256,128]{1,0:T(8,128)S(1)} %get-tuple-element.51), channel_id=1, source_target_pairs={{0,3},{1,2},{2,1},{3,0},{4,7},{5,6},{6,5},{7,4},{8,11},{9,10},{10,... | collective-permute-start | bytes 393224 | tf_op jit(solution)/shard_map/ppermute | solution.py:520
  58.6 11.1 %collective-permute-start.16 = (f32[256,128]{1,0:T(8,128)S(1)}, f32[256,128]{1,0:T(8,128)S(1)}, u32[]{:S(2)}, u32[]{:S(2)}) collective-permute-start(f32[256,128]{1,0:T(8,128)S(1)} %get-tuple-element.52), channel_id=1, source_target_pairs={{0,12},{1,13},{2,14},{3,15},{4,8},{5,9},{6,10},{7,11},{8,4},{9,5},... | collective-permute-start | bytes 393224 | tf_op jit(solution)/shard_map/ppermute | solution.py:520
  59.1 10.7 %collective-permute-start.17 = (f32[256,128]{1,0:T(8,128)S(1)}, f32[256,128]{1,0:T(8,128)S(1)}, u32[]{:S(2)}, u32[]{:S(2)}) collective-permute-start(f32[256,128]{1,0:T(8,128)S(1)} %get-tuple-element.53), channel_id=1, source_target_pairs={{0,10},{1,11},{2,8},{3,9},{4,14},{5,15},{6,12},{7,13},{8,2},{9,3},... | collective-permute-start | bytes 393224 | tf_op jit(solution)/shard_map/ppermute | solution.py:520
  59.3 11.7 %collective-permute-start.18 = (f32[256,128]{1,0:T(8,128)S(1)}, f32[256,128]{1,0:T(8,128)S(1)}, u32[]{:S(2)}, u32[]{:S(2)}) collective-permute-start(f32[256,128]{1,0:T(8,128)S(1)} %get-tuple-element.54), channel_id=1, source_target_pairs={{0,9},{1,8},{2,11},{3,10},{4,13},{5,12},{6,15},{7,14},{8,1},{9,0},... | collective-permute-start | bytes 393224 | tf_op jit(solution)/shard_map/ppermute | solution.py:520
  62.3 8.7 %collective-permute-start.19 = (f32[256,128]{1,0:T(8,128)S(1)}, f32[256,128]{1,0:T(8,128)S(1)}, u32[]{:S(2)}, u32[]{:S(2)}) collective-permute-start(f32[256,128]{1,0:T(8,128)S(1)} %get-tuple-element.55), channel_id=1, source_target_pairs={{0,4},{1,5},{2,6},{3,7},{4,0},{5,1},{6,2},{7,3},{8,12},{9,13},{10,... | collective-permute-start | bytes 393224 | tf_op jit(solution)/shard_map/ppermute | solution.py:520
  66.0 8.4 %collective-permute-start.20 = (f32[256,128]{1,0:T(8,128)S(1)}, f32[256,128]{1,0:T(8,128)S(1)}, u32[]{:S(2)}, u32[]{:S(2)}) collective-permute-start(f32[256,128]{1,0:T(8,128)S(1)} %get-tuple-element.56), channel_id=1, source_target_pairs={{0,6},{1,7},{2,4},{3,5},{4,2},{5,3},{6,0},{7,1},{8,14},{9,15},{10,... | collective-permute-start | bytes 393224 | tf_op jit(solution)/shard_map/ppermute | solution.py:520
  69.8 7.2 %collective-permute-start.21 = (f32[256,128]{1,0:T(8,128)S(1)}, f32[256,128]{1,0:T(8,128)S(1)}, u32[]{:S(2)}, u32[]{:S(2)}) collective-permute-start(f32[256,128]{1,0:T(8,128)S(1)} %get-tuple-element.57), channel_id=1, source_target_pairs={{0,5},{1,4},{2,7},{3,6},{4,1},{5,0},{6,3},{7,2},{8,13},{9,12},{10,... | collective-permute-start | bytes 393224 | tf_op jit(solution)/shard_map/ppermute | solution.py:520
  69.8 14.1 %collective-permute-start.22 = (f32[256,128]{1,0:T(8,128)S(1)}, f32[256,128]{1,0:T(8,128)S(1)}, u32[]{:S(2)}, u32[]{:S(2)}) collective-permute-start(f32[256,128]{1,0:T(8,128)S(1)} %get-tuple-element.58), channel_id=1, source_target_pairs={{0,7},{1,6},{2,5},{3,4},{4,3},{5,2},{6,1},{7,0},{8,15},{9,14},{10,... | collective-permute-start | bytes 393224 | tf_op jit(solution)/shard_map/ppermute | solution.py:520
  71.0 12.8 %collective-permute-start.23 = (f32[256,128]{1,0:T(8,128)S(1)}, f32[256,128]{1,0:T(8,128)S(1)}, u32[]{:S(2)}, u32[]{:S(2)}) collective-permute-start(f32[256,128]{1,0:T(8,128)S(1)} %get-tuple-element.59), channel_id=1, source_target_pairs={{0,8},{1,9},{2,10},{3,11},{4,12},{5,13},{6,14},{7,15},{8,0},{9,1},... | collective-permute-start | bytes 393224 | tf_op jit(solution)/shard_map/ppermute | solution.py:520
  71.0 15.7 %collective-permute-start.24 = (f32[256,128]{1,0:T(8,128)S(1)}, f32[256,128]{1,0:T(8,128)S(1)}, u32[]{:S(2)}, u32[]{:S(2)}) collective-permute-start(f32[256,128]{1,0:T(8,128)S(1)} %get-tuple-element.60), channel_id=1, source_target_pairs={{0,14},{1,15},{2,12},{3,13},{4,10},{5,11},{6,8},{7,9},{8,6},{9,7},... | collective-permute-start | bytes 393224 | tf_op jit(solution)/shard_map/ppermute | solution.py:520
  74.3 14.8 %collective-permute-start.25 = (f32[256,128]{1,0:T(8,128)S(1)}, f32[256,128]{1,0:T(8,128)S(1)}, u32[]{:S(2)}, u32[]{:S(2)}) collective-permute-start(f32[256,128]{1,0:T(8,128)S(1)} %get-tuple-element.61), channel_id=1, source_target_pairs={{0,1},{1,0},{2,3},{3,2},{4,5},{5,4},{6,7},{7,6},{8,9},{9,8},{10,11... | collective-permute-start | bytes 393224 | tf_op jit(solution)/shard_map/ppermute | solution.py:520
  76.9 15.4 %collective-permute-start.26 = (f32[256,128]{1,0:T(8,128)S(1)}, f32[256,128]{1,0:T(8,128)S(1)}, u32[]{:S(2)}, u32[]{:S(2)}) collective-permute-start(f32[256,128]{1,0:T(8,128)S(1)} %get-tuple-element.62), channel_id=1, source_target_pairs={{0,2},{1,3},{2,0},{3,1},{4,6},{5,7},{6,4},{7,5},{8,10},{9,11},{10,... | collective-permute-start | bytes 393224 | tf_op jit(solution)/shard_map/ppermute | solution.py:520
  83.8 13.2 %collective-permute-start.27 = (f32[256,128]{1,0:T(8,128)S(1)}, f32[256,128]{1,0:T(8,128)S(1)}, u32[]{:S(2)}, u32[]{:S(2)}) collective-permute-start(f32[256,128]{1,0:T(8,128)S(1)} %get-tuple-element.63), channel_id=1, source_target_pairs={{0,13},{1,12},{2,15},{3,14},{4,9},{5,8},{6,11},{7,10},{8,5},{9,4},... | collective-permute-start | bytes 393224 | tf_op jit(solution)/shard_map/ppermute | solution.py:520
  83.8 16.5 %collective-permute-start.28 = (f32[256,128]{1,0:T(8,128)S(1)}, f32[256,128]{1,0:T(8,128)S(1)}, u32[]{:S(2)}, u32[]{:S(2)}) collective-permute-start(f32[256,128]{1,0:T(8,128)S(1)} %get-tuple-element.64), channel_id=1, source_target_pairs={{0,11},{1,10},{2,9},{3,8},{4,15},{5,14},{6,13},{7,12},{8,3},{9,2},... | collective-permute-start | bytes 393224 | tf_op jit(solution)/shard_map/ppermute | solution.py:520
  86.8 16.4 %collective-permute-start.29 = (f32[256,128]{1,0:T(8,128)S(1)}, f32[256,128]{1,0:T(8,128)S(1)}, u32[]{:S(2)}, u32[]{:S(2)}) collective-permute-start(f32[256,128]{1,0:T(8,128)S(1)} %get-tuple-element.65), channel_id=1, source_target_pairs={{0,15},{1,14},{2,13},{3,12},{4,11},{5,10},{6,9},{7,8},{8,7},{9,6},... | collective-permute-start | bytes 393224 | tf_op jit(solution)/shard_map/ppermute | solution.py:520
  (4 other events, 128.5 us)
